TPU v7x, 32 devices: a whole 2x2x4 slice. The times are simulated.
32 devices in a mesh: item: 4 (over z), pair: 8 (over y, x, core).
Axes of the slice: x: 2, y: 2, z: 4, core: 2. Of those that a mesh axis runs over, the one named last changes fastest.
Arguments:
- pair_act: bfloat16 [4, 384, 384, 128], P('item', 'pair'), may hold values from -6 to 6
- targets: float32 [4, 384, 384], P('item', 'pair'), may hold values from -6 to 6
- pair_mask: int32 [4, 384, 384], P('item', 'pair'), may hold values from 0 to 1
- tri_proj: float32 [1, 128, 640], P(None, 'item'), may hold values from -0.5 to 0.5
- tri_out: float32 [1, 128, 128], P(None, 'item'), may hold values from -0.5 to 0.5
- attention_proj: float32 [1, 128, 512], P(None, 'item'), may hold values from -0.5 to 0.5
- bias_proj: float32 [1, 128, 4], P(None, 'item'), may hold values from -0.5 to 0.5
- output_proj: float32 [1, 128, 128], P(None, 'item'), may hold values from -1.5 to 1.5
- expand_proj: float32 [1, 128, 1024], P(None, 'item'), may hold values from -0.5 to 0.5
- shrink_proj: float32 [1, 512, 128], P(None, 'item'), may hold values from -0.25 to 0.25
- vectors: float32 [5, 128], P(None, 'item'), may hold values from -1 to 3
- first_tri: float32 [1, 128, 640], P(None, 'item'), may hold values from -1.1920929e-06 to 1.1920929e-06
- first_tri_out: float32 [1, 128, 128], P(None, 'item'), may hold values from -1.1920929e-06 to 1.1920929e-06
- first_attention: float32 [1, 128, 512], P(None, 'item'), may hold values from -1.1920929e-06 to 1.1920929e-06
- first_bias: float32 [1, 128, 4], P(None, 'item'), may hold values from -1.1920929e-06 to 1.1920929e-06
- first_output: float32 [1, 128, 128], P(None, 'item'), may hold values from -1.1920929e-06 to 1.1920929e-06
- first_expand: float32 [1, 128, 1024], P(None, 'item'), may hold values from -1.1920929e-06 to 1.1920929e-06
- first_shrink: float32 [1, 512, 128], P(None, 'item'), may hold values from -1.1920929e-06 to 1.1920929e-06
- first_vectors: float32 [5, 128], P(None, 'item'), may hold values from -5.340576e-05 to 5.340576e-05
- second_tri: float32 [1, 128, 640], P(None, 'item'), may hold values from 2.7e-15 to 1.06e-14
- second_tri_out: float32 [1, 128, 128], P(None, 'item'), may hold values from 2.7e-15 to 1.06e-14
- second_attention: float32 [1, 128, 512], P(None, 'item'), may hold values from 2.7e-15 to 1.06e-14
- second_bias: float32 [1, 128, 4], P(None, 'item'), may hold values from 2.7e-15 to 1.06e-14
- second_output: float32 [1, 128, 128], P(None, 'item'), may hold values from 2.7e-15 to 1.06e-14
- second_expand: float32 [1, 128, 1024], P(None, 'item'), may hold values from 2.7e-15 to 1.06e-14
- second_shrink: float32 [1, 512, 128], P(None, 'item'), may hold values from 2.7e-15 to 1.06e-14
- second_vectors: float32 [5, 128], P(None, 'item'), may hold values from 7.8125e-12 to 3.125e-11
Outputs:
- loss_sum: float32 [], replicated
- pair_count: float32 [], replicated
- grad_norm: float32 [], replicated
- new_tri: float32 [1, 128, 640], P(None, 'item')
- new_tri_out: float32 [1, 128, 128], P(None, 'item')
- new_attention: float32 [1, 128, 512], P(None, 'item')
- new_bias: float32 [1, 128, 4], P(None, 'item')
- new_output: float32 [1, 128, 128], P(None, 'item')
- new_expand: float32 [1, 128, 1024], P(None, 'item')
- new_shrink: float32 [1, 512, 128], P(None, 'item')
- new_vectors: float32 [5, 128], P(None, 'item')
- moment_tri: float32 [1, 128, 640], P(None, 'item')
- moment_tri_out: float32 [1, 128, 128], P(None, 'item')
- moment_attention: float32 [1, 128, 512], P(None, 'item')
- moment_bias: float32 [1, 128, 4], P(None, 'item')
- moment_output: float32 [1, 128, 128], P(None, 'item')
- moment_expand: float32 [1, 128, 1024], P(None, 'item')
- moment_shrink: float32 [1, 512, 128], P(None, 'item')
- moment_vectors: float32 [5, 128], P(None, 'item')
- square_tri: float32 [1, 128, 640], P(None, 'item')
- square_tri_out: float32 [1, 128, 128], P(None, 'item')
- square_attention: float32 [1, 128, 512], P(None, 'item')
- square_bias: float32 [1, 128, 4], P(None, 'item')
- square_output: float32 [1, 128, 128], P(None, 'item')
- square_expand: float32 [1, 128, 1024], P(None, 'item')
- square_shrink: float32 [1, 512, 128], P(None, 'item')
- square_vectors: float32 [5, 128], P(None, 'item')
All inputs are finite; a program needn't handle non-finite values.
Results may differ from a plain program's by a relative error of at most 0.015.
Values may be sent and summed in bfloat16 or wider, within the bound.
No kernel may reach another device: no remote copies, remote signals or barrier semaphores. Data moves between devices by JAX's collectives and lax.ppermute only.
A program may use at most 640 MiB of HBM per device.

v0:
```python
import jax
import jax.numpy as jnp
from jax import lax
from jax.sharding import PartitionSpec as P

STEP = 10


norm_epsilon = 1e-05
clip_limit = 0.001
learn_rate = 0.1
vector_rate = 0.8
beta_first = 0.9
beta_second = 0.999
adam_epsilon = 1e-08
weight_decay = 0.01


def normalize(stream, gain):
    mean = jnp.mean(stream, axis=-1, keepdims=True)
    centred = stream - mean
    scale = lax.rsqrt(jnp.mean(centred * centred, axis=-1, keepdims=True) + norm_epsilon)
    normed = centred * scale
    return (normed * gain, normed, scale)


def normalize_back(upstream, gain, normed, scale):
    inner = upstream * gain
    below = scale * (
        inner
        - jnp.mean(inner, axis=-1, keepdims=True)
        - normed * jnp.mean(inner * normed, axis=-1, keepdims=True)
    )
    return (below, jnp.sum(upstream * normed, axis=(0, 1, 2)))


def matmul(value, weight):
    return jnp.einsum("...c,cd->...d", value, weight, preferred_element_type=jnp.float32)


def matmul_back(value, weight):
    return jnp.einsum("...d,cd->...c", value, weight, preferred_element_type=jnp.float32)


def weight_grad(left, right):
    flat_left = left.reshape(-1, left.shape[-1])
    flat_right = right.reshape(-1, right.shape[-1])
    return lax.dot_general(
        flat_left, flat_right, (((0,), (0,)), ((), ())), preferred_element_type=jnp.float32
    )


def rounded(value):
    return value.astype(jnp.bfloat16).astype(jnp.float32)


def flatten_heads(value):
    return value.reshape(value.shape[0], value.shape[1], -1)


def column_slices(index, arrays, heads):
    pieces = []
    for array in arrays:
        piece = lax.dynamic_index_in_dim(array, index, 2, keepdims=False)
        pieces.append(piece.reshape(piece.shape[0], piece.shape[1], heads, -1))
    return pieces


def column_scores(query_col, keys_col, bias_full):
    scores = jnp.einsum("bihd,bkhd->bhki", query_col, keys_col, preferred_element_type=jnp.float32)
    return scores * query_col.shape[-1] ** (-0.5) + bias_full.astype(jnp.float32)


def attend(query, keys, values, bias_full):
    heads = bias_full.shape[1]

    def column(carry, index):
        query_col, keys_col, values_col = column_slices(index, (query, keys, values), heads)
        scores = column_scores(query_col, keys_col, bias_full)
        top = jnp.max(scores, axis=2, keepdims=True)
        expo = jnp.exp(scores - top)
        total = jnp.sum(expo, axis=2, keepdims=True)
        result = jnp.einsum(
            "bhki,bkhd->bihd",
            (expo / total).astype(jnp.bfloat16),
            values_col,
            preferred_element_type=jnp.float32,
        )
        return (carry, (flatten_heads(result), (top + jnp.log(total))[:, :, 0]))

    _, (outputs, logsum) = lax.scan(column, jnp.int32(0), jnp.arange(query.shape[2]))
    return (jnp.moveaxis(outputs, 0, 2), logsum)


def attend_back(query, keys, values, bias_full, logsum, grad_attended):
    heads = bias_full.shape[1]
    scale = (query.shape[-1] // heads) ** (-0.5)

    def column(carry, index):
        query_col, keys_col, values_col, grad_col = column_slices(
            index, (query, keys, values, grad_attended), heads
        )
        scores = column_scores(query_col, keys_col, bias_full)
        probs = jnp.exp(scores - logsum[index][:, :, None, :])
        grad_probs = jnp.einsum(
            "bihd,bkhd->bhki", grad_col, values_col, preferred_element_type=jnp.float32
        )
        grad_scores = probs * (grad_probs - jnp.sum(probs * grad_probs, axis=2, keepdims=True))
        score_low = grad_scores.astype(jnp.bfloat16)
        grad_query = (
            jnp.einsum("bhki,bkhd->bihd", score_low, keys_col, preferred_element_type=jnp.float32)
            * scale
        )
        grad_keys = (
            jnp.einsum("bhki,bihd->bkhd", score_low, query_col, preferred_element_type=jnp.float32)
            * scale
        )
        grad_values = jnp.einsum(
            "bhki,bihd->bkhd",
            probs.astype(jnp.bfloat16),
            grad_col,
            preferred_element_type=jnp.float32,
        )
        return (
            carry + score_low.astype(jnp.float32),
            (flatten_heads(grad_query), flatten_heads(grad_keys), flatten_heads(grad_values)),
        )

    start = jnp.zeros(bias_full.shape, jnp.float32)
    grad_bias, (grad_query, grad_keys, grad_values) = lax.scan(
        column, start, jnp.arange(query.shape[2])
    )
    return (
        grad_bias,
        jnp.moveaxis(grad_query, 0, 2),
        jnp.moveaxis(grad_keys, 0, 2),
        jnp.moveaxis(grad_values, 0, 2),
    )


def split_projected(projected, width):
    query = projected[..., :width].astype(jnp.bfloat16)
    keys = projected[..., width : 2 * width].astype(jnp.bfloat16)
    values = projected[..., 2 * width : 3 * width].astype(jnp.bfloat16)
    gate = jax.nn.sigmoid(projected[..., 3 * width :])
    return (query, keys, values, gate)


def incoming_parts(stream, tri_w, gain_tri):
    normed_in, normed, scale = normalize(stream, gain_tri)
    normed_low = normed_in.astype(jnp.bfloat16)
    projected = matmul(normed_low, tri_w)
    width = tri_w.shape[0]
    pieces = [projected[..., index * width : (index + 1) * width] for index in range(5)]
    left = (jax.nn.sigmoid(pieces[1]) * pieces[0]).astype(jnp.bfloat16)
    right = (jax.nn.sigmoid(pieces[3]) * pieces[2]).astype(jnp.bfloat16)
    return (normed_low, normed, scale, pieces, left, right)


def incoming_forward(stream, tri_w, tri_out_w, gain_tri, gain_centre):
    _, _, _, pieces, left, right = incoming_parts(stream, tri_w, gain_tri)
    part = jnp.einsum(
        "bkic,bkjc->bijc",
        lax.all_gather(left, "pair", axis=2, tiled=True),
        right,
        preferred_element_type=jnp.float32,
    )
    centre_in, _, _ = normalize(part, gain_centre)
    linear = matmul(centre_in.astype(jnp.bfloat16), tri_out_w)
    branch = (jax.nn.sigmoid(pieces[4]) * linear).astype(jnp.bfloat16)
    return (stream + branch.astype(jnp.float32), part)


def incoming_back(upstream, stream, product, tri_w, tri_out_w, gain_tri, gain_centre):
    normed_low, normed, scale, pieces, left, right = incoming_parts(stream, tri_w, gain_tri)
    centre_in, centre_normed, centre_scale = normalize(product, gain_centre)
    centre_low = centre_in.astype(jnp.bfloat16)
    linear = matmul(centre_low, tri_out_w)
    gate = jax.nn.sigmoid(pieces[4])
    grad_branch = rounded(upstream)
    grad_linear = (grad_branch * gate).astype(jnp.bfloat16)
    grad_gate = grad_branch * linear * gate * (1.0 - gate)
    grad_tri_out = weight_grad(centre_low, grad_linear)
    grad_centre = rounded(matmul_back(grad_linear, tri_out_w))
    grad_product, grad_gain_centre = normalize_back(
        grad_centre, gain_centre, centre_normed, centre_scale
    )
    grad_low = grad_product.astype(jnp.bfloat16)
    row_view = lax.all_to_all(grad_low, "pair", split_axis=1, concat_axis=2, tiled=True)
    left_piece = lax.all_gather(left, "pair", axis=2, tiled=True)
    right_piece = lax.all_gather(right, "pair", axis=2, tiled=True)
    grad_right = jnp.einsum(
        "bkic,bijc->bkjc", left_piece, grad_low, preferred_element_type=jnp.float32
    )
    grad_left = jnp.einsum(
        "bkjc,bijc->bkic", right_piece, row_view, preferred_element_type=jnp.float32
    )
    grad_left = rounded(grad_left)
    grad_right = rounded(grad_right)
    sig_left = jax.nn.sigmoid(pieces[1])
    sig_right = jax.nn.sigmoid(pieces[3])
    grad_projected = jnp.concatenate(
        [
            grad_left * sig_left,
            grad_left * pieces[0] * sig_left * (1.0 - sig_left),
            grad_right * sig_right,
            grad_right * pieces[2] * sig_right * (1.0 - sig_right),
            grad_gate,
        ],
        axis=-1,
    ).astype(jnp.bfloat16)
    grad_tri = weight_grad(normed_low, grad_projected)
    grad_normed = rounded(matmul_back(grad_projected, tri_w))
    below, grad_gain_tri = normalize_back(grad_normed, gain_tri, normed, scale)
    return (upstream + below, grad_tri, grad_tri_out, grad_gain_tri, grad_gain_centre)


def block_forward(stream, weights):
    (
        tri_w,
        tri_out_w,
        project_w,
        pairbias_w,
        output_w,
        expand_w,
        shrink_w,
        gain_tri,
        gain_centre,
        gain_attend,
        gain_expand,
    ) = weights
    after, product = incoming_forward(stream, tri_w, tri_out_w, gain_tri, gain_centre)
    normed_in, _, _ = normalize(after, gain_attend)
    inputs_col = normed_in.astype(jnp.bfloat16)
    query, keys, values, gate = split_projected(matmul(inputs_col, project_w), output_w.shape[0])
    bias_part = jnp.transpose(matmul(inputs_col, pairbias_w).astype(jnp.bfloat16), (0, 3, 1, 2))
    bias_full = lax.all_gather(bias_part, "pair", axis=3, tiled=True)
    attended, logsum = attend(query, keys, values, bias_full)
    gated = (gate * attended).astype(jnp.bfloat16)
    branch = matmul(gated, output_w).astype(jnp.bfloat16)
    middle = after + branch.astype(jnp.float32)
    expanded_in, _, _ = normalize(middle, gain_expand)
    expanded = matmul(expanded_in.astype(jnp.bfloat16), expand_w)
    hidden = expand_w.shape[1] // 2
    activated = (jax.nn.silu(expanded[..., :hidden]) * expanded[..., hidden:]).astype(jnp.bfloat16)
    result = middle + matmul(activated, shrink_w)
    return (result, (stream, product, after, inputs_col, attended, logsum, bias_full, middle))


def block_back(upstream, kept, weights):
    (
        tri_w,
        tri_out_w,
        project_w,
        pairbias_w,
        output_w,
        expand_w,
        shrink_w,
        gain_tri,
        gain_centre,
        gain_attend,
        gain_expand,
    ) = weights
    stream, product, after, inputs_col, attended, logsum, bias_full, middle = kept
    expanded_in, expanded_normed, expanded_scale = normalize(middle, gain_expand)
    expanded_low = expanded_in.astype(jnp.bfloat16)
    expanded = matmul(expanded_low, expand_w)
    hidden = expand_w.shape[1] // 2
    first_half = expanded[..., :hidden]
    second_half = expanded[..., hidden:]
    sigma = jax.nn.sigmoid(first_half)
    swish = first_half * sigma
    activated = (swish * second_half).astype(jnp.bfloat16)
    upstream_low = upstream.astype(jnp.bfloat16)
    grad_shrink = weight_grad(activated, upstream_low)
    grad_act = rounded(matmul_back(upstream_low, shrink_w))
    grad_first = grad_act * second_half * sigma * (1.0 + first_half * (1.0 - sigma))
    grad_second = grad_act * swish
    grad_expanded = jnp.concatenate([grad_first, grad_second], axis=-1).astype(jnp.bfloat16)
    grad_expand = weight_grad(expanded_low, grad_expanded)
    below, grad_gain_expand = normalize_back(
        matmul_back(grad_expanded, expand_w), gain_expand, expanded_normed, expanded_scale
    )
    upstream = upstream + below
    query, keys, values, gate = split_projected(matmul(inputs_col, project_w), output_w.shape[0])
    grad_branch = upstream.astype(jnp.bfloat16)
    gated = (gate * attended).astype(jnp.bfloat16)
    grad_output = weight_grad(gated, grad_branch)
    grad_gated = matmul_back(grad_branch, output_w)
    grad_attended = (grad_gated * gate).astype(jnp.bfloat16)
    grad_gate = grad_gated * attended * gate * (1.0 - gate)
    grad_bias, grad_query, grad_keys, grad_values = attend_back(
        query, keys, values, bias_full, logsum, grad_attended
    )
    bias_cols = lax.psum_scatter(grad_bias, "pair", scatter_dimension=3, tiled=True)
    bias_low = jnp.transpose(bias_cols, (0, 2, 3, 1)).astype(jnp.bfloat16)
    grad_projected = jnp.concatenate(
        [grad_query, grad_keys, grad_values, grad_gate], axis=-1
    ).astype(jnp.bfloat16)
    grad_project = weight_grad(inputs_col, grad_projected)
    grad_pairbias = weight_grad(inputs_col, bias_low)
    grad_inputs = rounded(
        matmul_back(grad_projected, project_w) + matmul_back(bias_low, pairbias_w)
    )
    _, normed, scale = normalize(after, gain_attend)
    below, grad_gain_attend = normalize_back(grad_inputs, gain_attend, normed, scale)
    upstream = upstream + below
    upstream, grad_tri, grad_tri_out, grad_gain_tri, grad_gain_centre = incoming_back(
        upstream, stream, product, tri_w, tri_out_w, gain_tri, gain_centre
    )
    return (
        upstream,
        (
            grad_tri,
            grad_tri_out,
            grad_project,
            grad_pairbias,
            grad_output,
            grad_expand,
            grad_shrink,
            grad_gain_tri,
            grad_gain_centre,
            grad_gain_attend,
            grad_gain_expand,
        ),
    )


def layer_weights(gathered, vector_full, index):
    return tuple((gathered[slot][index] for slot in range(7))) + tuple(
        (vector_full[4 * index + slot] for slot in range(4))
    )


def on_device(
    pair_act,
    targets,
    pair_mask,
    tri_proj,
    tri_out,
    attention_proj,
    bias_proj,
    output_proj,
    expand_proj,
    shrink_proj,
    vectors,
    first_tri,
    first_tri_out,
    first_attention,
    first_bias,
    first_output,
    first_expand,
    first_shrink,
    first_vectors,
    second_tri,
    second_tri_out,
    second_attention,
    second_bias,
    second_output,
    second_expand,
    second_shrink,
    second_vectors,
):
    gathered = (
        lax.all_gather(tri_proj.astype(jnp.bfloat16), "item", axis=1, tiled=True),
        lax.all_gather(tri_out.astype(jnp.bfloat16), "item", axis=1, tiled=True),
        lax.all_gather(attention_proj.astype(jnp.bfloat16), "item", axis=1, tiled=True),
        lax.all_gather(bias_proj.astype(jnp.bfloat16), "item", axis=1, tiled=True),
        lax.all_gather(output_proj.astype(jnp.bfloat16), "item", axis=1, tiled=True),
        lax.all_gather(expand_proj.astype(jnp.bfloat16), "item", axis=1, tiled=True),
        lax.all_gather(shrink_proj.astype(jnp.bfloat16), "item", axis=1, tiled=True),
        lax.all_gather(vectors.astype(jnp.bfloat16), "item", axis=1, tiled=True),
    )
    vector_full = gathered[7].astype(jnp.float32)
    layers = attention_proj.shape[0]
    weighting_rows = pair_mask.astype(jnp.float32)
    count = lax.psum(jnp.sum(weighting_rows), ("item", "pair"))
    stream = lax.all_to_all(pair_act, "pair", split_axis=2, concat_axis=1, tiled=True).astype(
        jnp.float32
    )
    target_cols, weighting = (
        lax.all_to_all(targets, "pair", split_axis=2, concat_axis=1, tiled=True),
        lax.all_to_all(weighting_rows, "pair", split_axis=2, concat_axis=1, tiled=True),
    )
    index = 0
    stream, kept = block_forward(stream, layer_weights(gathered, vector_full, index))
    kept_all = [kept]
    readout_w = vector_full[4 * layers]
    readout = jnp.sum(stream * readout_w, axis=-1)
    error = readout - target_cols
    loss_local = jnp.sum(weighting * error * error)
    grad_readout = 2.0 * weighting * error / count
    grad_vector_read = jnp.sum(grad_readout[..., None] * stream, axis=(0, 1, 2))
    upstream = grad_readout[..., None] * readout_w
    collected = []
    for index in reversed(range(layers)):
        upstream, grads = block_back(
            upstream, kept_all[index], layer_weights(gathered, vector_full, index)
        )
        collected.append(grads)
    collected = collected[::-1]
    gains = []
    for entry in collected:
        gains.extend([entry[7], entry[8], entry[9], entry[10]])
    gains.append(grad_vector_read)
    summed = lax.psum(
        (
            jnp.stack([entry[0] for entry in collected]),
            jnp.stack([entry[1] for entry in collected]),
            jnp.stack([entry[2] for entry in collected]),
            jnp.stack([entry[3] for entry in collected]),
            jnp.stack([entry[4] for entry in collected]),
            jnp.stack([entry[5] for entry in collected]),
            jnp.stack([entry[6] for entry in collected]),
            jnp.stack(gains),
            loss_local,
        ),
        "pair",
    )
    shards = (
        lax.psum_scatter(
            summed[0].astype(jnp.bfloat16), "item", scatter_dimension=1, tiled=True
        ).astype(jnp.float32),
        lax.psum_scatter(
            summed[1].astype(jnp.bfloat16), "item", scatter_dimension=1, tiled=True
        ).astype(jnp.float32),
        lax.psum_scatter(
            summed[2].astype(jnp.bfloat16), "item", scatter_dimension=1, tiled=True
        ).astype(jnp.float32),
        lax.psum_scatter(
            summed[3].astype(jnp.bfloat16), "item", scatter_dimension=1, tiled=True
        ).astype(jnp.float32),
        lax.psum_scatter(
            summed[4].astype(jnp.bfloat16), "item", scatter_dimension=1, tiled=True
        ).astype(jnp.float32),
        lax.psum_scatter(
            summed[5].astype(jnp.bfloat16), "item", scatter_dimension=1, tiled=True
        ).astype(jnp.float32),
        lax.psum_scatter(
            summed[6].astype(jnp.bfloat16), "item", scatter_dimension=1, tiled=True
        ).astype(jnp.float32),
        lax.psum_scatter(
            summed[7].astype(jnp.bfloat16), "item", scatter_dimension=1, tiled=True
        ).astype(jnp.float32),
    )
    squares = sum((jnp.sum(piece * piece) for piece in shards))
    totals = lax.psum((squares, summed[8]), "item")
    grad_norm = jnp.sqrt(totals[0])
    factor = jnp.minimum(1.0, clip_limit / (grad_norm + 1e-06))
    masters = (
        tri_proj,
        tri_out,
        attention_proj,
        bias_proj,
        output_proj,
        expand_proj,
        shrink_proj,
        vectors,
    )
    firsts = (
        first_tri,
        first_tri_out,
        first_attention,
        first_bias,
        first_output,
        first_expand,
        first_shrink,
        first_vectors,
    )
    seconds = (
        second_tri,
        second_tri_out,
        second_attention,
        second_bias,
        second_output,
        second_expand,
        second_shrink,
        second_vectors,
    )
    rates = (learn_rate,) * 7 + (vector_rate,)
    new_masters, new_firsts, new_seconds = ([], [], [])
    for master, grad, first, second, rate in zip(masters, shards, firsts, seconds, rates):
        clipped = grad * factor
        moment = beta_first * first + (1 - beta_first) * clipped
        square = beta_second * second + (1 - beta_second) * clipped * clipped
        stride = (
            moment
            / (1 - beta_first**STEP)
            / (jnp.sqrt(square / (1 - beta_second**STEP)) + adam_epsilon)
        )
        new_masters.append(master - rate * (stride + weight_decay * master))
        new_firsts.append(moment)
        new_seconds.append(square)
    return (
        (totals[1], count, grad_norm) + tuple(new_masters) + tuple(new_firsts) + tuple(new_seconds)
    )


def solution(mesh):
    in_specs = (
        P("item", "pair", None, None),
        P("item", "pair", None),
        P("item", "pair", None),
        P(None, "item", None),
        P(None, "item", None),
        P(None, "item", None),
        P(None, "item", None),
        P(None, "item", None),
        P(None, "item", None),
        P(None, "item", None),
        P(None, "item"),
        P(None, "item", None),
        P(None, "item", None),
        P(None, "item", None),
        P(None, "item", None),
        P(None, "item", None),
        P(None, "item", None),
        P(None, "item", None),
        P(None, "item"),
        P(None, "item", None),
        P(None, "item", None),
        P(None, "item", None),
        P(None, "item", None),
        P(None, "item", None),
        P(None, "item", None),
        P(None, "item", None),
        P(None, "item"),
    )
    out_specs = (
        P(),
        P(),
        P(),
        P(None, "item", None),
        P(None, "item", None),
        P(None, "item", None),
        P(None, "item", None),
        P(None, "item", None),
        P(None, "item", None),
        P(None, "item", None),
        P(None, "item"),
        P(None, "item", None),
        P(None, "item", None),
        P(None, "item", None),
        P(None, "item", None),
        P(None, "item", None),
        P(None, "item", None),
        P(None, "item", None),
        P(None, "item"),
        P(None, "item", None),
        P(None, "item", None),
        P(None, "item", None),
        P(None, "item", None),
        P(None, "item", None),
        P(None, "item", None),
        P(None, "item", None),
        P(None, "item"),
    )
    return jax.shard_map(
        on_device, mesh=mesh, in_specs=in_specs, out_specs=out_specs, check_vma=False
    )
```

profile of v0, /device:TPU:0, one launch (start us, length us, event | category | flops | bytes accessed | tf_op | source)
XLA Modules:
  0.0 2920.0 jit_solution(10365930460017414251)
XLA Ops:
  47.7 27.1 all-to-all-done.1
  94.7 19.8 convolution_bitcast_fusion.1
  183.9 128.5 %all-gather.5.cloned.1.call-done = bf16[1,384,384,128]{3,1,0,2:T(8,128)(2,1)} async-done(((bf16[1,384,48,128]{3,1,0,2:T(8,128)(2,1)}), bf16[1,384,384,128]{3,1,0,2:T(8,128)(2,1)}) %all-gather.5.cloned.1.call-update) | async-done | bytes 37748752 | tf_op jit(solution)/shard_map/all_gather | solution.py:164
  312.4 53.3 %copy.261 = bf16[1,384,384,128]{2,1,3,0:T(8,128)(2,1)} copy(bf16[1,384,384,128]{3,1,0,2:T(8,128)(2,1)} %all-gather.5.cloned.1.call-done) | data formatting | bytes 75497472 | tf_op jit(solution)/shard_map/all_gather | solution.py:164
  365.7 20.2 bitcast_reduce_fusion
  473.9 41.5 %psum.86 = f32[]{:T(128)} all-reduce(f32[]{:T(128)} %convert_reduce_fusion), channel_id=1, replica_groups=mesh['item'=4,'pair'=8] {'item','pair'}, use_global_device_ids=true, to_apply=%region_17.18 | all-reduce | flops 1 | bytes 8 | tf_op jit(solution)/shard_map/psum | solution.py:377
  555.8 22.7 fusion.216
  609.5 52.4 %copy.299 = bf16[1,384,384,128]{2,1,3,0:T(8,128)(2,1)} copy(bf16[1,384,384,128]{3,1,0,2:T(8,128)(2,1)} %all-gather.9.cloned.1.call-done) | data formatting | bytes 75497472 | tf_op jit(solution)/shard_map/all_gather | solution.py:191
  665.2 408.0 %while.31 = (s32[]{:T(128)}, f32[48,1,384,128]{3,2,0,1:T(8,128)}, f32[48,1,4,384]{3,2,1,0:T(4,128)}, s32[48]{0:T(128)S(1)}, bf16[1,384,48,128]{1,3,2,0:T(8,128)(...) while((s32[]{:T(128)}, f32[48,1,384,128]{3,2,0,1:T(8,128)}, ...), condition=%wide.region_9.10_spmd.clone, body=%wide.region_6.9_spmd.sunk.clone | while | flops 80804352 | bytes 10174619 | solution.py:91
  1097.7 29.4 %convolution_bitcast_fusion = f32[1,384,48,1024]{3,1,2,0:T(8,128)} fusion(f32[1,384,48,128]{3,1,2,0:T(8,128)} %copy-done, f32[128]{0:T(128)S(1)} %copy-done.71, f32[384,48]{0,1:T(8,128)S(1)} %add_rsqrt_fusion.1, f32[384,48]{0,1:T(8,128)S(1)} %broadcast_multiply_fusion.8, bf16[1,128,1024]{2,1,0:T(8,128)(2,1)S(1)} %all_gather.42), kind=kOutput, calls=%fused_computation.44 | convolution fusion | flops 4841275392 | bytes 85344768 | tf_op jit(solution)/shard_map/...c,cd->...d/dot_general | solution.py:38
  1127.1 32.3 %fusion.19 = bf16[384,48,512]{2,0,1:T(8,128)(2,1)} fusion(f32[1,384,48,1024]{3,1,2,0:T(8,128)} %convolution_bitcast_fusion), kind=kLoop, calls=%fused_computation.47 | loop fusion | flops 56623104 | bytes 94371840 | tf_op jit(solution)/shard_map/reshape.118
  1176.7 40.3 %fusion.21 = (bf16[384,48,512]{2,0,1:T(8,128)(2,1)}, bf16[384,48,512]{2,0,1:T(8,128)(2,1)}) fusion(f32[1,384,48,1024]{3,1,2,0:T(8,128)} %convolution_bitcast_fusion, bf16[1,512,128]{2,1,0:T(8,128)(2,1)} %copy-done.42, f32[128]{0:T(128)S(1)} %copy-done.85, f32[384,48]{0,1:T(8,128)} %multiply_divide_fusion), kind=kOutput, calls=%fused_computation.50 | convolution fusion | flops 2562195456 | bytes 113451520 | tf_op jit(solution)/shard_map/...d,cd->...c/dot_general | solution.py:42
  1266.1 1059.0 %while.32 = (s32[]{:T(128)}, f32[1,4,384,384]{3,2,1,0:T(8,128)}, bf16[48,1,384,128]{3,2,0,1:T(8,128)(2,1)}, bf16[48,1,384,128]{3,2,0,1:T(8,128)(2,1)}, bf16[48,1...) while((s32[]{:T(128)}, f32[1,4,384,384]{3,2,1,0:T(8,128)}, ...), condition=%wide.region_22.23_spmd.clone.clone, body=%wide.region_20.22_spmd.clone.sunk.clone | while | flops 196606464 | bytes 46430528 | solution.py:130
  2328.0 57.6 %all-reduce.5 = bf16[1,4,384,384]{2,1,0,3:T(4,128)(2,1)} all-reduce(f32[1,4,384,384]{2,1,0,3:T(4,128)S(1)} %copy.291), channel_id=2, replica_groups=mesh['item'=4,'pair'=8] {'pair'}, use_global_device_ids=true, to_apply=%region_23.24.clone | all-reduce | flops 589824 | bytes 3538944
  2415.4 28.2 fusion.32
  2472.2 21.4 fusion.12
  2534.4 23.6 fusion.122
  2586.6 21.0 fusion.10
  2677.8 52.3 %all-reduce.6 = (f32[]{:T(128)}, bf16[1,128,640]{2,1,0:T(8,128)(2,1)}, bf16[1,128,128]{2,1,0:T(8,128)(2,1)}, bf16[1,128,512]{2,1,0:T(8,128)(2,1)}, bf16[1,128,4]...) all-reduce(f32[]{:T(128)} %get-tuple-element.387, ...), channel_id=1, replica_groups=mesh['item'=4,'pair'=8] {'pair'}, use_global_device_ids=true, to_apply=%region_14.15 | all-reduce | flops 377985 | bytes 2267912 | tf_op jit(solution)/shard_map/psum | solution.py:406
  2749.9 18.5 reduce-scatter.27.cloned.1.call-done
  2769.7 18.3 reduce-scatter.15.cloned.1.call-done
  2789.4 18.7 reduce-scatter.19.cloned.1.call-done
  2809.3 18.9 reduce-scatter.17.cloned.1.call-done
  2829.6 18.9 reduce-scatter.23.cloned.1.call-done
  (2104 shorter events, 1939.1 us)
Async XLA Ops:
  14.8 60.0 %all-to-all-start.1 = ((bf16[1,48,384,128]{3,1,0,2:T(8,128)(2,1)}), bf16[1,48,384,128]{3,1,0,2:T(8,128)(2,1)}, u32[]{:S(2)}, u32[]{:S(2)}) async-start(bf16[1,48,384,128]{3,1,0,2:T(8,128)(2,1)} %copy.257), calls=%async_computation.1 | async-start | bytes 9437184 | tf_op jit(solution)/shard_map/all_to_all | solution.py:378
  20.0 292.4 %all-gather.5.cloned.1.call-start = ((), (), s32[]{:S(2)}) async-start(), calls=%async_computation.12 | async-start | bytes 42467328 | tf_op jit(solution)/shard_map/all_gather | solution.py:164
  47.7 345.7 %copy-start.83 = (f32[128]{0:T(128)}, f32[128]{0:T(128)S(1)}, u32[]{:S(2)}) copy-start(f32[128]{0:T(128)S(1)} %get-tuple-element.391) | copy-start | bytes 1540
  47.7 379.6 %copy-start.81 = (f32[128]{0:T(128)}, f32[128]{0:T(128)S(1)}, u32[]{:S(2)}) copy-start(f32[128]{0:T(128)S(1)} %get-tuple-element.390) | copy-start | bytes 1540
  132.5 477.0 %all-gather.9.cloned.1.call-start = ((), (), s32[]{:S(2)}) async-start(), calls=%async_computation.14 | async-start | bytes 42467328 | tf_op jit(solution)/shard_map/all_gather | solution.py:191
  136.0 321.1 %all-to-all-start = ((f32[8,1,2304]{2,1,0:T(1,128)}), f32[8,1,2304]{2,1,0:T(1,128)S(1)}, u32[]{:S(2)}, u32[]{:S(2)}) async-start(f32[8,1,2304]{2,1,0:T(1,128)} %reshape.752), calls=%async_computation | async-start | bytes 147456 | tf_op jit(solution)/shard_map/all_to_all | solution.py:383
  139.4 522.4 %all-gather.7.cloned.1.call-start = ((), (), s32[]{:S(2)}) async-start(), calls=%async_computation.13 | async-start | bytes 1327104 | tf_op jit(solution)/shard_map/all_gather | solution.py:237
  156.0 278.9 %copy-start.86 = (bf16[1,128,4]{1,2,0:T(4,128)(2,1)}, bf16[1,128,4]{1,2,0:T(4,128)(2,1)S(1)}, u32[]{:S(2)}) copy-start(bf16[1,128,4]{1,2,0:T(4,128)(2,1)S(1)} %copy.267) | copy-start | bytes 3076
  457.1 640.0 %copy-start.28 = (bf16[1,128,1024]{2,1,0:T(8,128)(2,1)}, bf16[1,128,1024]{2,1,0:T(8,128)(2,1)S(1)}, u32[]{:S(2)}) copy-start(bf16[1,128,1024]{2,1,0:T(8,128)(2,1)S(1)} %all_gather.42) | copy-start | bytes 786436
  457.1 95.2 %all-to-all-start.2 = ((f32[8,1,2304]{2,1,0:T(1,128)}), f32[8,1,2304]{2,1,0:T(1,128)S(1)}, u32[]{:S(2)}, u32[]{:S(2)}) async-start(f32[8,1,2304]{2,1,0:T(1,128)} %reshape.754), calls=%async_computation.2 | async-start | bytes 147456 | tf_op jit(solution)/shard_map/all_to_all | solution.py:382
  537.0 543.7 %copy-start.52 = (bf16[1,128,128]{2,1,0:T(8,128)(2,1)}, bf16[1,128,128]{2,1,0:T(8,128)(2,1)S(1)}, u32[]{:S(2)}) copy-start(bf16[1,128,128]{2,1,0:T(8,128)(2,1)S(1)} %all_gather.41) | copy-start | bytes 98308
  550.4 609.0 %copy-start.42 = (bf16[1,512,128]{2,1,0:T(8,128)(2,1)}, bf16[1,512,128]{2,1,0:T(8,128)(2,1)S(1)}, u32[]{:S(2)}) copy-start(bf16[1,512,128]{2,1,0:T(8,128)(2,1)S(1)} %all_gather.43) | copy-start | bytes 393220
  2514.1 59.4 %all-to-all-start.3 = ((bf16[1,384,48,128]{3,2,0,1:T(8,128)(2,1)}), bf16[1,384,48,128]{3,2,0,1:T(8,128)(2,1)}, u32[]{:S(2)}, u32[]{:S(2)}) async-start(bf16[1,384,48,128]{3,2,0,1:T(8,128)(2,1)} %copy.296), calls=%async_computation.3 | async-start | bytes 9437184 | tf_op jit(solution)/shard_map/all_to_all | solution.py:189
  2518.7 229.8 %reduce-scatter.25.cloned.1.call-start = ((), (), s32[]{:S(2)}) async-start(), calls=%async_computation.21 | async-start | bytes 40960
  2665.1 245.4 %copy-start.51 = (f32[1,128,128]{2,1,0:T(8,128)S(1)}, f32[1,128,128]{2,1,0:T(8,128)}, u32[]{:S(2)}) copy-start(f32[1,128,128]{2,1,0:T(8,128)} %param.40) | copy-start | bytes 196612
  2665.1 245.3 %copy-start.67 = (f32[1,128,128]{2,1,0:T(8,128)S(1)}, f32[1,128,128]{2,1,0:T(8,128)}, u32[]{:S(2)}) copy-start(f32[1,128,128]{2,1,0:T(8,128)} %param.48) | copy-start | bytes 196612
  2665.1 245.3 %copy-start.68 = (f32[1,128,128]{2,1,0:T(8,128)S(1)}, f32[1,128,128]{2,1,0:T(8,128)}, u32[]{:S(2)}) copy-start(f32[1,128,128]{2,1,0:T(8,128)} %param.56) | copy-start | bytes 196612
  2730.8 37.5 %reduce-scatter.27.cloned.1.call-start = ((), (), s32[]{:S(2)}) async-start(), calls=%async_computation.22 | async-start | bytes 40960
  2731.6 56.4 %reduce-scatter.15.cloned.1.call-start = ((), (), s32[]{:S(2)}) async-start(), calls=%async_computation.16 | async-start | bytes 40960 | tf_op jit(solution)/shard_map/reduce_scatter | solution.py:424
  2732.2 75.8 %reduce-scatter.19.cloned.1.call-start = ((), (), s32[]{:S(2)}) async-start(), calls=%async_computation.18 | async-start | bytes 40960 | tf_op jit(solution)/shard_map/reduce_scatter | solution.py:433
  2733.0 95.2 %reduce-scatter.17.cloned.1.call-start = ((), (), s32[]{:S(2)}) async-start(), calls=%async_computation.17 | async-start | bytes 163840 | tf_op jit(solution)/shard_map/reduce_scatter | solution.py:427
  2733.7 114.7 %reduce-scatter.23.cloned.1.call-start = ((), (), s32[]{:S(2)}) async-start(), calls=%async_computation.20 | async-start | bytes 163840 | tf_op jit(solution)/shard_map/reduce_scatter | solution.py:439
  2734.5 133.5 %reduce-scatter.13.cloned.1.call-start = ((), (), s32[]{:S(2)}) async-start(), calls=%async_computation.15 | async-start | bytes 204800 | tf_op jit(solution)/shard_map/reduce_scatter | solution.py:421
  2735.0 153.2 %reduce-scatter.21.cloned.1.call-start = ((), (), s32[]{:S(2)}) async-start(), calls=%async_computation.19 | async-start | bytes 327680 | tf_op jit(solution)/shard_map/reduce_scatter | solution.py:436
  (303 other events, 7562.8 us)
Sparse Core Ops, SparseCore 0:
  132.6 179.7 all-gather.4
  314.3 181.0 all-gather.8
  497.3 24.1 all-gather.6
  2731.0 17.4 reduce-scatter.24
  2751.2 17.1 reduce-scatter.26
  2771.0 16.9 reduce-scatter.14
  2791.0 17.0 reduce-scatter.18
  2810.9 17.3 reduce-scatter.16
  2831.1 17.2 reduce-scatter.22
  2850.5 17.3 reduce-scatter.12
  2870.3 17.8 reduce-scatter.20
where the time goes:
time: 2950 us; the launch traced here: 2920 us
  local copies, waits for them, and re-layouts  951 us (32%)
  matrix products  810 us (27%)
  other arithmetic  351 us (12%)
  waiting for transfers between devices  307 us (10%)
  blocking collectives  269 us (9%)
  loops' own time  192 us (7%)
    dynamic_update_slice x336, local copies, waits for them, and re-layouts, attend(): lax.scan(column, jnp.int32(0), jnp.arange(query.shape[2]))  282 us
    dynamic_slice x336, local copies, waits for them, and re-layouts, column_slices(): piece = lax.dynamic_index_in_dim(array, index, 2, keepdims=False)  270 us
    dot_general x96, matrix products, column_scores(): jnp.einsum('bihd,bkhd->bhki', query_col, keys_col, preferred_element_type...  192 us
    all_gather x1, waiting for transfers between devices, incoming_forward(): lax.all_gather(left, 'pair', axis=2, tiled=True)  129 us
    dot_general x7, matrix products, matmul_back(): jnp.einsum('...d,cd->...c', value, weight, preferred_element_type=jnp.flo...  118 us
    dot_general x7, matrix products, matmul(): jnp.einsum('...c,cd->...d', value, weight, preferred_element_type=jnp.flo...  110 us
    another operation x1, loops' own time, attend_back(): lax.scan(column, start, jnp.arange(query.shape[2]))  98 us
    dot_general x48, matrix products, column(): jnp.einsum('bhki,bihd->bkhd', probs.astype(jnp.bfloat16), grad_col, prefe...  96.8 us
  transfers between devices with their start and end apart: 15, of which 11 were waited for; matrix products, arithmetic and copies ran while one was open for 11% of the time, Pallas kernels for 0%

commit v1 on v0

v1 whole, which is shorter than its diff:
```python
import functools

import jax
import jax.numpy as jnp
from jax import lax
from jax.experimental import pallas as pl
from jax.experimental.pallas import tpu as pltpu
from jax.sharding import PartitionSpec as P

STEP = 10

norm_epsilon = 1e-05
clip_limit = 0.001
learn_rate = 0.1
vector_rate = 0.8
beta_first = 0.9
beta_second = 0.999
adam_epsilon = 1e-08
weight_decay = 0.01

BF = jnp.bfloat16
F32 = jnp.float32
LOG2E = 1.4426950408889634
EPS = norm_epsilon


def normalize(stream, gain):
    mean = jnp.mean(stream, axis=-1, keepdims=True)
    centred = stream - mean
    scale = lax.rsqrt(jnp.mean(centred * centred, axis=-1, keepdims=True) + norm_epsilon)
    normed = centred * scale
    return (normed * gain, normed, scale)


def normalize_back(upstream, gain, normed, scale):
    inner = upstream * gain
    below = scale * (
        inner
        - jnp.mean(inner, axis=-1, keepdims=True)
        - normed * jnp.mean(inner * normed, axis=-1, keepdims=True)
    )
    return (below, jnp.sum(upstream * normed, axis=(0, 1, 2)))


def matmul(value, weight):
    return jnp.einsum("...c,cd->...d", value, weight, preferred_element_type=jnp.float32)


def matmul_back(value, weight):
    return jnp.einsum("...d,cd->...c", value, weight, preferred_element_type=jnp.float32)


def weight_grad(left, right):
    flat_left = left.reshape(-1, left.shape[-1])
    flat_right = right.reshape(-1, right.shape[-1])
    return lax.dot_general(
        flat_left, flat_right, (((0,), (0,)), ((), ())), preferred_element_type=jnp.float32
    )


def rounded(value):
    return value.astype(jnp.bfloat16).astype(jnp.float32)


def nn(a, b):
    return lax.dot_general(a, b, (((1,), (0,)), ((), ())), preferred_element_type=F32)

def nt(a, b):
    return lax.dot_general(a, b, (((1,), (1,)), ((), ())), preferred_element_type=F32)

def sigm(v):
    return 0.5 * jnp.tanh(0.5 * v) + 0.5

def norm(v):
    mean = jnp.mean(v, axis=-1, keepdims=True)
    cen = v - mean
    scale = lax.rsqrt(jnp.mean(cen * cen, axis=-1, keepdims=True) + EPS)
    return cen * scale, scale

def norm_back(up, gain, n, scale):
    inner = up * gain
    return scale * (inner - jnp.mean(inner, axis=-1, keepdims=True) - n * jnp.mean(inner * n, axis=-1, keepdims=True))

def chunks(total, width):
    return [(s, min(width, total - s)) for s in range(0, total, width)]

def column_kernel(heads, after_ref, tgt_ref, msk_ref, bias_ref, w_ref, wt_ref, wo_ref, we_ref, vec_ref, z_ref,
                gx_ref, gmid_ref, gb_ref, gkvw_ref, gqgw_ref, gow_ref, gew_ref, svec_ref, small_ref,
                bias2, e_s, gs_s, acc, qbd, gobd, vaug, qn, gon, ores, cu, hv):
    j = pl.program_id(0)
    last = pl.num_programs(0) - 1
    n, c = after_ref.shape[1], after_ref.shape[2]
    dh = c // heads
    wide = heads * n
    scale = dh ** -0.5

    @pl.when(j == 0)
    def _():
        for h in range(heads):
            bias2[:, h * n:(h + 1) * n] = bias_ref[:, h * n:(h + 1) * n].astype(F32).T * LOG2E
        acc[...] = jnp.zeros_like(acc)
        qbd[...] = jnp.zeros_like(qbd)
        gobd[...] = jnp.zeros_like(gobd)
        lane = lax.broadcasted_iota(jnp.int32, (n, c), 1)
        vaug[:, c:] = jnp.where(lane < 3, 1.0, 0.0).astype(BF)
        for ref in (gkvw_ref, gqgw_ref, gow_ref, gew_ref, svec_ref, small_ref):
            ref[...] = jnp.zeros_like(ref)

    lane = lax.broadcasted_iota(jnp.int32, (n, c), 1)
    g3 = vec_ref[2:3, :]
    g4 = vec_ref[3:4, :]
    wr = vec_ref[4:5, :]
    after = after_ref[0]
    n3, _ = norm(after)
    x = (n3 * g3).astype(BF)
    nat = nn(x, w_ref[:, :3 * c])
    k_nat = nat[:, c:2 * c].astype(BF)
    vaug[:, :c] = nat[:, 2 * c:].astype(BF)
    q_nat = (nat[:, :c] * (scale * LOG2E)).astype(BF)
    for h in range(heads):
        qn[h * n:(h + 1) * n, :] = jnp.where((lane >= h * dh) & (lane < (h + 1) * dh), q_nat, jnp.zeros_like(q_nat))
    tr = nt(wt_ref[...], x)
    q_t = (tr[:c] * (scale * LOG2E)).astype(BF)
    k_t = tr[c:2 * c].astype(BF)
    v_t = jnp.concatenate([tr[2 * c:3 * c], jnp.ones((16, n), F32)], axis=0).astype(BF)
    gate_t = sigm(tr[3 * c:])
    for h in range(heads):
        qbd[h * dh:(h + 1) * dh, h * n:(h + 1) * n] = q_t[h * dh:(h + 1) * dh]

    for s0, w0 in chunks(wide, 256):
        sl = slice(s0, s0 + w0)
        sc = nn(k_nat, qbd[:, sl]) + bias2[:, sl]
        top = jnp.max(sc, axis=0, keepdims=True)
        ex = jnp.exp2(sc - top).astype(BF)
        e_s[:, sl] = ex
        ores[:, sl] = nn(v_t, ex)
    o_parts, r_parts = [], []
    for h in range(heads):
        r = 1.0 / ores[c:c + 1, h * n:(h + 1) * n]
        r_parts.append(r)
        o_parts.append(ores[h * dh:(h + 1) * dh, h * n:(h + 1) * n] * r)
    o_t = jnp.concatenate(o_parts, axis=0)
    y_t = (gate_t * o_t).astype(BF)
    out = nn(y_t.astype(F32).T.astype(BF), wo_ref[...]).astype(BF)
    mid = after + out.astype(F32)

    n4, sc4 = norm(mid)
    t = (n4 * g4).astype(BF)
    f = we_ref.shape[1] // 2
    racc = mid * wr
    for q in range(f // 128):
        u = nn(t, we_ref[:, q * 256:(q + 1) * 256])
        a, b = u[:, :128], u[:, 128:]
        zc = z_ref[:, q * 128:(q + 1) * 128]
        sig = sigm(a)
        silu = a * sig
        h_low = (silu * b).astype(BF)
        hv[:, q * 128:(q + 1) * 128] = h_low
        racc += h_low.astype(F32) * zc
        cu[:, q * 256:q * 256 + 128] = (zc * b * (sig + silu - silu * sig)).astype(BF)
        cu[:, q * 256 + 128:(q + 1) * 256] = (zc * silu).astype(BF)
    readout = jnp.sum(racc, axis=-1, keepdims=True)
    pick = lax.broadcasted_iota(jnp.int32, tgt_ref.shape, 1) == j
    tgt = jnp.sum(jnp.where(pick, tgt_ref[...], 0.0), axis=1, keepdims=True)
    msk = jnp.sum(jnp.where(pick, msk_ref[...], 0.0), axis=1, keepdims=True)
    err = readout - tgt
    wer = msk * err
    gr = 2.0 * wer
    small_ref[0:1, :] += jnp.sum(gr * mid, axis=0, keepdims=True)
    small_ref[2:3, :] += jnp.sum(jnp.where(lane == 0, wer * err, 0.0), axis=0, keepdims=True)
    svec_ref[...] += jnp.sum(gr * hv[...].astype(F32), axis=0, keepdims=True)
    gew_ref[...] += nn((gr * t.astype(F32)).T.astype(BF), cu[...])
    gt = gr * nt(cu[...], we_ref[...])
    small_ref[1:2, :] += jnp.sum(gt * n4, axis=0, keepdims=True)
    gmid = gr * wr + norm_back(gt, g4, n4, sc4)
    gmid_ref[0] = gmid

    gout = gmid.astype(BF)
    gow_ref[...] += nn(y_t, gout)
    gy_t = nt(wo_ref[...], gout)
    ggl_t = gy_t * o_t * gate_t * (1.0 - gate_t)
    go_t = (gy_t * gate_t).astype(BF).astype(F32)
    row = lax.broadcasted_iota(jnp.int32, (16, n), 0)
    gos = []
    for h in range(heads):
        part = (go_t[h * dh:(h + 1) * dh] * r_parts[h]).astype(BF)
        gobd[h * dh:(h + 1) * dh, h * n:(h + 1) * n] = part
        part = part.astype(F32)
        gos.append(part)
        d = -jnp.sum(part * o_parts[h], axis=0, keepdims=True)
        hi = d.astype(BF).astype(F32)
        mi = (d - hi).astype(BF).astype(F32)
        lo = d - hi - mi
        gobd[c:, h * n:(h + 1) * n] = jnp.where(row == 0, hi, jnp.where(row == 1, mi, jnp.where(row == 2, lo, 0.0))).astype(BF)
    go_n = jnp.concatenate(gos, axis=0).T.astype(BF)
    for h in range(heads):
        gon[h * n:(h + 1) * n, :] = jnp.where((lane >= h * dh) & (lane < (h + 1) * dh), go_n, jnp.zeros_like(go_n))

    vk = vaug[:, :c + 16]
    for s0, w0 in chunks(wide, 256):
        sl = slice(s0, s0 + w0)
        g = e_s[:, sl].astype(F32) * nn(vk, gobd[:, sl])
        acc[:, sl] += g
        gl = g.astype(BF)
        gs_s[:, sl] = gl
        ores[:c, sl] = nn(k_t, gl)
    gq_t = jnp.concatenate([ores[h * dh:(h + 1) * dh, h * n:(h + 1) * n] for h in range(heads)], axis=0) * scale
    gqg_t = jnp.concatenate([gq_t, ggl_t], axis=0).astype(BF)
    gk = nn(gs_s[...], qn[...]) * (1.0 / LOG2E)
    gv = nn(e_s[...], gon[...])
    gkv = jnp.concatenate([gk, gv], axis=1).astype(BF)
    gqgw_ref[...] += nn(gqg_t, x)
    gkvw_ref[...] += nn(x.astype(F32).T.astype(BF), gkv)
    w_qg = jnp.concatenate([w_ref[:, :c], w_ref[:, 3 * c:]], axis=1)
    gx_ref[0] = nt(gkv, w_ref[:, c:3 * c]) + nn(w_qg, gqg_t).T

    @pl.when(j == last)
    def _():
        for h in range(heads):
            gb_ref[:, h * n:(h + 1) * n] = acc[:, h * n:(h + 1) * n].T.astype(gb_ref.dtype)


def column_pass(after, tgt, msk, bias, w, wt, wo, we, vec, z):
    cols, n, c = after.shape
    heads = bias.shape[1] // n
    f = we.shape[1] // 2
    wide = heads * n
    full = lambda shape: pl.BlockSpec(shape, lambda j: (0,) * len(shape))
    col = pl.BlockSpec((1, n, c), lambda j: (j, 0, 0))
    outs = [
        jax.ShapeDtypeStruct((cols, n, c), F32),
        jax.ShapeDtypeStruct((cols, n, c), F32),
        jax.ShapeDtypeStruct((n, wide), BF),
        jax.ShapeDtypeStruct((c, 2 * c), F32),
        jax.ShapeDtypeStruct((2 * c, c), F32),
        jax.ShapeDtypeStruct((c, c), F32),
        jax.ShapeDtypeStruct((c, 2 * f), F32),
        jax.ShapeDtypeStruct((1, f), F32),
        jax.ShapeDtypeStruct((8, c), F32),
    ]
    return pl.pallas_call(
        functools.partial(column_kernel, heads),
        grid=(cols,),
        in_specs=[col] + [full(v.shape) for v in (tgt, msk, bias, w, wt, wo, we, vec, z)],
        out_specs=[col, col] + [full(o.shape) for o in outs[2:]],
        out_shape=outs,
        scratch_shapes=[
            pltpu.VMEM((n, wide), F32),
            pltpu.VMEM((n, wide), BF),
            pltpu.VMEM((n, wide), BF),
            pltpu.VMEM((n, wide), F32),
            pltpu.VMEM((c, wide), BF),
            pltpu.VMEM((c + 16, wide), BF),
            pltpu.VMEM((n, 2 * c), BF),
            pltpu.VMEM((wide, c), BF),
            pltpu.VMEM((wide, c), BF),
            pltpu.VMEM((c + 16, wide), F32),
            pltpu.VMEM((n, 2 * f), BF),
            pltpu.VMEM((n, f), BF),
        ],
        compiler_params=pltpu.CompilerParams(vmem_limit_bytes=56 << 20),
        name="columns",
    )(after, tgt, msk, bias, w, wt, wo, we, vec, z)


def incoming_parts(stream, tri_w, gain_tri):
    normed_in, normed, scale = normalize(stream, gain_tri)
    normed_low = normed_in.astype(jnp.bfloat16)
    projected = matmul(normed_low, tri_w)
    width = tri_w.shape[0]
    pieces = [projected[..., index * width : (index + 1) * width] for index in range(5)]
    left = (jax.nn.sigmoid(pieces[1]) * pieces[0]).astype(jnp.bfloat16)
    right = (jax.nn.sigmoid(pieces[3]) * pieces[2]).astype(jnp.bfloat16)
    return (normed_low, normed, scale, pieces, left, right)


def incoming_forward(stream, tri_w, tri_out_w, gain_tri, gain_centre):
    _, _, _, pieces, left, right = incoming_parts(stream, tri_w, gain_tri)
    part = jnp.einsum(
        "bkic,bkjc->bijc",
        lax.all_gather(left, "pair", axis=2, tiled=True),
        right,
        preferred_element_type=jnp.float32,
    )
    centre_in, _, _ = normalize(part, gain_centre)
    linear = matmul(centre_in.astype(jnp.bfloat16), tri_out_w)
    branch = (jax.nn.sigmoid(pieces[4]) * linear).astype(jnp.bfloat16)
    return (stream + branch.astype(jnp.float32), part)


def incoming_back(upstream, stream, product, tri_w, tri_out_w, gain_tri, gain_centre):
    normed_low, normed, scale, pieces, left, right = incoming_parts(stream, tri_w, gain_tri)
    centre_in, centre_normed, centre_scale = normalize(product, gain_centre)
    centre_low = centre_in.astype(jnp.bfloat16)
    linear = matmul(centre_low, tri_out_w)
    gate = jax.nn.sigmoid(pieces[4])
    grad_branch = rounded(upstream)
    grad_linear = (grad_branch * gate).astype(jnp.bfloat16)
    grad_gate = grad_branch * linear * gate * (1.0 - gate)
    grad_tri_out = weight_grad(centre_low, grad_linear)
    grad_centre = rounded(matmul_back(grad_linear, tri_out_w))
    grad_product, grad_gain_centre = normalize_back(
        grad_centre, gain_centre, centre_normed, centre_scale
    )
    grad_low = grad_product.astype(jnp.bfloat16)
    row_view = lax.all_to_all(grad_low, "pair", split_axis=1, concat_axis=2, tiled=True)
    left_piece = lax.all_gather(left, "pair", axis=2, tiled=True)
    right_piece = lax.all_gather(right, "pair", axis=2, tiled=True)
    grad_right = jnp.einsum(
        "bkic,bijc->bkjc", left_piece, grad_low, preferred_element_type=jnp.float32
    )
    grad_left = jnp.einsum(
        "bkjc,bijc->bkic", right_piece, row_view, preferred_element_type=jnp.float32
    )
    grad_left = rounded(grad_left)
    grad_right = rounded(grad_right)
    sig_left = jax.nn.sigmoid(pieces[1])
    sig_right = jax.nn.sigmoid(pieces[3])
    grad_projected = jnp.concatenate(
        [
            grad_left * sig_left,
            grad_left * pieces[0] * sig_left * (1.0 - sig_left),
            grad_right * sig_right,
            grad_right * pieces[2] * sig_right * (1.0 - sig_right),
            grad_gate,
        ],
        axis=-1,
    ).astype(jnp.bfloat16)
    grad_tri = weight_grad(normed_low, grad_projected)
    grad_normed = rounded(matmul_back(grad_projected, tri_w))
    below, grad_gain_tri = normalize_back(grad_normed, gain_tri, normed, scale)
    return (upstream + below, grad_tri, grad_tri_out, grad_gain_tri, grad_gain_centre)


def gather_weights(tri, tri_out, attn, bias, outp, expand, shrink, vectors):
    rows = tri.shape[1]
    pieces = [tri[0], tri_out[0], attn[0], outp[0], expand[0], shrink[0].reshape(rows, -1), bias[0], vectors.T]
    widths = [p.shape[1] for p in pieces]
    packed = lax.all_gather(jnp.concatenate([p.astype(BF) for p in pieces], axis=1), "item", axis=0, tiled=True)
    got, at = [], 0
    for w in widths:
        got.append(packed[:, at : at + w])
        at += w
    tri, tri_out, attn, outp, expand, shr, bias, vec = got
    return tri, tri_out, attn, bias, outp, expand, shr.reshape(-1, shrink.shape[2]), vec.T


def on_device(
    pair_act,
    targets,
    pair_mask,
    tri_proj,
    tri_out,
    attention_proj,
    bias_proj,
    output_proj,
    expand_proj,
    shrink_proj,
    vectors,
    first_tri,
    first_tri_out,
    first_attention,
    first_bias,
    first_output,
    first_expand,
    first_shrink,
    first_vectors,
    second_tri,
    second_tri_out,
    second_attention,
    second_bias,
    second_output,
    second_expand,
    second_shrink,
    second_vectors,
):
    layers = attention_proj.shape[0]
    assert layers == 1
    weight = gather_weights(
        tri_proj, tri_out, attention_proj, bias_proj, output_proj, expand_proj, shrink_proj, vectors
    )
    tri_w, tri_out_w, project_w, pairbias_w, output_w, expand_w, shrink_w, vector_low = weight
    vec = vector_low.astype(F32)
    weighting_rows = pair_mask.astype(F32)
    stream = lax.all_to_all(pair_act, "pair", split_axis=2, concat_axis=1, tiled=True).astype(F32)
    both = lax.all_to_all(
        jnp.concatenate([targets, weighting_rows]), "pair", split_axis=2, concat_axis=1, tiled=True
    )
    after, product = incoming_forward(stream, tri_w, tri_out_w, vec[0], vec[1])
    after_c = jnp.swapaxes(after[0], 0, 1)
    inputs_col = normalize(after_c, vec[2])[0].astype(BF)
    cols, tokens, width = after_c.shape
    bias_part = jnp.swapaxes(matmul(inputs_col, pairbias_w).astype(BF), 1, 2)
    bias_full = lax.all_gather(bias_part.reshape(cols, -1), "pair", axis=0, tiled=True)
    hidden = expand_w.shape[1] // 2
    expand_mix = (
        expand_w.reshape(width, 2, hidden // 128, 128).swapaxes(1, 2).reshape(width, 2 * hidden)
    )
    z = jnp.sum(shrink_w.astype(F32) * vec[4], axis=1)[None]
    vec8 = jnp.concatenate([vec, jnp.zeros((3, width), F32)])
    gx, upstream, gb, gkv_w, gqg_w, gow, gew, svec, small = column_pass(
        after_c, both[0], both[1], bias_full, project_w, project_w.T, output_w, expand_mix, vec8, z
    )
    bias_cols = lax.psum_scatter(gb.astype(F32), "pair", scatter_dimension=0, tiled=True)
    bias_low = jnp.swapaxes(bias_cols.reshape(cols, -1, tokens), 1, 2).astype(BF)
    grad_pairbias = weight_grad(inputs_col, bias_low)
    grad_inputs = rounded(gx + matmul_back(bias_low, pairbias_w))
    _, normed, scale = normalize(after_c, vec[2])
    below, grad_gain_attend = normalize_back(grad_inputs[None], vec[2], normed[None], scale[None])
    upstream = jnp.swapaxes(upstream + below[0], 0, 1)[None]
    upstream, grad_tri, grad_tri_out, grad_gain_tri, grad_gain_centre = incoming_back(
        upstream, stream, product, tri_w, tri_out_w, vec[0], vec[1]
    )
    summed = lax.psum(
        (
            grad_tri,
            grad_tri_out,
            gkv_w,
            gqg_w,
            grad_pairbias,
            gow,
            gew,
            svec,
            small,
            jnp.stack([grad_gain_tri, grad_gain_centre, grad_gain_attend]),
            jnp.sum(weighting_rows),
        ),
        ("item", "pair"),
    )
    g_tri, g_tri_out, g_kv, g_qg, g_bias, g_out, g_exp, s_sum, sm, gains, count = summed
    g_project = jnp.concatenate([g_qg[:width].T, g_kv, g_qg[width:].T], axis=1)
    g_expand = (
        g_exp.reshape(width, hidden // 128, 2, 128).swapaxes(1, 2).reshape(width, 2 * hidden)
    )
    g_shrink = s_sum[0][:, None] * vec[4][None, :]
    g_read = sm[0] + jnp.sum(s_sum[0][:, None] * shrink_w.astype(F32), axis=0)
    g_vec = jnp.concatenate([gains, sm[1:2], g_read[None]])
    grads = [
        g / count for g in (g_tri, g_tri_out, g_project, g_bias, g_out, g_expand, g_shrink, g_vec)
    ]
    loss_sum = jnp.sum(sm[2])
    grad_norm = jnp.sqrt(sum(jnp.sum(g * g) for g in grads))
    factor = jnp.minimum(1.0, clip_limit / (grad_norm + 1e-06))
    place = lax.axis_index("item")
    shards = []
    for master, grad in zip((tri_proj, tri_out, attention_proj, bias_proj, output_proj, expand_proj, shrink_proj), grads):
        rows = master.shape[1]
        shards.append(lax.dynamic_slice_in_dim(grad, place * rows, rows, 0)[None])
    shards.append(lax.dynamic_slice_in_dim(grads[7], place * vectors.shape[1], vectors.shape[1], 1))
    masters = (
        tri_proj,
        tri_out,
        attention_proj,
        bias_proj,
        output_proj,
        expand_proj,
        shrink_proj,
        vectors,
    )
    firsts = (
        first_tri,
        first_tri_out,
        first_attention,
        first_bias,
        first_output,
        first_expand,
        first_shrink,
        first_vectors,
    )
    seconds = (
        second_tri,
        second_tri_out,
        second_attention,
        second_bias,
        second_output,
        second_expand,
        second_shrink,
        second_vectors,
    )
    rates = (learn_rate,) * 7 + (vector_rate,)
    new_masters, new_firsts, new_seconds = ([], [], [])
    for master, grad, first, second, rate in zip(masters, shards, firsts, seconds, rates):
        clipped = grad * factor
        moment = beta_first * first + (1 - beta_first) * clipped
        square = beta_second * second + (1 - beta_second) * clipped * clipped
        stride = (
            moment
            / (1 - beta_first**STEP)
            / (jnp.sqrt(square / (1 - beta_second**STEP)) + adam_epsilon)
        )
        new_masters.append(master - rate * (stride + weight_decay * master))
        new_firsts.append(moment)
        new_seconds.append(square)
    return (
        (loss_sum, count, grad_norm) + tuple(new_masters) + tuple(new_firsts) + tuple(new_seconds)
    )


def solution(mesh):
    in_specs = (
        P("item", "pair", None, None),
        P("item", "pair", None),
        P("item", "pair", None),
        P(None, "item", None),
        P(None, "item", None),
        P(None, "item", None),
        P(None, "item", None),
        P(None, "item", None),
        P(None, "item", None),
        P(None, "item", None),
        P(None, "item"),
        P(None, "item", None),
        P(None, "item", None),
        P(None, "item", None),
        P(None, "item", None),
        P(None, "item", None),
        P(None, "item", None),
        P(None, "item", None),
        P(None, "item"),
        P(None, "item", None),
        P(None, "item", None),
        P(None, "item", None),
        P(None, "item", None),
        P(None, "item", None),
        P(None, "item", None),
        P(None, "item", None),
        P(None, "item"),
    )
    out_specs = (
        P(),
        P(),
        P(),
        P(None, "item", None),
        P(None, "item", None),
        P(None, "item", None),
        P(None, "item", None),
        P(None, "item", None),
        P(None, "item", None),
        P(None, "item", None),
        P(None, "item"),
        P(None, "item", None),
        P(None, "item", None),
        P(None, "item", None),
        P(None, "item", None),
        P(None, "item", None),
        P(None, "item", None),
        P(None, "item", None),
        P(None, "item"),
        P(None, "item", None),
        P(None, "item", None),
        P(None, "item", None),
        P(None, "item", None),
        P(None, "item", None),
        P(None, "item", None),
        P(None, "item", None),
        P(None, "item"),
    )
    return jax.shard_map(
        on_device, mesh=mesh, in_specs=in_specs, out_specs=out_specs, check_vma=False
    )
```

time: 2950 us -> 1490 us (0.51)
  local copies, waits for them, and re-layouts: 951 us -> 176 us
  matrix products: 810 us -> 171 us
  Pallas kernels: 0 us -> 346 us
  waiting for transfers between devices: 307 us -> 545 us
  blocking collectives: 269 us -> 60.4 us
  other arithmetic: 351 us -> 153 us
  loops' own time: 192 us -> 0 us
    dot_general x336 -> x0, matrix products: 446 us -> none  [the longest x96 192 us: column_scores(): jnp.einsum('bihd,bkhd->bhki', query_col, keys_col, preferred_element_type...]
    pallas_call x0 -> x1, Pallas kernels: none -> 346 us  [column_pass(): pl.pallas_call(functools.partial(column_kernel, heads), grid=(cols,), in_...]
    dynamic_slice x432 -> x0, local copies, waits for them, and re-layouts: 326 us -> none  [the longest x336 270 us: column_slices(): piece = lax.dynamic_index_in_dim(array, index, 2, keepdims=False)]
    dynamic_update_slice x336 -> x0, local copies, waits for them, and re-layouts: 282 us -> none  [attend(): lax.scan(column, jnp.int32(0), jnp.arange(query.shape[2]))]
    another operation x2 -> x0, loops' own time: 192 us -> none  [the longest x1 98 us: attend_back(): lax.scan(column, start, jnp.arange(query.shape[2]))]
    all_gather x1, waiting for transfers between devices: 0.01 us -> 161 us  [incoming_back(): right_piece = lax.all_gather(right, 'pair', axis=2, tiled=True)]
    psum x0 -> x1, waiting for transfers between devices: none -> 130 us  [on_device(): lax.psum((grad_tri, grad_tri_out, gkv_w, gqg_w, grad_pairbias, gow, gew,...]
    while x389 -> x0, local copies, waits for them, and re-layouts: 95.1 us -> none
  transfers between devices with their start and end apart: 15 -> 8, of which waited for: 11 -> 7; matrix products, arithmetic and copies ran while one was open for 11% -> 12% of each run, Pallas kernels for 0% -> 0%
where the time goes in v1:
time: 1490 us
  waiting for transfers between devices  545 us (37%)
  Pallas kernels  346 us (23%)
  local copies, waits for them, and re-layouts  176 us (12%)
  matrix products  171 us (11%)
  other arithmetic  153 us (10%)
  blocking collectives  60.4 us (4%)
  between operations  21.7 us (1%)
    pallas_call x1, Pallas kernels, column_pass(): pl.pallas_call(functools.partial(column_kernel, heads), grid=(cols,), in_...  346 us
    all_gather x1, waiting for transfers between devices, incoming_forward(): lax.all_gather(left, 'pair', axis=2, tiled=True)  173 us
    all_gather x1, waiting for transfers between devices, incoming_back(): right_piece = lax.all_gather(right, 'pair', axis=2, tiled=True)  161 us
    psum x1, waiting for transfers between devices, on_device(): lax.psum((grad_tri, grad_tri_out, gkv_w, gqg_w, grad_pairbias, gow, gew,...  130 us
    all_gather x1, local copies, waits for them, and re-layouts, incoming_back(): right_piece = lax.all_gather(right, 'pair', axis=2, tiled=True)  52.5 us
    all_gather x1, local copies, waits for them, and re-layouts, incoming_forward(): lax.all_gather(left, 'pair', axis=2, tiled=True)  52.4 us
    dot_general x3, matrix products, matmul(): jnp.einsum('...c,cd->...d', value, weight, preferred_element_type=jnp.flo...  41.6 us
    unnamed x11, other arithmetic  40.8 us
  transfers between devices with their start and end apart: 8, of which 7 were waited for; matrix products, arithmetic and copies ran while one was open for 12% of the time, Pallas kernels for 0%

profile of v1, /device:TPU:0, one launch (start us, length us, event | category | flops | bytes accessed | tf_op | source)
XLA Modules:
  0.0 1486.3 jit_solution(8573855106446438576)
XLA Ops:
  20.6 20.8 %all_gather.13 = bf16[128,2953]{1,0:T(8,128)(2,1)S(1)} all-gather(bf16[32,2953]{1,0:T(8,128)(2,1)S(1)} %concatenate.35), channel_id=1, replica_groups=mesh['item'=4,'pair'=8] {'item'}, dimensions={0}, use_global_device_ids=true | all-gather | bytes 944960 | tf_op jit(solution)/shard_map/all_gather | solution.py:339
  41.7 33.3 %all-to-all-done = bf16[1,48,384,128]{3,1,0,2:T(8,128)(2,1)} async-done(((bf16[1,48,384,128]{3,1,0,2:T(8,128)(2,1)}), bf16[1,48,384,128]{3,1,0,2:T(8,128)(2,1)}, u32[]{:S(2)}, u32[]{:S(2)}) %all-to-all-start) | async-done | bytes 4718624 | tf_op jit(solution)/shard_map/all_to_all | solution.py:385
  94.5 20.4 %convolution_bitcast_fusion = f32[1,384,48,640]{3,1,2,0:T(8,128)} fusion(f32[384,48,128]{2,0,1:T(8,128)} %bitcast.371, f32[128]{0:T(128)S(1)} %get-tuple-element.117, f32[384,48]{0,1:T(8,128)S(1)} %rsqrt.35, f32[384,48]{0,1:T(8,128)S(1)} %div.222, bf16[128,2953]{1,0:T(8,128)(2,1)S(1)} %all_gather.13), kind=kOutput, calls=%fused_computation.6 | convolution fusion | flops 3029336064 | bytes 56934912 | tf_op jit(solution)/shard_map/...c,cd->...d/dot_general | solution.py:46
  114.9 17.8 %fusion.58 = (bf16[1,384,48,128]{3,1,0,2:T(8,128)(2,1)}, bf16[1,384,48,128]{3,1,2,0:T(8,128)(2,1)}) fusion(f32[1,384,48,640]{3,1,2,0:T(8,128)} %convolution_bitcast_fusion), kind=kLoop, calls=%fused_computation.88 | loop fusion | flops 23592960 | bytes 47185920 | tf_op jit(solution)/shard_map/convert_element_type | solution.py:272
  140.1 172.5 %all-gather.4.cloned.1.call-done = bf16[1,384,384,128]{3,1,0,2:T(8,128)(2,1)} async-done(((bf16[1,384,48,128]{3,1,0,2:T(8,128)(2,1)}), bf16[1,384,384,128]{3,1,0,2:T(8,128)(2,1)}) %all-gather.4.cloned.1.call-update) | async-done | bytes 37748752 | tf_op jit(solution)/shard_map/all_gather | solution.py:281
  312.6 52.4 %copy.192 = bf16[1,384,384,128]{2,1,3,0:T(8,128)(2,1)} copy(bf16[1,384,384,128]{3,1,0,2:T(8,128)(2,1)} %all-gather.4.cloned.1.call-done) | data formatting | bytes 75497472 | tf_op jit(solution)/shard_map/all_gather | solution.py:281
  365.0 20.2 %bitcast_reduce_fusion = (f32[384,48]{0,1:T(8,128)S(1)}, f32[128,48,384]{2,1,0:T(8,128)}) fusion(bf16[384,48,128]{0,1,2:T(8,128)(2,1)} %copy.193, bf16[1,384,384,128]{2,1,3,0:T(8,128)(2,1)} %copy.192), kind=kOutput, calls=%fused_computation.70 | convolution fusion | flops 1814280192 | bytes 51978240 | tf_op jit(solution)/shard_map/bkic,bkjc->bijc/dot_general | solution.py:279
  395.0 12.4 bitcast_add_fusion
  449.3 345.7 %columns.1 = (f32[48,384,128]{2,1,0:T(8,128)}, f32[48,384,128]{2,1,0:T(8,128)}, bf16[384,1536]{1,0:T(8,128)(2,1)}, f32[128,256]{1,0:T(8,128)}, f32[256,128]{1,0:...) custom-call(f32[48,384,128]{2,1,0:T(8,128)} %bitcast.364, ...), custom_call_target="tpu_custom_call" | custom-call | tf_op jit(solution)/shard_map/columns/pallas_call | solution.py:241
  795.6 36.3 %reduce-scatter.2.cloned.1.call-done = bf16[48,1536]{1,0:T(8,128)(2,1)} async-done(((bf16[384,1536]{1,0:T(8,128)(2,1)}), bf16[48,1536]{1,0:T(8,128)(2,1)}) %reduce-scatter.2.cloned.1.call-update) | async-done | bytes 147472 | tf_op jit(solution)/shard_map/reduce_scatter | solution.py:404
  832.9 19.5 %fusion.17 = (f32[128]{0:T(128)}, f32[48,384]{1,0:T(8,128)S(1)}, f32[48,384]{1,0:T(8,128)S(1)}, bf16[48,384,128]{2,1,0:T(8,128)(2,1)S(1)}) fusion(f32[48,384]{1,0:T(8,128)S(1)} %add_rsqrt_fusion.1, f32[48,384]{1,0:T(8,128)S(1)} %broadcast_multiply_fusion.3, f32[1,384,48,128]{3,1,2,0:T(8,128)} %copy-done, f32[128]{0:T(128)S(1)} %get-tuple-element.115, ...), kind=kOutput, calls=%fused_computation.24 | convolution fusion | flops 44789632 | bytes 24069120 | tf_op jit(solution)/shard_map/...d,cd->...c/dot_general | solution.py:50
  852.4 15.0 %fusion.68 = bf16[384,48,128]{2,0,1:T(8,128)(2,1)S(1)} fusion(f32[48,384,128]{2,1,0:T(8,128)} %get-tuple-element.37, f32[48,384]{1,0:T(8,128)S(1)} %broadcast_multiply_fusion.1, f32[48,384]{1,0:T(8,128)S(1)} %broadcast_multiply_fusion.3, f32[1,384,48,128]{3,1,2,0:T(8,128)S(1)} %bitcast.366, f32[48,384]{1,0:T(8,128)S(1)} %broadcast_multiply_fusion.2, ...), kind=kLoop, calls=%fused_computation.98 | loop fusion | flops 37748736 | bytes 38044160 | tf_op jit(solution)/shard_map/reshape.35
  895.6 160.8 %all-gather.8.cloned.1.call-done = bf16[1,384,384,128]{3,1,0,2:T(8,128)(2,1)} async-done(((bf16[1,384,48,128]{3,1,0,2:T(8,128)(2,1)}), bf16[1,384,384,128]{3,1,0,2:T(8,128)(2,1)}) %all-gather.8.cloned.1.call-update) | async-done | bytes 37748752 | tf_op jit(solution)/shard_map/all_gather | solution.py:308
  1056.4 52.5 %copy.209 = bf16[1,384,384,128]{2,1,3,0:T(8,128)(2,1)} copy(bf16[1,384,384,128]{3,1,0,2:T(8,128)(2,1)} %all-gather.8.cloned.1.call-done) | data formatting | bytes 75497472 | tf_op jit(solution)/shard_map/all_gather | solution.py:308
  1108.9 21.0 %fusion.2 = bf16[128,48,384]{2,1,0:T(8,128)(2,1)} fusion(bf16[1,384,384,128]{2,1,3,0:T(8,128)(2,1)} %copy.192, bf16[1,384,48,128]{1,2,3,0:T(8,128)(2,1)} %fusion.21), kind=kOutput, calls=%fused_computation.2 | convolution fusion | flops 1811939328 | bytes 47185920 | tf_op jit(solution)/shard_map/bkic,bijc->bkjc/dot_general | solution.py:309
  1136.9 11.4 convolution_bitcast_fusion.2
  1165.9 21.0 %fusion = bf16[128,48,384]{2,1,0:T(8,128)(2,1)} fusion(bf16[48,384,128]{1,0,2:T(8,128)(2,1)} %copy.210, bf16[1,384,384,128]{2,1,3,0:T(8,128)(2,1)} %copy.209), kind=kOutput, calls=%fused_computation | convolution fusion | flops 1811939328 | bytes 47185920 | tf_op jit(solution)/shard_map/bkjc,bijc->bkic/dot_general | solution.py:312
  1203.7 10.4 fusion.61
  1223.3 11.4 fusion.65
  1234.8 15.2 %fusion.70 = bf16[384,48,640]{2,0,1:T(8,128)(2,1)} fusion(bf16[384,48,640]{2,0,1:T(8,128)(2,1)} %fusion.65, f32[384,48,128]{2,0,1:T(8,128)} %get-tuple-element.122, f32[48,384,128]{2,1,0:T(8,128)} %get-tuple-element.37, f32[48,384]{1,0:T(8,128)S(1)} %broadcast_multiply_fusion.1, f32[48,384]{1,0:T(8,128)S(1)} %broadcast_multiply_fusion.3, ...), kind=kLoop, calls=%fused_computation.100 | loop fusion | flops 44826624 | bytes 47481344 | tf_op jit(solution)/shard_map/concatenate | solution.py:319
  1250.1 12.1 multiply_reduce_fusion
  1262.5 17.9 %convolution_bitcast_fusion.1 = f32[128,640]{1,0:T(8,128)} fusion(bf16[384,48,640]{2,0,1:T(8,128)(2,1)} %fusion.70, f32[384,48,128]{2,0,1:T(8,128)S(1)} %bitcast.375, f32[128]{0:T(128)S(1)} %copy-done.35, f32[384,48]{0,1:T(8,128)S(1)} %copy-done.10, f32[384,48]{0,1:T(8,128)S(1)} %copy-done.8), kind=kOutput, calls=%fused_computation.106 | convolution fusion | flops 3029336064 | bytes 33505792 | tf_op jit(solution)/shard_map/dot_general | solution.py:56
  1280.5 39.6 %all-reduce.1 = (f32[8,128]{1,0:T(8,128)S(1)}, f32[]{:T(128)}, f32[128,4]{0,1:T(4,128)S(1)}, f32[512]{0:T(512)S(1)}, f32[3,128]{1,0:T(4,128)S(1)}) all-reduce(f32[8,128]{1,0:T(8,128)S(1)} %copy-done.46, f32[]{:T(128)} %convert_reduce_fusion, ...), channel_id=1, replica_groups=mesh['item'=4,'pair'=8] {'item','pair'}, use_global_device_ids=true, to_apply=%region_7.0 | all-reduce | flops 2433 | bytes 19464 | tf_op jit(solution)/shard_map/psum | solution.py:414
  1324.6 129.7 %all-reduce.5.cloned.1.call-done = (f32[128,640]{1,0:T(8,128)}, f32[128,128]{1,0:T(8,128)}, f32[256,128]{1,0:T(8,128)}, f32[128,256]{1,0:T(8,128)}, f32[128,128]{1,0:T(8,128)}, /*index=5*/f32[128,1024]{1,0:T(8,128)}) async-done(((f32[128,640]{1,0:T(8,128)}, f32[128,128]{1,0:T(8,128)}, f32[256,128]{1,0:T(8,128)}, f32[128,256]{1,0:T(8,128)}, f32[128,128]{1,0:T(8,128)}, /*index=5*/f32[128,1024]{1,0:T(8,128)}), ...) | async-done | bytes 1245200 | tf_op jit(solution)/shard_map/psum | solution.py:414
  (260 shorter events, 195.4 us)
Async XLA Ops:
  14.9 60.0 %all-to-all-start = ((bf16[1,48,384,128]{3,1,0,2:T(8,128)(2,1)}), bf16[1,48,384,128]{3,1,0,2:T(8,128)(2,1)}, u32[]{:S(2)}, u32[]{:S(2)}) async-start(bf16[1,48,384,128]{3,1,0,2:T(8,128)(2,1)} %copy.186), calls=%async_computation | async-start | bytes 9437184 | tf_op jit(solution)/shard_map/all_to_all | solution.py:385
  20.1 292.5 %all-gather.4.cloned.1.call-start = ((), (), s32[]{:S(2)}) async-start(), calls=%async_computation.4 | async-start | bytes 42467328 | tf_op jit(solution)/shard_map/all_gather | solution.py:281
  41.7 391.8 %copy-start.44 = (f32[128]{0:T(128)}, f32[128]{0:T(128)S(1)}, u32[]{:S(2)}) copy-start(f32[128]{0:T(128)S(1)} %get-tuple-element.114) | copy-start | bytes 1540
  132.7 316.6 %all-gather.6.cloned.1.call-start = ((), (), s32[]{:S(2)}) async-start(), calls=%async_computation.5 | async-start | bytes 1327104 | tf_op jit(solution)/shard_map/all_gather | solution.py:394
  426.6 9.1 all-to-all-start.1
  430.0 401.9 %reduce-scatter.2.cloned.1.call-start = ((), (), s32[]{:S(2)}) async-start(), calls=%async_computation.6 | async-start | bytes 1327104 | tf_op jit(solution)/shard_map/reduce_scatter | solution.py:404
  430.8 364.2 %copy-start.5 = (f32[512,128]{1,0:T(8,128)}, f32[512,128]{1,0:T(8,128)S(1)}, u32[]{:S(2)}) copy-start(f32[512,128]{1,0:T(8,128)S(1)} %reshape.412) | copy-start | bytes 786436
  795.0 261.4 %all-gather.8.cloned.1.call-start = ((), (), s32[]{:S(2)}) async-start(), calls=%async_computation.7 | async-start | bytes 42467328 | tf_op jit(solution)/shard_map/all_gather | solution.py:308
  890.3 262.7 %all-to-all-start.2 = ((bf16[1,384,48,128]{3,2,0,1:T(8,128)(2,1)}), bf16[1,384,48,128]{3,2,0,1:T(8,128)(2,1)}, u32[]{:S(2)}, u32[]{:S(2)}) async-start(bf16[1,384,48,128]{3,2,0,1:T(8,128)(2,1)} %copy.206), calls=%async_computation.3 | async-start | bytes 9437184 | tf_op jit(solution)/shard_map/all_to_all | solution.py:306
  894.9 559.4 %all-reduce.5.cloned.1.call-start = ((), (), s32[]{:S(2)}) async-start(), calls=%async_computation.8 | async-start | bytes 2490368 | tf_op jit(solution)/shard_map/psum | solution.py:414
  1262.3 210.4 %copy-start.41 = (f32[5,32]{1,0:T(8,128)S(1)}, f32[5,32]{1,0:T(8,128)}, u32[]{:S(2)}) copy-start(f32[5,32]{1,0:T(8,128)} %param.37) | copy-start | bytes 1924
  1262.3 210.4 %copy-start.47 = (f32[5,32]{1,0:T(8,128)S(1)}, f32[5,32]{1,0:T(8,128)}, u32[]{:S(2)}) copy-start(f32[5,32]{1,0:T(8,128)} %param.45) | copy-start | bytes 1924
  1262.3 211.1 %copy-start.13 = (f32[1,32,1024]{2,1,0:T(8,128)S(1)}, f32[1,32,1024]{2,1,0:T(8,128)}, u32[]{:S(2)}) copy-start(f32[1,32,1024]{2,1,0:T(8,128)} %param.35) | copy-start | bytes 393220
  1262.3 211.1 %copy-start.21 = (f32[1,32,1024]{2,1,0:T(8,128)S(1)}, f32[1,32,1024]{2,1,0:T(8,128)}, u32[]{:S(2)}) copy-start(f32[1,32,1024]{2,1,0:T(8,128)} %param.43) | copy-start | bytes 393220
  1262.3 211.1 %copy-start.22 = (f32[1,32,1024]{2,1,0:T(8,128)S(1)}, f32[1,32,1024]{2,1,0:T(8,128)}, u32[]{:S(2)}) copy-start(f32[1,32,1024]{2,1,0:T(8,128)} %param.51) | copy-start | bytes 393220
  1262.3 211.9 %copy-start.31 = (f32[1,32,128]{2,1,0:T(8,128)S(1)}, f32[1,32,128]{2,1,0:T(8,128)}, u32[]{:S(2)}) copy-start(f32[1,32,128]{2,1,0:T(8,128)} %param.34) | copy-start | bytes 49156
  1262.4 211.9 %copy-start.36 = (f32[1,32,128]{2,1,0:T(8,128)S(1)}, f32[1,32,128]{2,1,0:T(8,128)}, u32[]{:S(2)}) copy-start(f32[1,32,128]{2,1,0:T(8,128)} %param.42) | copy-start | bytes 49156
  1262.4 211.9 %copy-start.37 = (f32[1,32,128]{2,1,0:T(8,128)S(1)}, f32[1,32,128]{2,1,0:T(8,128)}, u32[]{:S(2)}) copy-start(f32[1,32,128]{2,1,0:T(8,128)} %param.50) | copy-start | bytes 49156
  1262.4 212.5 %copy-start.43 = (f32[1,32,4]{1,2,0:T(4,128)S(1)}, f32[1,32,4]{1,2,0:T(4,128)}, u32[]{:S(2)}) copy-start(f32[1,32,4]{1,2,0:T(4,128)} %param.33) | copy-start | bytes 1540
  1262.4 212.5 %copy-start.50 = (f32[1,32,4]{1,2,0:T(4,128)S(1)}, f32[1,32,4]{1,2,0:T(4,128)}, u32[]{:S(2)}) copy-start(f32[1,32,4]{1,2,0:T(4,128)} %param.41) | copy-start | bytes 1540
  1262.4 212.5 %copy-start.51 = (f32[1,32,4]{1,2,0:T(4,128)S(1)}, f32[1,32,4]{1,2,0:T(4,128)}, u32[]{:S(2)}) copy-start(f32[1,32,4]{1,2,0:T(4,128)} %param.49) | copy-start | bytes 1540
  1262.4 213.1 %copy-start.18 = (f32[1,32,512]{2,1,0:T(8,128)S(1)}, f32[1,32,512]{2,1,0:T(8,128)}, u32[]{:S(2)}) copy-start(f32[1,32,512]{2,1,0:T(8,128)} %param.32) | copy-start | bytes 196612
  1262.4 213.1 %copy-start.26 = (f32[1,32,512]{2,1,0:T(8,128)S(1)}, f32[1,32,512]{2,1,0:T(8,128)}, u32[]{:S(2)}) copy-start(f32[1,32,512]{2,1,0:T(8,128)} %param.40) | copy-start | bytes 196612
  1262.4 213.1 %copy-start.27 = (f32[1,32,512]{2,1,0:T(8,128)S(1)}, f32[1,32,512]{2,1,0:T(8,128)}, u32[]{:S(2)}) copy-start(f32[1,32,512]{2,1,0:T(8,128)} %param.48) | copy-start | bytes 196612
  (55 other events, 2805.7 us)
Sparse Core Ops, SparseCore 0:
  132.8 179.7 all-gather.3
  425.2 24.0 all-gather.5
  795.1 36.7 reduce-scatter.1
  833.8 222.4 all-gather.7
  1320.2 134.0 all-reduce.4

commit v2 on v1

--- a/solution.py
+++ b/solution.py
@@ -22,44 +22,6 @@
 F32 = jnp.float32
 LOG2E = 1.4426950408889634
 EPS = norm_epsilon
-
-
-def normalize(stream, gain):
-    mean = jnp.mean(stream, axis=-1, keepdims=True)
-    centred = stream - mean
-    scale = lax.rsqrt(jnp.mean(centred * centred, axis=-1, keepdims=True) + norm_epsilon)
-    normed = centred * scale
-    return (normed * gain, normed, scale)
-
-
-def normalize_back(upstream, gain, normed, scale):
-    inner = upstream * gain
-    below = scale * (
-        inner
-        - jnp.mean(inner, axis=-1, keepdims=True)
-        - normed * jnp.mean(inner * normed, axis=-1, keepdims=True)
-    )
-    return (below, jnp.sum(upstream * normed, axis=(0, 1, 2)))
-
-
-def matmul(value, weight):
-    return jnp.einsum("...c,cd->...d", value, weight, preferred_element_type=jnp.float32)
-
-
-def matmul_back(value, weight):
-    return jnp.einsum("...d,cd->...c", value, weight, preferred_element_type=jnp.float32)
-
-
-def weight_grad(left, right):
-    flat_left = left.reshape(-1, left.shape[-1])
-    flat_right = right.reshape(-1, right.shape[-1])
-    return lax.dot_general(
-        flat_left, flat_right, (((0,), (0,)), ((), ())), preferred_element_type=jnp.float32
-    )
-
-
-def rounded(value):
-    return value.astype(jnp.bfloat16).astype(jnp.float32)
 
 
 def nn(a, b):
@@ -263,73 +225,304 @@
     )(after, tgt, msk, bias, w, wt, wo, we, vec, z)
 
 
-def incoming_parts(stream, tri_w, gain_tri):
-    normed_in, normed, scale = normalize(stream, gain_tri)
-    normed_low = normed_in.astype(jnp.bfloat16)
-    projected = matmul(normed_low, tri_w)
-    width = tri_w.shape[0]
-    pieces = [projected[..., index * width : (index + 1) * width] for index in range(5)]
-    left = (jax.nn.sigmoid(pieces[1]) * pieces[0]).astype(jnp.bfloat16)
-    right = (jax.nn.sigmoid(pieces[3]) * pieces[2]).astype(jnp.bfloat16)
-    return (normed_low, normed, scale, pieces, left, right)
-
-
-def incoming_forward(stream, tri_w, tri_out_w, gain_tri, gain_centre):
-    _, _, _, pieces, left, right = incoming_parts(stream, tri_w, gain_tri)
-    part = jnp.einsum(
-        "bkic,bkjc->bijc",
-        lax.all_gather(left, "pair", axis=2, tiled=True),
-        right,
-        preferred_element_type=jnp.float32,
-    )
-    centre_in, _, _ = normalize(part, gain_centre)
-    linear = matmul(centre_in.astype(jnp.bfloat16), tri_out_w)
-    branch = (jax.nn.sigmoid(pieces[4]) * linear).astype(jnp.bfloat16)
-    return (stream + branch.astype(jnp.float32), part)
-
-
-def incoming_back(upstream, stream, product, tri_w, tri_out_w, gain_tri, gain_centre):
-    normed_low, normed, scale, pieces, left, right = incoming_parts(stream, tri_w, gain_tri)
-    centre_in, centre_normed, centre_scale = normalize(product, gain_centre)
-    centre_low = centre_in.astype(jnp.bfloat16)
-    linear = matmul(centre_low, tri_out_w)
-    gate = jax.nn.sigmoid(pieces[4])
-    grad_branch = rounded(upstream)
-    grad_linear = (grad_branch * gate).astype(jnp.bfloat16)
-    grad_gate = grad_branch * linear * gate * (1.0 - gate)
-    grad_tri_out = weight_grad(centre_low, grad_linear)
-    grad_centre = rounded(matmul_back(grad_linear, tri_out_w))
-    grad_product, grad_gain_centre = normalize_back(
-        grad_centre, gain_centre, centre_normed, centre_scale
-    )
-    grad_low = grad_product.astype(jnp.bfloat16)
-    row_view = lax.all_to_all(grad_low, "pair", split_axis=1, concat_axis=2, tiled=True)
-    left_piece = lax.all_gather(left, "pair", axis=2, tiled=True)
-    right_piece = lax.all_gather(right, "pair", axis=2, tiled=True)
-    grad_right = jnp.einsum(
-        "bkic,bijc->bkjc", left_piece, grad_low, preferred_element_type=jnp.float32
-    )
-    grad_left = jnp.einsum(
-        "bkjc,bijc->bkic", right_piece, row_view, preferred_element_type=jnp.float32
-    )
-    grad_left = rounded(grad_left)
-    grad_right = rounded(grad_right)
-    sig_left = jax.nn.sigmoid(pieces[1])
-    sig_right = jax.nn.sigmoid(pieces[3])
-    grad_projected = jnp.concatenate(
-        [
-            grad_left * sig_left,
-            grad_left * pieces[0] * sig_left * (1.0 - sig_left),
-            grad_right * sig_right,
-            grad_right * pieces[2] * sig_right * (1.0 - sig_right),
-            grad_gate,
+GROUP = 16
+
+
+def spread(scr, start, count, stride, value):
+    for t in range(scr.shape[0]):
+        scr[t, pl.ds(start, count, stride=stride), :] = value[:, t * 128 : (t + 1) * 128]
+
+
+def joined(scr, rows=slice(None)):
+    return jnp.concatenate([scr[t, rows] for t in range(scr.shape[0])], axis=1)
+
+
+def padded(count):
+    return -(-count // 128) * 128
+
+
+def operand_kernel(cols, off_ref, x_ref, wl_ref, wr_ref, *refs):
+    left_ref, right_ref, n_ref, nc_ref, xc_ref, lscr, rscr, nscr, xscr, cscr = refs[-10:]
+    rows, n, c = x_ref.shape
+    half = wl_ref.shape[0] // 2
+    wide = nc_ref.shape[1]
+    own = off_ref[0]
+    other = off_ref[1]
+
+    def step(k, carry):
+        x = x_ref[k].astype(F32)
+        nrm, _ = norm(x)
+        low = nrm.astype(BF)
+        n_ref[k] = low
+        nscr[...] = nrm
+        xscr[...] = x
+        p = nt(wl_ref[...], low)
+        spread(lscr, k, half, rows, p[:half] * sigm(p[half:]))
+        near = [nscr[pl.ds(own, cols), :], nscr[pl.ds(other, cols), :]]
+        if wide > 2 * cols:
+            near.append(jnp.zeros((wide - 2 * cols, c), F32))
+        near = jnp.concatenate(near, axis=0).astype(BF)
+        nc_ref[k] = near
+        p = nt(wr_ref[...], near)
+        spread(rscr, k, half, rows, p[:half] * sigm(p[half:]))
+        cscr[pl.ds(k, cols, stride=rows), :] = xscr[pl.ds(own, cols), :]
+        return carry
+
+    lax.fori_loop(0, rows, step, 0)
+    left_ref[...] = joined(lscr).astype(BF).reshape(left_ref.shape)
+    right_ref[...] = joined(rscr).astype(BF).reshape(right_ref.shape)
+    xc_ref[...] = cscr[...].astype(BF).reshape(xc_ref.shape)
+
+
+def operands(offs, x, wl, wr, cols, place, bufs):
+    n, c = x.shape[1], x.shape[2]
+    half = wl.shape[0] // 2
+    wide = padded(2 * cols)
+    g = GROUP
+    shapes = [
+        ((half, n, n), (half, g, n), lambda b: (0, place(b), 0)),
+        ((half, n, wide), (half, g, wide), lambda b: (0, place(b), 0)),
+        ((n, n, c), (g, n, c), lambda b: (place(b), 0, 0)),
+        ((n, wide, c), (g, wide, c), lambda b: (place(b), 0, 0)),
+        ((cols, n, c), (cols, g, c), lambda b: (0, place(b), 0)),
+    ]
+    full = lambda v: pl.BlockSpec(v.shape, lambda b: (0,) * v.ndim)
+    ins = [offs, x, wl, wr]
+    specs = [
+        pl.BlockSpec(memory_space=pltpu.SMEM),
+        pl.BlockSpec((g, n, c), lambda b: (b, 0, 0)),
+        full(wl),
+        full(wr),
+    ]
+    alias = {}
+    if bufs is not None:
+        alias = {4 + i: i for i in range(5)}
+        ins += list(bufs)
+        specs += [pl.BlockSpec(memory_space=pl.ANY)] * 5
+    return pl.pallas_call(
+        functools.partial(operand_kernel, cols),
+        grid=(x.shape[0] // g,),
+        in_specs=specs,
+        out_specs=[pl.BlockSpec(b, m) for _, b, m in shapes],
+        out_shape=[jax.ShapeDtypeStruct(s, BF) for s, _, _ in shapes],
+        scratch_shapes=[
+            pltpu.VMEM((n // 128, half * g, 128), F32),
+            pltpu.VMEM((wide // 128, half * g, 128), F32),
+            pltpu.VMEM((n, c), F32),
+            pltpu.VMEM((n, c), F32),
+            pltpu.VMEM((cols * g, c), F32),
         ],
-        axis=-1,
-    ).astype(jnp.bfloat16)
-    grad_tri = weight_grad(normed_low, grad_projected)
-    grad_normed = rounded(matmul_back(grad_projected, tri_w))
-    below, grad_gain_tri = normalize_back(grad_normed, gain_tri, normed, scale)
-    return (upstream + below, grad_tri, grad_tri_out, grad_gain_tri, grad_gain_centre)
+        input_output_aliases=alias,
+        compiler_params=pltpu.CompilerParams(vmem_limit_bytes=56 << 20),
+        name="operands",
+    )(*ins)
+
+
+def product_kernel(left_ref, right_ref, mine_ref, theirs_ref, scr):
+    g = left_ref.shape[0]
+    cols = mine_ref.shape[0]
+    for e in range(g):
+        part = lax.dot_general(right_ref[e], left_ref[e], (((0,), (0,)), ((), ())), preferred_element_type=F32)
+        spread(scr, e, 2 * cols, g, part[: 2 * cols])
+    mine_ref[...] = joined(scr, slice(0, cols * g)).astype(mine_ref.dtype).reshape(mine_ref.shape)
+    theirs_ref[...] = joined(scr, slice(cols * g, None)).astype(theirs_ref.dtype).reshape(theirs_ref.shape)
+
+
+def products(left, right, cols):
+    half, n, _ = left.shape
+    wide = right.shape[2]
+    g = GROUP
+    out = jax.ShapeDtypeStruct((cols, half, n), BF)
+    return pl.pallas_call(
+        product_kernel,
+        grid=(half // g,),
+        in_specs=[pl.BlockSpec((g, n, n), lambda b: (b, 0, 0)), pl.BlockSpec((g, n, wide), lambda b: (b, 0, 0))],
+        out_specs=[pl.BlockSpec((cols, g, n), lambda b: (0, b, 0))] * 2,
+        out_shape=[out, out],
+        scratch_shapes=[pltpu.VMEM((n // 128, 2 * cols * g, 128), F32)],
+        compiler_params=pltpu.CompilerParams(vmem_limit_bytes=56 << 20),
+        name="products",
+    )(left, right)
+
+
+def after_kernel(heads, xc_ref, mine_ref, theirs_ref, w4_ref, wout_ref, wb_ref, vec_ref, after_ref, bias_ref):
+    n, c = xc_ref.shape[1:]
+    x = xc_ref[0].astype(F32)
+    n0, _ = norm(x)
+    gate = sigm(nn(n0.astype(BF), w4_ref[...]))
+    prod = jnp.concatenate([mine_ref[0].astype(F32), theirs_ref[0].astype(F32)], axis=0).T
+    nc, _ = norm(prod)
+    lin = nn((nc * vec_ref[1:2, :]).astype(BF), wout_ref[...])
+    after = x + (gate * lin).astype(BF).astype(F32)
+    after_ref[0] = after
+    n3, _ = norm(after)
+    bias = nt(wb_ref[...], (n3 * vec_ref[2:3, :]).astype(BF))
+    for h in range(heads):
+        bias_ref[0, :, h * n:(h + 1) * n] = bias[h:h + 1]
+
+
+def afters(xc, mine, theirs, w4, wout, wb, vec, heads):
+    cols, n, c = xc.shape
+    half = mine.shape[1]
+    full = lambda v: pl.BlockSpec(v.shape, lambda b: (0,) * v.ndim)
+    col = lambda a, b: pl.BlockSpec((1, a, b), lambda j: (j, 0, 0))
+    return pl.pallas_call(
+        functools.partial(after_kernel, heads),
+        grid=(cols,),
+        in_specs=[col(n, c), col(half, n), col(half, n), full(w4), full(wout), full(wb), full(vec)],
+        out_specs=[col(n, c), col(1, heads * n)],
+        out_shape=[jax.ShapeDtypeStruct((cols, n, c), F32), jax.ShapeDtypeStruct((cols, 1, heads * n), F32)],
+        compiler_params=pltpu.CompilerParams(vmem_limit_bytes=40 << 20),
+        name="afters",
+    )(xc, mine, theirs, w4, wout, wb, vec)
+
+
+def back_kernel(after_ref, gx_ref, gmid_ref, gb_ref, xc_ref, mine_ref, theirs_ref, w4_ref, wout_ref, wb_ref, vec_ref,
+                gmine_ref, gtheirs_ref, gwb_ref, gwout_ref, gw4_ref, small_ref):
+    j = pl.program_id(0)
+
+    @pl.when(j == 0)
+    def _():
+        for ref in (gwb_ref, gwout_ref, gw4_ref, small_ref):
+            ref[...] = jnp.zeros_like(ref)
+
+    n, c = xc_ref.shape[1:]
+    half = mine_ref.shape[1]
+    heads = gb_ref.shape[2]
+    g1 = vec_ref[1:2, :]
+    g2 = vec_ref[2:3, :]
+    n3, s3 = norm(after_ref[0])
+    x3 = (n3 * g2).astype(BF)
+    gb = gb_ref[0, 0].astype(F32)
+    for d in range(1, gb_ref.shape[0]):
+        gb = gb + gb_ref[d, 0].astype(F32)
+    gb = jnp.concatenate([gb, jnp.zeros((wb_ref.shape[0] - heads, n), F32)], axis=0)
+    gwb_ref[...] += nn(gb.astype(BF), x3)
+    gx = (gx_ref[0] + nn(gb.T.astype(BF), wb_ref[...])).astype(BF).astype(F32)
+    small_ref[0:1, :] += jnp.sum(gx * n3, axis=0, keepdims=True)
+    gafter = (gmid_ref[0] + norm_back(gx, g2, n3, s3)).astype(BF).astype(F32)
+
+    n0, _ = norm(xc_ref[0].astype(F32))
+    n0 = n0.astype(BF)
+    gate = sigm(nn(n0, w4_ref[...]))
+    prod = jnp.concatenate([mine_ref[0].astype(F32), theirs_ref[0].astype(F32)], axis=0).T
+    nc, sc = norm(prod)
+    centre = (nc * g1).astype(BF)
+    lin = nn(centre, wout_ref[...])
+    glin = (gafter * gate).astype(BF)
+    gp4 = (gafter * lin * gate * (1.0 - gate)).astype(BF)
+    gwout_ref[...] += nn(centre.astype(F32).T.astype(BF), glin)
+    gw4_ref[...] += nn(n0.astype(F32).T.astype(BF), gp4)
+    gc = nt(glin, wout_ref[...]).astype(BF).astype(F32)
+    small_ref[1:2, :] += jnp.sum(gc * nc, axis=0, keepdims=True)
+    gprod = norm_back(gc, g1, nc, sc).T
+    gmine_ref[0] = gprod[:half].astype(BF)
+    gtheirs_ref[0] = gprod[half:].astype(BF)
+
+
+def back_pass(after, gx, gmid, gb, xc, mine, theirs, w4, wout, wb, vec):
+    cols, n, c = xc.shape
+    half = mine.shape[1]
+    heads = gb.shape[2]
+    full = lambda shape: pl.BlockSpec(shape, lambda b: (0,) * len(shape))
+    col = lambda a, b: pl.BlockSpec((1, a, b), lambda j: (j, 0, 0))
+    accs = [wb.shape, (c, c), (c, c), (8, c)]
+    return pl.pallas_call(
+        back_kernel,
+        grid=(cols,),
+        in_specs=[col(n, c)] * 3 + [pl.BlockSpec((gb.shape[0], 1, heads, n), lambda j: (0, j, 0, 0)), col(n, c), col(half, n), col(half, n)]
+        + [full(v.shape) for v in (w4, wout, wb, vec)],
+        out_specs=[col(half, n)] * 2 + [full(s) for s in accs],
+        out_shape=[jax.ShapeDtypeStruct((cols, half, n), BF)] * 2 + [jax.ShapeDtypeStruct(s, F32) for s in accs],
+        compiler_params=pltpu.CompilerParams(vmem_limit_bytes=40 << 20),
+        name="back",
+    )(after, gx, gmid, gb, xc, mine, theirs, w4, wout, wb, vec)
+
+
+def operand_grads_kernel(left_ref, right_ref, gm_ref, gt_ref, gl_ref, gr_ref, scr, lscr, rscr):
+    g, n, _ = left_ref.shape
+    cols = gm_ref.shape[0]
+    wide = right_ref.shape[2]
+    gm = gm_ref[...].astype(F32).reshape(cols * g, n)
+    gt = gt_ref[...].astype(F32).reshape(cols * g, n)
+    for t in range(n // 128):
+        scr[t, : cols * g] = gm[:, t * 128 : (t + 1) * 128]
+        scr[t, cols * g :] = gt[:, t * 128 : (t + 1) * 128]
+    for e in range(g):
+        gp = jnp.concatenate([scr[t, pl.ds(e, 2 * cols, stride=g), :] for t in range(n // 128)], axis=1)
+        if wide > 2 * cols:
+            gp = jnp.concatenate([gp, jnp.zeros((wide - 2 * cols, n), F32)], axis=0)
+        gp = gp.astype(BF)
+        spread(rscr, e, n, g, nt(left_ref[e], gp))
+        spread(lscr, e, n, g, nn(right_ref[e], gp))
+    gl_ref[...] = joined(lscr).astype(BF).reshape(gl_ref.shape)
+    gr_ref[...] = joined(rscr).astype(BF).reshape(gr_ref.shape)
+
+
+def operand_grads(left, right, gmine, gtheirs):
+    half, n, _ = left.shape
+    wide = right.shape[2]
+    cols = gmine.shape[0]
+    g = GROUP
+    return pl.pallas_call(
+        operand_grads_kernel,
+        grid=(half // g,),
+        in_specs=[pl.BlockSpec((g, n, n), lambda b: (b, 0, 0)), pl.BlockSpec((g, n, wide), lambda b: (b, 0, 0))]
+        + [pl.BlockSpec((cols, g, n), lambda b: (0, b, 0))] * 2,
+        out_specs=[pl.BlockSpec((n, g, n), lambda b: (0, b, 0)), pl.BlockSpec((n, g, wide), lambda b: (0, b, 0))],
+        out_shape=[jax.ShapeDtypeStruct((n, half, n), BF), jax.ShapeDtypeStruct((n, half, wide), BF)],
+        scratch_shapes=[
+            pltpu.VMEM((n // 128, 2 * cols * g, 128), F32),
+            pltpu.VMEM((n // 128, n * g, 128), F32),
+            pltpu.VMEM((wide // 128, n * g, 128), F32),
+        ],
+        compiler_params=pltpu.CompilerParams(vmem_limit_bytes=60 << 20),
+        name="operand_grads",
+    )(left, right, gmine, gtheirs)
+
+
+def tri_grads_kernel(n_ref, nc_ref, gl_ref, gr_ref, wl_ref, wr_ref, al_ref, ar_ref):
+    @pl.when(pl.program_id(0) == 0)
+    def _():
+        al_ref[...] = jnp.zeros_like(al_ref)
+        ar_ref[...] = jnp.zeros_like(ar_ref)
+
+    rows = n_ref.shape[0]
+    half = gl_ref.shape[1]
+
+    def one(low, grad, w):
+        p = nt(w, low)
+        s = sigm(p[half:])
+        first = grad.astype(F32) * s
+        gp = jnp.concatenate([first, first * p[:half] * (1.0 - s)], axis=0).astype(BF)
+        return nn(gp, low)
+
+    left = al_ref[...]
+    right = ar_ref[...]
+    for k in range(rows):
+        left += one(n_ref[k], gl_ref[k], wl_ref[...])
+        right += one(nc_ref[k], gr_ref[k], wr_ref[...])
+    al_ref[...] = left
+    ar_ref[...] = right
+
+
+def tri_grads(nrm, near, gl, gr, wl, wr):
+    n, _, c = nrm.shape
+    half = gl.shape[1]
+    wide = near.shape[1]
+    rows = 8
+    full = lambda v: pl.BlockSpec(v.shape, lambda b: (0,) * v.ndim)
+    row = lambda a, b: pl.BlockSpec((rows, a, b), lambda k: (k, 0, 0))
+    out = jax.ShapeDtypeStruct((2 * half, c), F32)
+    return pl.pallas_call(
+        tri_grads_kernel,
+        grid=(n // rows,),
+        in_specs=[row(n, c), row(wide, c), row(half, n), row(half, wide), full(wl), full(wr)],
+        out_specs=[pl.BlockSpec(out.shape, lambda k: (0, 0))] * 2,
+        out_shape=[out] * 2,
+        compiler_params=pltpu.CompilerParams(vmem_limit_bytes=40 << 20),
+        name="tri_grads",
+    )(nrm, near, gl, gr, wl, wr)
 
 
 def gather_weights(tri, tri_out, attn, bias, outp, expand, shrink, vectors):
@@ -343,6 +536,52 @@
         at += w
     tri, tri_out, attn, outp, expand, shr, bias, vec = got
     return tri, tri_out, attn, bias, outp, expand, shr.reshape(-1, shrink.shape[2]), vec.T
+
+
+def gather_rows(pair_act, pieces):
+    rows = pair_act.shape[1] // pieces
+    return [
+        lax.all_gather(pair_act[0, m * rows : (m + 1) * rows], "pair", axis=0, tiled=True)
+        for m in range(pieces)
+    ]
+
+
+def swap_cores(value):
+    size = lax.axis_size("pair")
+    return lax.ppermute(value, "pair", [(d, d ^ 1) for d in range(size)])
+
+
+def exchange(value, axis, bit):
+    size = lax.axis_size(axis)
+    return lax.ppermute(value, axis, [(d, d ^ bit) for d in range(size)])
+
+
+def sum_axis(value, axis):
+    bit = 1
+    while bit < lax.axis_size(axis):
+        value = value + exchange(value, axis, bit)
+        bit *= 2
+    return value
+
+
+def sum_all(value):
+    return sum_axis(sum_axis(value, "item"), "pair")
+
+
+def sum_shards(parts):
+    size = lax.axis_size("item")
+    here = lax.axis_index("item")
+    bit = size // 2
+    while bit:
+        upper = (here // bit) % 2
+        kept, sent = [], []
+        for part in parts:
+            rows = part.shape[0] // 2
+            kept.append(lax.dynamic_slice_in_dim(part, upper * rows, rows, 0))
+            sent.append(lax.dynamic_slice_in_dim(part, (1 - upper) * rows, rows, 0))
+        parts = [k + exchange(s.astype(BF), "item", bit).astype(F32) for k, s in zip(kept, sent)]
+        bit //= 2
+    return [sum_axis(part, "pair") for part in parts]
 
 
 def on_device(
@@ -376,77 +615,117 @@
 ):
     layers = attention_proj.shape[0]
     assert layers == 1
+    cols, tokens, width = pair_act.shape[1:]
+    half = width // 2
+    heads = bias_proj.shape[2]
+    here = lax.axis_index("pair")
+    core = here % 2
+    pieces = 3 if cols % (3 * GROUP) == 0 else 1
+    gathered = gather_rows(pair_act, pieces)
     weight = gather_weights(
         tri_proj, tri_out, attention_proj, bias_proj, output_proj, expand_proj, shrink_proj, vectors
     )
     tri_w, tri_out_w, project_w, pairbias_w, output_w, expand_w, shrink_w, vector_low = weight
     vec = vector_low.astype(F32)
     weighting_rows = pair_mask.astype(F32)
-    stream = lax.all_to_all(pair_act, "pair", split_axis=2, concat_axis=1, tiled=True).astype(F32)
     both = lax.all_to_all(
         jnp.concatenate([targets, weighting_rows]), "pair", split_axis=2, concat_axis=1, tiled=True
     )
-    after, product = incoming_forward(stream, tri_w, tri_out_w, vec[0], vec[1])
-    after_c = jnp.swapaxes(after[0], 0, 1)
-    inputs_col = normalize(after_c, vec[2])[0].astype(BF)
-    cols, tokens, width = after_c.shape
-    bias_part = jnp.swapaxes(matmul(inputs_col, pairbias_w).astype(BF), 1, 2)
-    bias_full = lax.all_gather(bias_part.reshape(cols, -1), "pair", axis=0, tiled=True)
+
+    scaled = (tri_w.astype(F32) * vec[0][:, None]).astype(BF).T
+    halves = [
+        lax.dynamic_slice_in_dim(scaled, width * s + half * core, half, 0) for s in range(4)
+    ]
+    w_left = jnp.concatenate(halves[:2])
+    w_right = jnp.concatenate(halves[2:])
+    w_gate = scaled[4 * width :].T
+    wout = jnp.roll(tri_out_w, -half * core, axis=0)
+    gain_c = jnp.roll(vec[1], -half * core)
+    vec8 = jnp.concatenate([vec[:1], gain_c[None], vec[2:], jnp.zeros((3, width), F32)])
+    wb = jnp.concatenate([pairbias_w.T, jnp.zeros((16 - heads, width), BF)])
+
+    offs = jnp.stack([here * cols, (here + 1 - 2 * core) * cols]).astype(jnp.int32)
+    span = cols // pieces // GROUP
+    bufs = None
+    for m in range(pieces):
+        if pieces == 1:
+            place = lambda b: b
+        else:
+            place = lambda b, m=m: (b // span) * (span * pieces) + m * span + b % span
+        bufs = operands(offs, gathered[m], w_left, w_right, cols, place, bufs)
+    left, right, nrm, near, xc = bufs
+    mine, send = products(left, right, cols)
+    theirs = swap_cores(send)
+    after_c, bias_part = afters(xc, mine, theirs, w_gate, wout, wb, vec8, heads)
+    bias_full = lax.all_gather(bias_part[:, 0].astype(BF), "pair", axis=0, tiled=True)
     hidden = expand_w.shape[1] // 2
     expand_mix = (
         expand_w.reshape(width, 2, hidden // 128, 128).swapaxes(1, 2).reshape(width, 2 * hidden)
     )
     z = jnp.sum(shrink_w.astype(F32) * vec[4], axis=1)[None]
-    vec8 = jnp.concatenate([vec, jnp.zeros((3, width), F32)])
-    gx, upstream, gb, gkv_w, gqg_w, gow, gew, svec, small = column_pass(
+    gx, gmid, gb, gkv_w, gqg_w, gow, gew, svec, small = column_pass(
         after_c, both[0], both[1], bias_full, project_w, project_w.T, output_w, expand_mix, vec8, z
     )
-    bias_cols = lax.psum_scatter(gb.astype(F32), "pair", scatter_dimension=0, tiled=True)
-    bias_low = jnp.swapaxes(bias_cols.reshape(cols, -1, tokens), 1, 2).astype(BF)
-    grad_pairbias = weight_grad(inputs_col, bias_low)
-    grad_inputs = rounded(gx + matmul_back(bias_low, pairbias_w))
-    _, normed, scale = normalize(after_c, vec[2])
-    below, grad_gain_attend = normalize_back(grad_inputs[None], vec[2], normed[None], scale[None])
-    upstream = jnp.swapaxes(upstream + below[0], 0, 1)[None]
-    upstream, grad_tri, grad_tri_out, grad_gain_tri, grad_gain_centre = incoming_back(
-        upstream, stream, product, tri_w, tri_out_w, vec[0], vec[1]
-    )
-    summed = lax.psum(
-        (
-            grad_tri,
-            grad_tri_out,
-            gkv_w,
-            gqg_w,
-            grad_pairbias,
-            gow,
-            gew,
-            svec,
-            small,
-            jnp.stack([grad_gain_tri, grad_gain_centre, grad_gain_attend]),
-            jnp.sum(weighting_rows),
-        ),
-        ("item", "pair"),
-    )
-    g_tri, g_tri_out, g_kv, g_qg, g_bias, g_out, g_exp, s_sum, sm, gains, count = summed
-    g_project = jnp.concatenate([g_qg[:width].T, g_kv, g_qg[width:].T], axis=1)
-    g_expand = (
-        g_exp.reshape(width, hidden // 128, 2, 128).swapaxes(1, 2).reshape(width, 2 * hidden)
-    )
-    g_shrink = s_sum[0][:, None] * vec[4][None, :]
-    g_read = sm[0] + jnp.sum(s_sum[0][:, None] * shrink_w.astype(F32), axis=0)
-    g_vec = jnp.concatenate([gains, sm[1:2], g_read[None]])
-    grads = [
-        g / count for g in (g_tri, g_tri_out, g_project, g_bias, g_out, g_expand, g_shrink, g_vec)
+    bias_cols = lax.all_to_all(gb, "pair", split_axis=0, concat_axis=0, tiled=True)
+    early = sum_shards(
+        [
+            jnp.concatenate(
+                [gqg_w[:width].T, gkv_w, gqg_w[width:].T, gow, gew, svec.reshape(width, -1)], axis=1
+            )
+        ]
+    )
+    scalars = sum_all(jnp.stack([jnp.sum(small[2]), jnp.sum(weighting_rows)]))
+    gmine, gsend, gwb, gwout, gw4, small2 = back_pass(
+        after_c, gx, gmid, bias_cols.reshape(-1, cols, heads, tokens), xc, mine, theirs,
+        w_gate, wout, wb, vec8,
+    )
+    gtheirs = swap_cores(gsend)
+    gl, gr = operand_grads(left, right, gmine, gtheirs)
+    al, ar = tri_grads(nrm, near, gl, gr, w_left, w_right)
+
+    def halfway(part):
+        zero = jnp.zeros_like(part)
+        return [jnp.where(core == 0, part, zero), jnp.where(core == 1, part, zero)]
+
+    a_tri = jnp.concatenate(
+        halfway(al[:half]) + halfway(al[half:]) + halfway(ar[:half]) + halfway(ar[half:]) + [gw4.T]
+    ).T
+    g_read = small[0] + jnp.sum(svec[0][:, None] * shrink_w.astype(F32), axis=0)
+    g_vec = jnp.stack(
+        [
+            jnp.sum(a_tri * tri_w.astype(F32), axis=1),
+            jnp.roll(small2[1], half * core),
+            small2[0],
+            small[1],
+            g_read,
+        ]
+    )
+    late = sum_shards(
+        [
+            jnp.concatenate(
+                [a_tri * vec[0][:, None], jnp.roll(gwout, half * core, axis=0), gwb[:heads].T, g_vec.T],
+                axis=1,
+            )
+        ]
+    )
+    loss_sum, count = scalars[0], scalars[1]
+    at = [width * s for s in range(11)]
+    tall = early[0]
+    shards = [
+        late[0][:, : at[5]],
+        late[0][:, at[5] : at[6]],
+        tall[:, : at[4]],
+        late[0][:, at[6] : at[6] + heads],
+        tall[:, at[4] : at[5]],
+        tall[:, at[5] : at[5] + 2 * hidden].reshape(-1, hidden // 128, 2, 128).swapaxes(1, 2).reshape(-1, 2 * hidden),
+        tall[:, at[5] + 2 * hidden :].reshape(-1, 1) * vec[4][None, :],
+        late[0][:, at[6] + heads :].T,
     ]
-    loss_sum = jnp.sum(sm[2])
-    grad_norm = jnp.sqrt(sum(jnp.sum(g * g) for g in grads))
+    shards = [s / count for s in shards]
+    squares = sum_axis(sum(jnp.sum(s * s) for s in shards), "item")
+    grad_norm = jnp.sqrt(squares)
     factor = jnp.minimum(1.0, clip_limit / (grad_norm + 1e-06))
-    place = lax.axis_index("item")
-    shards = []
-    for master, grad in zip((tri_proj, tri_out, attention_proj, bias_proj, output_proj, expand_proj, shrink_proj), grads):
-        rows = master.shape[1]
-        shards.append(lax.dynamic_slice_in_dim(grad, place * rows, rows, 0)[None])
-    shards.append(lax.dynamic_slice_in_dim(grads[7], place * vectors.shape[1], vectors.shape[1], 1))
+    shards = [s[None] for s in shards[:7]] + shards[7:]
     masters = (
         tri_proj,
         tri_out,

time: 1490 us -> 1160 us (0.78)
  Pallas kernels: 346 us -> 845 us
  waiting for transfers between devices: 545 us -> 131 us
  matrix products: 171 us -> 0 us
  other arithmetic: 153 us -> 38 us
  local copies, waits for them, and re-layouts: 176 us -> 69.2 us
  blocking collectives: 60.4 us -> 21.3 us
    pallas_call x0 -> x8, Pallas kernels: none -> 499 us  [the longest x3 183 us: operands(): pl.pallas_call(functools.partial(operand_kernel, cols), grid=(x.shape[0]...]
    all_gather x3 -> x4, waiting for transfers between devices: 344 us -> 77.6 us  [the longest x3 75.5 us: gather_rows(): lax.all_gather(pair_act[0, m * rows:(m + 1) * rows], 'pair', axis=0, tile...]
    dot_general x12 -> x0, matrix products: 171 us -> none  [the longest x3 41.6 us: matmul(): jnp.einsum('...c,cd->...d', value, weight, preferred_element_type=jnp.flo...]
    psum x1 -> x0, waiting for transfers between devices: 130 us -> none  [on_device(): lax.psum((grad_tri, grad_tri_out, gkv_w, gqg_w, grad_pairbias, gow, gew,...]
    all_gather x2 -> x0, local copies, waits for them, and re-layouts: 105 us -> none  [the longest x1 52.5 us: incoming_back(): right_piece = lax.all_gather(right, 'pair', axis=2, tiled=True)]
    ppermute x0 -> x19, waiting for transfers between devices: none -> 51.5 us  [the longest x17 49.1 us: exchange(): return lax.ppermute(value, axis, [(d, d ^ bit) for d in range(size)])]
    unnamed x11 -> x8, other arithmetic: 40.8 us -> 0.05 us
    psum x1 -> x0, blocking collectives: 39.6 us -> none  [on_device(): lax.psum((grad_tri, grad_tri_out, gkv_w, gqg_w, grad_pairbias, gow, gew,...]
  transfers between devices with their start and end apart: 8 -> 25, of which waited for: 7 -> 17; matrix products, arithmetic and copies ran while one was open for 12% -> 5% of each run, Pallas kernels for 0% -> 33%
where the time goes in v2:
time: 1160 us; the launch traced here: 1150 us
  Pallas kernels  845 us (73%)
  waiting for transfers between devices  131 us (11%)
  local copies, waits for them, and re-layouts  69.2 us (6%)
  other arithmetic  38 us (3%)
  starting transfers between devices  27.8 us (2%)
  between operations  22.5 us (2%)
  blocking collectives  21.3 us (2%)
    pallas_call x1, Pallas kernels, column_pass(): pl.pallas_call(functools.partial(column_kernel, heads), grid=(cols,), in_...  346 us
    pallas_call x3, Pallas kernels, operands(): pl.pallas_call(functools.partial(operand_kernel, cols), grid=(x.shape[0]...  183 us
    pallas_call x1, Pallas kernels, tri_grads(): pl.pallas_call(tri_grads_kernel, grid=(n // rows,), in_specs=[row(n, c),...  147 us
    pallas_call x1, Pallas kernels, back_pass(): pl.pallas_call(back_kernel, grid=(cols,), in_specs=[col(n, c)] * 3 + [pl....  76.4 us
    all_gather x3, waiting for transfers between devices, gather_rows(): lax.all_gather(pair_act[0, m * rows:(m + 1) * rows], 'pair', axis=0, tile...  75.5 us
    ppermute x17, waiting for transfers between devices, exchange(): return lax.ppermute(value, axis, [(d, d ^ bit) for d in range(size)])  49.1 us
    unnamed x179, local copies, waits for them, and re-layouts  41.5 us
    pallas_call x1, Pallas kernels, afters(): pl.pallas_call(functools.partial(after_kernel, heads), grid=(cols,), in_s...  40.6 us
  transfers between devices with their start and end apart: 25, of which 17 were waited for; matrix products, arithmetic and copies ran while one was open for 5% of the time, Pallas kernels for 33%

profile of v2, /device:TPU:0, one launch (start us, length us, event | category | flops | bytes accessed | tf_op | source)
XLA Modules:
  0.0 1153.9 jit_solution(7523315792105286282)
XLA Ops:
  7.2 4.7 fusion.27
  14.1 21.3 %all_gather.16 = bf16[128,2953]{1,0:T(8,128)(2,1)S(1)} all-gather(bf16[32,2953]{1,0:T(8,128)(2,1)S(1)} %concatenate.38), channel_id=1, replica_groups=mesh['item'=4,'pair'=8] {'item'}, dimensions={0}, use_global_device_ids=true | all-gather | bytes 944960 | tf_op jit(solution)/shard_map/all_gather | solution.py:532
  38.2 48.8 %all-gather.13.cloned.1.call-done = bf16[1,128,384,128]{3,2,0,1:T(8,128)(2,1)} async-done(((bf16[1,16,384,128]{3,2,0,1:T(8,128)(2,1)}), bf16[1,128,384,128]{3,2,0,1:T(8,128)(2,1)}) %all-gather.13.cloned.1.call-update) | async-done | bytes 12582928 | tf_op jit(solution)/shard_map/all_gather | solution.py:544
  87.0 60.8 %operands.3 = (bf16[64,384,384]{2,1,0:T(8,128)(2,1)}, bf16[64,384,128]{2,1,0:T(8,128)(2,1)}, bf16[384,384,128]{2,1,0:T(8,128)(2,1)}, bf16[384,128,128]{2,1,0:T(8,128)(2,1)}, bf16[48,384,128]{2,1,0:T(8,128)(2,1)}) custom-call(s32[2]{0:T(128)} %pad_add_fusion.off_ref, bf16[128,384,128]{2,1,0:T(8,128)(2,1)} %bitcast.130, ...), custom_call_target="tpu_custom_call" | custom-call | tf_op jit(solution)/shard_map/operands/pallas_call | solution.py:302
  147.9 13.4 %all-gather.11.cloned.1.call-done = bf16[1,128,384,128]{3,2,0,1:T(8,128)(2,1)} async-done(((bf16[1,16,384,128]{3,2,0,1:T(8,128)(2,1)}), bf16[1,128,384,128]{3,2,0,1:T(8,128)(2,1)}) %all-gather.11.cloned.1.call-update) | async-done | bytes 12582928 | tf_op jit(solution)/shard_map/all_gather | solution.py:544
  161.2 60.9 %operands.4 = (bf16[64,384,384]{2,1,0:T(8,128)(2,1)}, bf16[64,384,128]{2,1,0:T(8,128)(2,1)}, bf16[384,384,128]{2,1,0:T(8,128)(2,1)}, bf16[384,128,128]{2,1,0:T(8,128)(2,1)}, bf16[48,384,128]{2,1,0:T(8,128)(2,1)}) custom-call(s32[2]{0:T(128)} %pad_add_fusion.off_ref, ...), custom_call_target="tpu_custom_call", output_to_operand_aliasing={{0}: (4, {}), {1}: (5, {}), {2}: (6, {}), {3}: (7, {}), {4}... | custom-call | tf_op jit(solution)/shard_map/operands/pallas_call | solution.py:302
  222.1 13.3 %all-gather.9.cloned.1.call-done = bf16[1,128,384,128]{3,2,0,1:T(8,128)(2,1)} async-done(((bf16[1,16,384,128]{3,2,0,1:T(8,128)(2,1)}), bf16[1,128,384,128]{3,2,0,1:T(8,128)(2,1)}) %all-gather.9.cloned.1.call-update) | async-done | bytes 12582928 | tf_op jit(solution)/shard_map/all_gather | solution.py:544
  235.4 60.9 %operands.5 = (bf16[64,384,384]{2,1,0:T(8,128)(2,1)}, bf16[64,384,128]{2,1,0:T(8,128)(2,1)}, bf16[384,384,128]{2,1,0:T(8,128)(2,1)}, bf16[384,128,128]{2,1,0:T(8,128)(2,1)}, bf16[48,384,128]{2,1,0:T(8,128)(2,1)}) custom-call(s32[2]{0:T(128)} %pad_add_fusion.off_ref, ...), custom_call_target="tpu_custom_call", output_to_operand_aliasing={{0}: (4, {}), {1}: (5, {}), {2}: (6, {}), {3}: (7, {}), {4}... | custom-call | tf_op jit(solution)/shard_map/operands/pallas_call | solution.py:302
  296.4 13.7 %products.1 = (bf16[48,64,384]{2,1,0:T(8,128)(2,1)}, bf16[48,64,384]{2,1,0:T(8,128)(2,1)}) custom-call(bf16[64,384,384]{2,1,0:T(8,128)(2,1)} %get-tuple-element.77.left_ref, bf16[64,384,128]{2,1,0:T(8,128)(2,1)} %get-tuple-element.78.right_ref), custom_call_target="tpu_custom_call" | custom-call | tf_op jit(solution)/shard_map/products/pallas_call | solution.py:336
  314.8 3.2 copy-done
  319.6 40.6 %afters.1 = (f32[48,384,128]{2,1,0:T(8,128)}, f32[48,1,1536]{2,1,0:T(1,128)S(1)}) custom-call(bf16[48,384,128]{2,1,0:T(8,128)(2,1)S(1)} %copy-done, bf16[48,64,384]{2,1,0:T(8,128)(2,1)S(1)} %copy-done.1, bf16[48,64,384]{2,1,0:T(8,128)(2,1)S(1)} %collective-permute-done.theirs_ref, bf16[128,128]{1,0:T(8,128)(2,1)S(1)} %copy.353.w4_ref, ...), custom_call_target="tpu_custom_call" | custom-call | tf_op jit(solution)/shard_map/afters/pallas_call | solution.py:369
  363.5 3.6 all-to-all-start
  385.6 345.7 %columns.1 = (f32[48,384,128]{2,1,0:T(8,128)}, f32[48,384,128]{2,1,0:T(8,128)}, bf16[384,1536]{1,0:T(8,128)(2,1)}, f32[128,256]{1,0:T(8,128)}, f32[256,128]{1,0:...) custom-call(f32[48,384,128]{2,1,0:T(8,128)} %get-tuple-element.81.after_ref, ...), custom_call_target="tpu_custom_call" | custom-call | tf_op jit(solution)/shard_map/columns/pallas_call | solution.py:203
  731.3 4.6 all-to-all-start.1
  760.5 76.4 %back.1 = (bf16[48,64,384]{2,1,0:T(8,128)(2,1)S(1)}, bf16[48,64,384]{2,1,0:T(8,128)(2,1)}, f32[16,128]{1,0:T(8,128)S(1)}, f32[128,128]{1,0:T(8,128)S(1)}, f32[128,128]{1,0:T(8,128)S(1)}, /*index=5*/f32[8,128]{1,0:T(8,128)S(1)}) custom-call(f32[48,384,128]{2,1,0:T(8,128)} %get-tuple-element.81.after_ref, f32[48,384,128]{2,1,0:T(8,128)} %get-tuple-element.86.gx_ref, ...), custom_call_target="tpu_custom_call" | custom-call | tf_op jit(solution)/shard_map/back/pallas_call | solution.py:430
  845.3 8.9 collective-permute-done.13
  873.9 38.4 %operand_grads.1 = (bf16[384,64,384]{2,1,0:T(8,128)(2,1)}, bf16[384,64,128]{2,1,0:T(8,128)(2,1)}) custom-call(bf16[64,384,384]{2,1,0:T(8,128)(2,1)} %get-tuple-element.77.left_ref, bf16[64,384,128]{2,1,0:T(8,128)(2,1)} %get-tuple-element.78.right_ref, bf16[48,64,384]{2,1,0:T(8,128)(2,1)} %copy-done.6, bf16[48,64,384]{2,1,0:T(8,128)(2,1)} %collective-permute-done.6.gt_ref), custom_call_target="tpu_custom_call" | custom-call | tf_op jit(solution)/shard_map/operand_grads/pallas_call | solution.py:467
  912.3 2.8 copy-done.5
  915.1 147.1 %tri_grads.1 = (f32[128,128]{1,0:T(8,128)S(1)}, f32[128,128]{1,0:T(8,128)S(1)}) custom-call(bf16[384,384,128]{2,1,0:T(8,128)(2,1)} %get-tuple-element.84.n_ref, bf16[384,128,128]{2,1,0:T(8,128)(2,1)} %get-tuple-element.85.nc_ref, bf16[384,64,384]{2,1,0:T(8,128)(2,1)} %get-tuple-element.91.gl_ref, bf16[384,64,128]{2,1,0:T(8,128)(2,1)S(1)} %copy-done.5, ...), custom_call_target="tpu_custom_call" | custom-call | tf_op jit(solution)/shard_map/tri_grads/pallas_call | solution.py:517
  1064.7 7.7 collective-permute-done.7
  1074.5 4.1 collective-permute-done.8
  1083.5 8.6 collective-permute-done.10
  1093.9 8.8 collective-permute-done.11
  1117.3 2.5 collective-permute-start.18
  (348 shorter events, 130.5 us)
Async XLA Ops:
  7.2 79.8 %all-gather.13.cloned.1.call-start = ((), (), s32[]{:S(2)}) async-start(), calls=%async_computation.4 | async-start | bytes 14155776 | tf_op jit(solution)/shard_map/all_gather | solution.py:544
  12.1 149.2 %all-gather.11.cloned.1.call-start = ((), (), s32[]{:S(2)}) async-start(), calls=%async_computation.3 | async-start | bytes 14155776 | tf_op jit(solution)/shard_map/all_gather | solution.py:544
  12.8 222.6 %all-gather.9.cloned.1.call-start = ((), (), s32[]{:S(2)}) async-start(), calls=%async_computation.2 | async-start | bytes 14155776 | tf_op jit(solution)/shard_map/all_gather | solution.py:544
  13.5 372.1 %all-gather.15.cloned.1.call-start = ((), (), s32[]{:S(2)}) async-start(), calls=%async_computation.5 | async-start | bytes 1327104 | tf_op jit(solution)/shard_map/all_gather | solution.py:660
  310.0 4.7 collective-permute-start
  363.5 16.8 %all-to-all-start = ((f32[8,1,4608]{2,1,0:T(1,128)}), f32[8,1,4608]{2,1,0:T(1,128)S(1)}, u32[]{:S(2)}, u32[]{:S(2)}) async-start(f32[8,1,4608]{2,1,0:T(1,128)} %reshape.296), calls=%async_computation | async-start | bytes 294912 | tf_op jit(solution)/shard_map/all_to_all | solution.py:631
  731.3 23.5 %all-to-all-start.1 = ((bf16[8,48,1536]{2,1,0:T(8,128)(2,1)}), bf16[8,48,1536]{2,1,0:T(8,128)(2,1)}, u32[]{:S(2)}, u32[]{:S(2)}) async-start(bf16[8,48,1536]{2,1,0:T(8,128)(2,1)} %bitcast.139), calls=%async_computation.1 | async-start | bytes 2359296 | tf_op jit(solution)/shard_map/all_to_all | solution.py:669
  750.3 90.1 %collective-permute-start.12 = (bf16[64,1668]{0,1:T(8,128)(2,1)}, bf16[64,1668]{0,1:T(8,128)(2,1)}, u32[]{:S(2)}, u32[]{:S(2)}) collective-permute-start(bf16[64,1668]{0,1:T(8,128)(2,1)} %dynamic-slice_convert_fusion.1), channel_id=1, source_target_pairs={{0,16},{8,24},{16,0},{24,8},{1,17},{9,25},{17,1},{25,9},{2,18},{10... | collective-permute-start | bytes 640520 | tf_op jit(solution)/shard_map/ppermute | solution.py:556
  840.4 33.6 %collective-permute-start.6 = (bf16[48,64,384]{2,1,0:T(8,128)(2,1)}, bf16[48,64,384]{2,1,0:T(8,128)(2,1)}, u32[]{:S(2)}, u32[]{:S(2)}) collective-permute-start(bf16[48,64,384]{2,1,0:T(8,128)(2,1)} %get-tuple-element.90), channel_id=1, source_target_pairs={{0,1},{1,0},{2,3},{3,2},{4,5},{5,4},{6,7},{7,6},{8,9},{9,8},{10,11... | collective-permute-start | bytes 7077896 | tf_op jit(solution)/shard_map/ppermute | solution.py:551
  841.9 12.3 %collective-permute-start.13 = (bf16[32,1668]{0,1:T(8,128)(2,1)S(1)}, bf16[32,1668]{0,1:T(8,128)(2,1)S(1)}, u32[]{:S(2)}, u32[]{:S(2)}) collective-permute-start(bf16[32,1668]{0,1:T(8,128)(2,1)S(1)} %dynamic-slice_convert_fusion), channel_id=1, source_target_pairs={{0,8},{8,0},{16,24},{24,16},{1,9},{9,1},{17,25},{25,17},{2,10},{10... | collective-permute-start | bytes 320264 | tf_op jit(solution)/shard_map/ppermute | solution.py:556
  844.8 10.1 collective-permute-start.1
  854.8 2.0 collective-permute-start.14
  856.2 4.5 collective-permute-start.2
  857.4 12.9 %collective-permute-start.15 = (f32[32,1668]{1,0:T(8,128)S(1)}, f32[32,1668]{1,0:T(8,128)S(1)}, u32[]{:S(2)}, u32[]{:S(2)}) collective-permute-start(f32[32,1668]{1,0:T(8,128)S(1)} %copy.370), channel_id=1, source_target_pairs={{0,2},{1,3},{2,0},{3,1},{4,6},{5,7},{6,4},{7,5},{8,10},{9,11},{10,... | collective-permute-start | bytes 640520 | tf_op jit(solution)/shard_map/ppermute | solution.py:556
  863.2 3.5 collective-permute-start.4
  866.7 3.5 collective-permute-start.5
  871.0 193.3 %collective-permute-start.16 = (f32[32,1668]{1,0:T(8,128)S(1)}, f32[32,1668]{1,0:T(8,128)S(1)}, u32[]{:S(2)}, u32[]{:S(2)}) collective-permute-start(f32[32,1668]{1,0:T(8,128)S(1)} %copy.372), channel_id=1, source_target_pairs={{0,4},{1,5},{2,6},{3,7},{4,0},{5,1},{6,2},{7,3},{8,12},{9,13},{10,... | collective-permute-start | bytes 640520 | tf_op jit(solution)/shard_map/ppermute | solution.py:556
  1062.7 9.8 collective-permute-start.7
  1072.8 5.8 collective-permute-start.8
  1078.8 1.8 collective-permute-start.9
  1080.7 11.4 collective-permute-start.10
  1092.2 10.6 collective-permute-start.11
  1113.1 3.7 collective-permute-start.17
  1117.3 4.6 collective-permute-start.18
  (73 other events, 2819.0 us)
Sparse Core Ops, SparseCore 0:
  12.2 74.8 all-gather.12
  88.9 72.2 all-gather.10
  163.1 72.2 all-gather.8
  361.2 24.3 all-gather.14

commit v3 on v2

--- a/solution.py
+++ b/solution.py
@@ -24,6 +24,10 @@
 EPS = norm_epsilon
 
 
+def cost(flops, moved, exps=0):
+    return pl.CostEstimate(flops=int(flops), bytes_accessed=int(moved), transcendentals=int(exps))
+
+
 def nn(a, b):
     return lax.dot_general(a, b, (((1,), (0,)), ((), ())), preferred_element_type=F32)
 
@@ -49,22 +53,27 @@
 def column_kernel(heads, after_ref, tgt_ref, msk_ref, bias_ref, w_ref, wt_ref, wo_ref, we_ref, vec_ref, z_ref,
                 gx_ref, gmid_ref, gb_ref, gkvw_ref, gqgw_ref, gow_ref, gew_ref, svec_ref, small_ref,
                 bias2, e_s, gs_s, acc, qbd, gobd, vaug, qn, gon, ores, cu, hv):
-    j = pl.program_id(0)
+    step = pl.program_id(0)
     last = pl.num_programs(0) - 1
-    n, c = after_ref.shape[1], after_ref.shape[2]
+    cb, n, c = after_ref.shape
     dh = c // heads
     wide = heads * n
     scale = dh ** -0.5
-
-    @pl.when(j == 0)
+    every = range(cb)
+    pairs = [(b, h) for b in every for h in range(heads)]
+    lanes = lambda b, h: slice(b * wide + h * n, b * wide + (h + 1) * n)
+    rows = lambda b: slice(b * n, (b + 1) * n)
+    chans = lambda h: slice(h * dh, (h + 1) * dh)
+
+    @pl.when(step == 0)
     def _():
         for h in range(heads):
             bias2[:, h * n:(h + 1) * n] = bias_ref[:, h * n:(h + 1) * n].astype(F32).T * LOG2E
         acc[...] = jnp.zeros_like(acc)
         qbd[...] = jnp.zeros_like(qbd)
         gobd[...] = jnp.zeros_like(gobd)
-        lane = lax.broadcasted_iota(jnp.int32, (n, c), 1)
-        vaug[:, c:] = jnp.where(lane < 3, 1.0, 0.0).astype(BF)
+        first = lax.broadcasted_iota(jnp.int32, (cb * n, c), 1)
+        vaug[:, c:] = jnp.where(first < 3, 1.0, 0.0).astype(BF)
         for ref in (gkvw_ref, gqgw_ref, gow_ref, gew_ref, svec_ref, small_ref):
             ref[...] = jnp.zeros_like(ref)
 
@@ -72,36 +81,33 @@
     g3 = vec_ref[2:3, :]
     g4 = vec_ref[3:4, :]
     wr = vec_ref[4:5, :]
-    after = after_ref[0]
+    after = after_ref[...].reshape(cb * n, c)
     n3, _ = norm(after)
     x = (n3 * g3).astype(BF)
     nat = nn(x, w_ref[:, :3 * c])
     k_nat = nat[:, c:2 * c].astype(BF)
     vaug[:, :c] = nat[:, 2 * c:].astype(BF)
     q_nat = (nat[:, :c] * (scale * LOG2E)).astype(BF)
-    for h in range(heads):
-        qn[h * n:(h + 1) * n, :] = jnp.where((lane >= h * dh) & (lane < (h + 1) * dh), q_nat, jnp.zeros_like(q_nat))
     tr = nt(wt_ref[...], x)
     q_t = (tr[:c] * (scale * LOG2E)).astype(BF)
     k_t = tr[c:2 * c].astype(BF)
-    v_t = jnp.concatenate([tr[2 * c:3 * c], jnp.ones((16, n), F32)], axis=0).astype(BF)
+    v_t = jnp.concatenate([tr[2 * c:3 * c], jnp.ones((16, cb * n), F32)], axis=0).astype(BF)
     gate_t = sigm(tr[3 * c:])
-    for h in range(heads):
-        qbd[h * dh:(h + 1) * dh, h * n:(h + 1) * n] = q_t[h * dh:(h + 1) * dh]
-
-    for s0, w0 in chunks(wide, 256):
-        sl = slice(s0, s0 + w0)
-        sc = nn(k_nat, qbd[:, sl]) + bias2[:, sl]
-        top = jnp.max(sc, axis=0, keepdims=True)
-        ex = jnp.exp2(sc - top).astype(BF)
-        e_s[:, sl] = ex
-        ores[:, sl] = nn(v_t, ex)
-    o_parts, r_parts = [], []
-    for h in range(heads):
-        r = 1.0 / ores[c:c + 1, h * n:(h + 1) * n]
-        r_parts.append(r)
-        o_parts.append(ores[h * dh:(h + 1) * dh, h * n:(h + 1) * n] * r)
-    o_t = jnp.concatenate(o_parts, axis=0)
+    for b, h in pairs:
+        qbd[chans(h), lanes(b, h)] = q_t[chans(h), rows(b)]
+        qn[lanes(b, h), :] = jnp.where((lane >= h * dh) & (lane < (h + 1) * dh), q_nat[rows(b)], jnp.zeros((n, c), BF))
+
+    for s0, w0 in chunks(wide, wide):
+        for b in every:
+            sl = slice(b * wide + s0, b * wide + s0 + w0)
+            sc = nn(k_nat[rows(b)], qbd[:, sl]) + bias2[:, s0:s0 + w0]
+            top = jnp.max(sc, axis=0, keepdims=True)
+            ex = jnp.exp2(sc - top).astype(BF)
+            e_s[:, sl] = ex
+            ores[:, sl] = nn(v_t[:, rows(b)], ex)
+    r_of = {p: 1.0 / ores[c:c + 1, lanes(*p)] for p in pairs}
+    o_of = {p: ores[chans(p[1]), lanes(*p)] * r_of[p] for p in pairs}
+    o_t = jnp.concatenate([jnp.concatenate([o_of[b, h] for h in range(heads)], axis=0) for b in every], axis=1)
     y_t = (gate_t * o_t).astype(BF)
     out = nn(y_t.astype(F32).T.astype(BF), wo_ref[...]).astype(BF)
     mid = after + out.astype(F32)
@@ -122,20 +128,21 @@
         cu[:, q * 256:q * 256 + 128] = (zc * b * (sig + silu - silu * sig)).astype(BF)
         cu[:, q * 256 + 128:(q + 1) * 256] = (zc * silu).astype(BF)
     readout = jnp.sum(racc, axis=-1, keepdims=True)
-    pick = lax.broadcasted_iota(jnp.int32, tgt_ref.shape, 1) == j
-    tgt = jnp.sum(jnp.where(pick, tgt_ref[...], 0.0), axis=1, keepdims=True)
-    msk = jnp.sum(jnp.where(pick, msk_ref[...], 0.0), axis=1, keepdims=True)
-    err = readout - tgt
-    wer = msk * err
+    spot = lax.broadcasted_iota(jnp.int32, tgt_ref.shape, 1)
+    pick = lambda ref: jnp.concatenate(
+        [jnp.sum(jnp.where(spot == step * cb + b, ref[...], 0.0), axis=1, keepdims=True) for b in every], axis=0)
+    err = readout - pick(tgt_ref)
+    wer = pick(msk_ref) * err
     gr = 2.0 * wer
     small_ref[0:1, :] += jnp.sum(gr * mid, axis=0, keepdims=True)
-    small_ref[2:3, :] += jnp.sum(jnp.where(lane == 0, wer * err, 0.0), axis=0, keepdims=True)
+    first = lax.broadcasted_iota(jnp.int32, (cb * n, c), 1)
+    small_ref[2:3, :] += jnp.sum(jnp.where(first == 0, wer * err, 0.0), axis=0, keepdims=True)
     svec_ref[...] += jnp.sum(gr * hv[...].astype(F32), axis=0, keepdims=True)
     gew_ref[...] += nn((gr * t.astype(F32)).T.astype(BF), cu[...])
     gt = gr * nt(cu[...], we_ref[...])
     small_ref[1:2, :] += jnp.sum(gt * n4, axis=0, keepdims=True)
     gmid = gr * wr + norm_back(gt, g4, n4, sc4)
-    gmid_ref[0] = gmid
+    gmid_ref[...] = gmid.reshape(gmid_ref.shape)
 
     gout = gmid.astype(BF)
     gow_ref[...] += nn(y_t, gout)
@@ -143,40 +150,43 @@
     ggl_t = gy_t * o_t * gate_t * (1.0 - gate_t)
     go_t = (gy_t * gate_t).astype(BF).astype(F32)
     row = lax.broadcasted_iota(jnp.int32, (16, n), 0)
-    gos = []
-    for h in range(heads):
-        part = (go_t[h * dh:(h + 1) * dh] * r_parts[h]).astype(BF)
-        gobd[h * dh:(h + 1) * dh, h * n:(h + 1) * n] = part
+    gos = {}
+    for b, h in pairs:
+        part = (go_t[chans(h), rows(b)] * r_of[b, h]).astype(BF)
+        gobd[chans(h), lanes(b, h)] = part
         part = part.astype(F32)
-        gos.append(part)
-        d = -jnp.sum(part * o_parts[h], axis=0, keepdims=True)
+        gos[b, h] = part
+        d = -jnp.sum(part * o_of[b, h], axis=0, keepdims=True)
         hi = d.astype(BF).astype(F32)
         mi = (d - hi).astype(BF).astype(F32)
         lo = d - hi - mi
-        gobd[c:, h * n:(h + 1) * n] = jnp.where(row == 0, hi, jnp.where(row == 1, mi, jnp.where(row == 2, lo, 0.0))).astype(BF)
-    go_n = jnp.concatenate(gos, axis=0).T.astype(BF)
-    for h in range(heads):
-        gon[h * n:(h + 1) * n, :] = jnp.where((lane >= h * dh) & (lane < (h + 1) * dh), go_n, jnp.zeros_like(go_n))
-
-    vk = vaug[:, :c + 16]
-    for s0, w0 in chunks(wide, 256):
-        sl = slice(s0, s0 + w0)
-        g = e_s[:, sl].astype(F32) * nn(vk, gobd[:, sl])
-        acc[:, sl] += g
-        gl = g.astype(BF)
-        gs_s[:, sl] = gl
-        ores[:c, sl] = nn(k_t, gl)
-    gq_t = jnp.concatenate([ores[h * dh:(h + 1) * dh, h * n:(h + 1) * n] for h in range(heads)], axis=0) * scale
+        gobd[c:, lanes(b, h)] = jnp.where(row == 0, hi, jnp.where(row == 1, mi, jnp.where(row == 2, lo, 0.0))).astype(BF)
+    go_n = jnp.concatenate([jnp.concatenate([gos[b, h] for h in range(heads)], axis=0) for b in every], axis=1).T.astype(BF)
+    for b, h in pairs:
+        gon[lanes(b, h), :] = jnp.where((lane >= h * dh) & (lane < (h + 1) * dh), go_n[rows(b)], jnp.zeros((n, c), BF))
+
+    for s0, w0 in chunks(wide, wide):
+        total = acc[:, s0:s0 + w0]
+        for b in every:
+            sl = slice(b * wide + s0, b * wide + s0 + w0)
+            g = e_s[:, sl].astype(F32) * nn(vaug[rows(b), :c + 16], gobd[:, sl])
+            total += g
+            gl = g.astype(BF)
+            gs_s[:, sl] = gl
+            ores[:c, sl] = nn(k_t[:, rows(b)], gl)
+        acc[:, s0:s0 + w0] = total
+    gq_t = jnp.concatenate(
+        [jnp.concatenate([ores[chans(h), lanes(b, h)] for h in range(heads)], axis=0) for b in every], axis=1) * scale
     gqg_t = jnp.concatenate([gq_t, ggl_t], axis=0).astype(BF)
-    gk = nn(gs_s[...], qn[...]) * (1.0 / LOG2E)
-    gv = nn(e_s[...], gon[...])
-    gkv = jnp.concatenate([gk, gv], axis=1).astype(BF)
+    gk = [nn(gs_s[:, b * wide:(b + 1) * wide], qn[b * wide:(b + 1) * wide, :]) * (1.0 / LOG2E) for b in every]
+    gv = [nn(e_s[:, b * wide:(b + 1) * wide], gon[b * wide:(b + 1) * wide, :]) for b in every]
+    gkv = jnp.concatenate([jnp.concatenate([gk[b], gv[b]], axis=1) for b in every], axis=0).astype(BF)
     gqgw_ref[...] += nn(gqg_t, x)
     gkvw_ref[...] += nn(x.astype(F32).T.astype(BF), gkv)
     w_qg = jnp.concatenate([w_ref[:, :c], w_ref[:, 3 * c:]], axis=1)
-    gx_ref[0] = nt(gkv, w_ref[:, c:3 * c]) + nn(w_qg, gqg_t).T
-
-    @pl.when(j == last)
+    gx_ref[...] = (nt(gkv, w_ref[:, c:3 * c]) + nn(w_qg, gqg_t).T).reshape(gx_ref.shape)
+
+    @pl.when(step == last)
     def _():
         for h in range(heads):
             gb_ref[:, h * n:(h + 1) * n] = acc[:, h * n:(h + 1) * n].T.astype(gb_ref.dtype)
@@ -187,8 +197,9 @@
     heads = bias.shape[1] // n
     f = we.shape[1] // 2
     wide = heads * n
+    cb = batch(cols, 3)
     full = lambda shape: pl.BlockSpec(shape, lambda j: (0,) * len(shape))
-    col = pl.BlockSpec((1, n, c), lambda j: (j, 0, 0))
+    col = pl.BlockSpec((cb, n, c), lambda j: (j, 0, 0))
     outs = [
         jax.ShapeDtypeStruct((cols, n, c), F32),
         jax.ShapeDtypeStruct((cols, n, c), F32),
@@ -202,30 +213,33 @@
     ]
     return pl.pallas_call(
         functools.partial(column_kernel, heads),
-        grid=(cols,),
+        grid=(cols // cb,),
         in_specs=[col] + [full(v.shape) for v in (tgt, msk, bias, w, wt, wo, we, vec, z)],
         out_specs=[col, col] + [full(o.shape) for o in outs[2:]],
         out_shape=outs,
         scratch_shapes=[
             pltpu.VMEM((n, wide), F32),
-            pltpu.VMEM((n, wide), BF),
-            pltpu.VMEM((n, wide), BF),
+            pltpu.VMEM((n, cb * wide), BF),
+            pltpu.VMEM((n, cb * wide), BF),
             pltpu.VMEM((n, wide), F32),
-            pltpu.VMEM((c, wide), BF),
-            pltpu.VMEM((c + 16, wide), BF),
-            pltpu.VMEM((n, 2 * c), BF),
-            pltpu.VMEM((wide, c), BF),
-            pltpu.VMEM((wide, c), BF),
-            pltpu.VMEM((c + 16, wide), F32),
-            pltpu.VMEM((n, 2 * f), BF),
-            pltpu.VMEM((n, f), BF),
+            pltpu.VMEM((c, cb * wide), BF),
+            pltpu.VMEM((c + 16, cb * wide), BF),
+            pltpu.VMEM((cb * n, 2 * c), BF),
+            pltpu.VMEM((cb * wide, c), BF),
+            pltpu.VMEM((cb * wide, c), BF),
+            pltpu.VMEM((c + 16, cb * wide), F32),
+            pltpu.VMEM((cb * n, 2 * f), BF),
+            pltpu.VMEM((cb * n, f), BF),
         ],
         compiler_params=pltpu.CompilerParams(vmem_limit_bytes=56 << 20),
+        cost_estimate=cost(12 * cols * heads * n * n * 128, 16 * cols * n * c, cols * heads * n * n),
         name="columns",
     )(after, tgt, msk, bias, w, wt, wo, we, vec, z)
 
 
 GROUP = 16
+AFTER_BATCH = 4
+BACK_BATCH = 4
 
 
 def spread(scr, start, count, stride, value):
@@ -248,27 +262,24 @@
     wide = nc_ref.shape[1]
     own = off_ref[0]
     other = off_ref[1]
-
-    def step(k, carry):
+    for k in range(rows):
         x = x_ref[k].astype(F32)
         nrm, _ = norm(x)
         low = nrm.astype(BF)
         n_ref[k] = low
-        nscr[...] = nrm
-        xscr[...] = x
+        nscr[k] = nrm
+        xscr[k] = x
         p = nt(wl_ref[...], low)
         spread(lscr, k, half, rows, p[:half] * sigm(p[half:]))
-        near = [nscr[pl.ds(own, cols), :], nscr[pl.ds(other, cols), :]]
+    for k in range(rows):
+        near = [nscr[k, pl.ds(own, cols), :], nscr[k, pl.ds(other, cols), :]]
         if wide > 2 * cols:
             near.append(jnp.zeros((wide - 2 * cols, c), F32))
         near = jnp.concatenate(near, axis=0).astype(BF)
         nc_ref[k] = near
         p = nt(wr_ref[...], near)
         spread(rscr, k, half, rows, p[:half] * sigm(p[half:]))
-        cscr[pl.ds(k, cols, stride=rows), :] = xscr[pl.ds(own, cols), :]
-        return carry
-
-    lax.fori_loop(0, rows, step, 0)
+        cscr[pl.ds(k, cols, stride=rows), :] = xscr[k, pl.ds(own, cols), :]
     left_ref[...] = joined(lscr).astype(BF).reshape(left_ref.shape)
     right_ref[...] = joined(rscr).astype(BF).reshape(right_ref.shape)
     xc_ref[...] = cscr[...].astype(BF).reshape(xc_ref.shape)
@@ -308,12 +319,13 @@
         scratch_shapes=[
             pltpu.VMEM((n // 128, half * g, 128), F32),
             pltpu.VMEM((wide // 128, half * g, 128), F32),
-            pltpu.VMEM((n, c), F32),
-            pltpu.VMEM((n, c), F32),
+            pltpu.VMEM((g, n, c), F32),
+            pltpu.VMEM((g, n, c), F32),
             pltpu.VMEM((cols * g, c), F32),
         ],
         input_output_aliases=alias,
         compiler_params=pltpu.CompilerParams(vmem_limit_bytes=56 << 20),
+        cost_estimate=cost(4 * x.shape[0] * n * c * 2 * half, 6 * x.shape[0] * n * c, x.shape[0] * n * half),
         name="operands",
     )(*ins)
 
@@ -341,72 +353,90 @@
         out_shape=[out, out],
         scratch_shapes=[pltpu.VMEM((n // 128, 2 * cols * g, 128), F32)],
         compiler_params=pltpu.CompilerParams(vmem_limit_bytes=56 << 20),
+        cost_estimate=cost(2 * half * n * n * wide, 4 * half * n * n),
         name="products",
     )(left, right)
 
 
+def batch(count, most):
+    return max(b for b in range(1, most + 1) if count % b == 0)
+
+
+def product_rows(mine_ref, theirs_ref):
+    return jnp.concatenate(
+        [
+            jnp.concatenate([mine_ref[b].astype(F32), theirs_ref[b].astype(F32)], axis=0).T
+            for b in range(mine_ref.shape[0])
+        ],
+        axis=0,
+    )
+
+
 def after_kernel(heads, xc_ref, mine_ref, theirs_ref, w4_ref, wout_ref, wb_ref, vec_ref, after_ref, bias_ref):
-    n, c = xc_ref.shape[1:]
-    x = xc_ref[0].astype(F32)
+    cb, n, c = xc_ref.shape
+    x = xc_ref[...].astype(F32).reshape(cb * n, c)
     n0, _ = norm(x)
     gate = sigm(nn(n0.astype(BF), w4_ref[...]))
-    prod = jnp.concatenate([mine_ref[0].astype(F32), theirs_ref[0].astype(F32)], axis=0).T
-    nc, _ = norm(prod)
+    nc, _ = norm(product_rows(mine_ref, theirs_ref))
     lin = nn((nc * vec_ref[1:2, :]).astype(BF), wout_ref[...])
     after = x + (gate * lin).astype(BF).astype(F32)
-    after_ref[0] = after
+    after_ref[...] = after.reshape(after_ref.shape)
     n3, _ = norm(after)
     bias = nt(wb_ref[...], (n3 * vec_ref[2:3, :]).astype(BF))
-    for h in range(heads):
-        bias_ref[0, :, h * n:(h + 1) * n] = bias[h:h + 1]
+    for b in range(cb):
+        for h in range(heads):
+            bias_ref[b, :, h * n:(h + 1) * n] = bias[h:h + 1, b * n:(b + 1) * n]
 
 
 def afters(xc, mine, theirs, w4, wout, wb, vec, heads):
     cols, n, c = xc.shape
     half = mine.shape[1]
+    cb = batch(cols, AFTER_BATCH)
     full = lambda v: pl.BlockSpec(v.shape, lambda b: (0,) * v.ndim)
-    col = lambda a, b: pl.BlockSpec((1, a, b), lambda j: (j, 0, 0))
+    col = lambda a, b: pl.BlockSpec((cb, a, b), lambda j: (j, 0, 0))
     return pl.pallas_call(
         functools.partial(after_kernel, heads),
-        grid=(cols,),
+        grid=(cols // cb,),
         in_specs=[col(n, c), col(half, n), col(half, n), full(w4), full(wout), full(wb), full(vec)],
         out_specs=[col(n, c), col(1, heads * n)],
         out_shape=[jax.ShapeDtypeStruct((cols, n, c), F32), jax.ShapeDtypeStruct((cols, 1, heads * n), F32)],
-        compiler_params=pltpu.CompilerParams(vmem_limit_bytes=40 << 20),
+        compiler_params=pltpu.CompilerParams(vmem_limit_bytes=56 << 20),
+        cost_estimate=cost(8 * cols * n * c * c, 10 * cols * n * c, cols * n * c),
         name="afters",
     )(xc, mine, theirs, w4, wout, wb, vec)
 
 
 def back_kernel(after_ref, gx_ref, gmid_ref, gb_ref, xc_ref, mine_ref, theirs_ref, w4_ref, wout_ref, wb_ref, vec_ref,
                 gmine_ref, gtheirs_ref, gwb_ref, gwout_ref, gw4_ref, small_ref):
-    j = pl.program_id(0)
-
-    @pl.when(j == 0)
+    @pl.when(pl.program_id(0) == 0)
     def _():
         for ref in (gwb_ref, gwout_ref, gw4_ref, small_ref):
             ref[...] = jnp.zeros_like(ref)
 
-    n, c = xc_ref.shape[1:]
+    cb, n, c = xc_ref.shape
     half = mine_ref.shape[1]
     heads = gb_ref.shape[2]
+    flat = lambda ref: ref[...].reshape(cb * n, c)
     g1 = vec_ref[1:2, :]
     g2 = vec_ref[2:3, :]
-    n3, s3 = norm(after_ref[0])
+    n3, s3 = norm(flat(after_ref))
     x3 = (n3 * g2).astype(BF)
-    gb = gb_ref[0, 0].astype(F32)
-    for d in range(1, gb_ref.shape[0]):
-        gb = gb + gb_ref[d, 0].astype(F32)
-    gb = jnp.concatenate([gb, jnp.zeros((wb_ref.shape[0] - heads, n), F32)], axis=0)
+    parts = []
+    for b in range(cb):
+        gb = gb_ref[0, b].astype(F32)
+        for d in range(1, gb_ref.shape[0]):
+            gb = gb + gb_ref[d, b].astype(F32)
+        parts.append(jnp.concatenate([gb, jnp.zeros((wb_ref.shape[0] - heads, n), F32)], axis=0))
+    gb = jnp.concatenate(parts, axis=1)
     gwb_ref[...] += nn(gb.astype(BF), x3)
-    gx = (gx_ref[0] + nn(gb.T.astype(BF), wb_ref[...])).astype(BF).astype(F32)
+    gx = (flat(gx_ref) + nn(gb.T.astype(BF), wb_ref[...])).astype(BF).astype(F32)
     small_ref[0:1, :] += jnp.sum(gx * n3, axis=0, keepdims=True)
-    gafter = (gmid_ref[0] + norm_back(gx, g2, n3, s3)).astype(BF).astype(F32)
-
-    n0, _ = norm(xc_ref[0].astype(F32))
+    gafter = (flat(gmid_ref) + norm_back(gx, g2, n3, s3)).astype(BF).astype(F32)
+
+    n0, _ = norm(flat(xc_ref).astype(F32))
     n0 = n0.astype(BF)
     gate = sigm(nn(n0, w4_ref[...]))
-    prod = jnp.concatenate([mine_ref[0].astype(F32), theirs_ref[0].astype(F32)], axis=0).T
-    nc, sc = norm(prod)
+    nc, sc = norm(product_rows(mine_ref, theirs_ref))
     centre = (nc * g1).astype(BF)
     lin = nn(centre, wout_ref[...])
     glin = (gafter * gate).astype(BF)
@@ -415,26 +445,31 @@
     gw4_ref[...] += nn(n0.astype(F32).T.astype(BF), gp4)
     gc = nt(glin, wout_ref[...]).astype(BF).astype(F32)
     small_ref[1:2, :] += jnp.sum(gc * nc, axis=0, keepdims=True)
-    gprod = norm_back(gc, g1, nc, sc).T
-    gmine_ref[0] = gprod[:half].astype(BF)
-    gtheirs_ref[0] = gprod[half:].astype(BF)
+    gprod = norm_back(gc, g1, nc, sc)
+    for b in range(cb):
+        part = gprod[b * n:(b + 1) * n].T.astype(BF)
+        gmine_ref[b] = part[:half]
+        gtheirs_ref[b] = part[half:]
 
 
 def back_pass(after, gx, gmid, gb, xc, mine, theirs, w4, wout, wb, vec):
     cols, n, c = xc.shape
     half = mine.shape[1]
     heads = gb.shape[2]
+    cb = batch(cols, BACK_BATCH)
     full = lambda shape: pl.BlockSpec(shape, lambda b: (0,) * len(shape))
-    col = lambda a, b: pl.BlockSpec((1, a, b), lambda j: (j, 0, 0))
+    col = lambda a, b: pl.BlockSpec((cb, a, b), lambda j: (j, 0, 0))
     accs = [wb.shape, (c, c), (c, c), (8, c)]
     return pl.pallas_call(
         back_kernel,
-        grid=(cols,),
-        in_specs=[col(n, c)] * 3 + [pl.BlockSpec((gb.shape[0], 1, heads, n), lambda j: (0, j, 0, 0)), col(n, c), col(half, n), col(half, n)]
+        grid=(cols // cb,),
+        in_specs=[col(n, c)] * 3
+        + [pl.BlockSpec((gb.shape[0], cb, heads, n), lambda j: (0, j, 0, 0)), col(n, c), col(half, n), col(half, n)]
         + [full(v.shape) for v in (w4, wout, wb, vec)],
         out_specs=[col(half, n)] * 2 + [full(s) for s in accs],
         out_shape=[jax.ShapeDtypeStruct((cols, half, n), BF)] * 2 + [jax.ShapeDtypeStruct(s, F32) for s in accs],
-        compiler_params=pltpu.CompilerParams(vmem_limit_bytes=40 << 20),
+        compiler_params=pltpu.CompilerParams(vmem_limit_bytes=56 << 20),
+        cost_estimate=cost(16 * cols * n * c * c, 24 * cols * n * c, cols * n * c),
         name="back",
     )(after, gx, gmid, gb, xc, mine, theirs, w4, wout, wb, vec)
 
@@ -477,40 +512,40 @@
             pltpu.VMEM((wide // 128, n * g, 128), F32),
         ],
         compiler_params=pltpu.CompilerParams(vmem_limit_bytes=60 << 20),
+        cost_estimate=cost(4 * half * n * n * wide, 8 * half * n * n),
         name="operand_grads",
     )(left, right, gmine, gtheirs)
 
 
-def tri_grads_kernel(n_ref, nc_ref, gl_ref, gr_ref, wl_ref, wr_ref, al_ref, ar_ref):
+def tri_grads_kernel(n_ref, nc_ref, gl_ref, gr_ref, wl_ref, wr_ref, al_ref, ar_ref, lg, rg):
     @pl.when(pl.program_id(0) == 0)
     def _():
         al_ref[...] = jnp.zeros_like(al_ref)
         ar_ref[...] = jnp.zeros_like(ar_ref)
-
-    rows = n_ref.shape[0]
+    rows, n, c = n_ref.shape
+    wide = nc_ref.shape[1]
     half = gl_ref.shape[1]
-
     def one(low, grad, w):
         p = nt(w, low)
         s = sigm(p[half:])
         first = grad.astype(F32) * s
-        gp = jnp.concatenate([first, first * p[:half] * (1.0 - s)], axis=0).astype(BF)
-        return nn(gp, low)
-
-    left = al_ref[...]
-    right = ar_ref[...]
+        return first.astype(BF), (first * p[:half] * (1.0 - s)).astype(BF)
     for k in range(rows):
-        left += one(n_ref[k], gl_ref[k], wl_ref[...])
-        right += one(nc_ref[k], gr_ref[k], wr_ref[...])
-    al_ref[...] = left
-    ar_ref[...] = right
+        a, b = one(n_ref[k], gl_ref[k], wl_ref[...])
+        lg[:half, k*n:(k+1)*n] = a
+        lg[half:, k*n:(k+1)*n] = b
+        a, b = one(nc_ref[k], gr_ref[k], wr_ref[...])
+        rg[:half, k*wide:(k+1)*wide] = a
+        rg[half:, k*wide:(k+1)*wide] = b
+    al_ref[...] += nn(lg[...], n_ref[...].reshape(rows*n, c))
+    ar_ref[...] += nn(rg[...], nc_ref[...].reshape(rows*wide, c))
 
 
 def tri_grads(nrm, near, gl, gr, wl, wr):
     n, _, c = nrm.shape
     half = gl.shape[1]
     wide = near.shape[1]
-    rows = 8
+    rows = 24
     full = lambda v: pl.BlockSpec(v.shape, lambda b: (0,) * v.ndim)
     row = lambda a, b: pl.BlockSpec((rows, a, b), lambda k: (k, 0, 0))
     out = jax.ShapeDtypeStruct((2 * half, c), F32)
@@ -520,7 +555,9 @@
         in_specs=[row(n, c), row(wide, c), row(half, n), row(half, wide), full(wl), full(wr)],
         out_specs=[pl.BlockSpec(out.shape, lambda k: (0, 0))] * 2,
         out_shape=[out] * 2,
-        compiler_params=pltpu.CompilerParams(vmem_limit_bytes=40 << 20),
+        scratch_shapes=[pltpu.VMEM((2*half, rows*n), BF), pltpu.VMEM((2*half, rows*wide), BF)],
+        compiler_params=pltpu.CompilerParams(vmem_limit_bytes=56 << 20),
+        cost_estimate=cost(8 * n * n * c * c, 8 * n * n * c, n * n * half),
         name="tri_grads",
     )(nrm, near, gl, gr, wl, wr)
 
@@ -667,13 +704,6 @@
         after_c, both[0], both[1], bias_full, project_w, project_w.T, output_w, expand_mix, vec8, z
     )
     bias_cols = lax.all_to_all(gb, "pair", split_axis=0, concat_axis=0, tiled=True)
-    early = sum_shards(
-        [
-            jnp.concatenate(
-                [gqg_w[:width].T, gkv_w, gqg_w[width:].T, gow, gew, svec.reshape(width, -1)], axis=1
-            )
-        ]
-    )
     scalars = sum_all(jnp.stack([jnp.sum(small[2]), jnp.sum(weighting_rows)]))
     gmine, gsend, gwb, gwout, gw4, small2 = back_pass(
         after_c, gx, gmid, bias_cols.reshape(-1, cols, heads, tokens), xc, mine, theirs,
@@ -700,26 +730,40 @@
             g_read,
         ]
     )
-    late = sum_shards(
+    (total,) = sum_shards(
         [
             jnp.concatenate(
-                [a_tri * vec[0][:, None], jnp.roll(gwout, half * core, axis=0), gwb[:heads].T, g_vec.T],
+                [
+                    gqg_w[:width].T,
+                    gkv_w,
+                    gqg_w[width:].T,
+                    gow,
+                    gew,
+                    a_tri * vec[0][:, None],
+                    jnp.roll(gwout, half * core, axis=0),
+                    svec.reshape(width, -1),
+                    gwb[:heads].T,
+                    g_vec.T,
+                ],
                 axis=1,
             )
         ]
     )
     loss_sum, count = scalars[0], scalars[1]
-    at = [width * s for s in range(11)]
-    tall = early[0]
+    widths = (4 * width, width, 2 * hidden, 5 * width, width, svec.shape[1] // width, heads)
+    cuts = []
+    for w in widths:
+        cuts.append(total[:, :w])
+        total = total[:, w:]
     shards = [
-        late[0][:, : at[5]],
-        late[0][:, at[5] : at[6]],
-        tall[:, : at[4]],
-        late[0][:, at[6] : at[6] + heads],
-        tall[:, at[4] : at[5]],
-        tall[:, at[5] : at[5] + 2 * hidden].reshape(-1, hidden // 128, 2, 128).swapaxes(1, 2).reshape(-1, 2 * hidden),
-        tall[:, at[5] + 2 * hidden :].reshape(-1, 1) * vec[4][None, :],
-        late[0][:, at[6] + heads :].T,
+        cuts[3],
+        cuts[4],
+        cuts[0],
+        cuts[6],
+        cuts[1],
+        cuts[2].reshape(-1, hidden // 128, 2, 128).swapaxes(1, 2).reshape(-1, 2 * hidden),
+        cuts[5].reshape(-1, 1) * vec[4][None, :],
+        total.T,
     ]
     shards = [s / count for s in shards]
     squares = sum_axis(sum(jnp.sum(s * s) for s in shards), "item")

time: 1160 us -> 805 us (0.69)
  Pallas kernels: 845 us -> 457 us
  waiting for transfers between devices: 131 us -> 181 us
  local copies, waits for them, and re-layouts: 69.2 us -> 27.7 us
  blocking collectives: 21.3 us -> 41.5 us
    pallas_call x3, Pallas kernels: 463 us -> 267 us  [the longest x1 202 us: column_pass(): pl.pallas_call(functools.partial(column_kernel, heads), grid=(cols // cb,...]
    pallas_call x1, Pallas kernels: 147 us -> 43.3 us  [tri_grads(): pl.pallas_call(tri_grads_kernel, grid=(n // rows,), in_specs=[row(n, c),...]
    pallas_call x3, Pallas kernels: 183 us -> 94.8 us  [operands(): pl.pallas_call(functools.partial(operand_kernel, cols), grid=(x.shape[0]...]
    all_gather x3, waiting for transfers between devices: 75.5 us -> 134 us  [gather_rows(): lax.all_gather(pair_act[0, m * rows:(m + 1) * rows], 'pair', axis=0, tile...]
    unnamed x179 -> x86, local copies, waits for them, and re-layouts: 41.5 us -> 9.69 us
    all_to_all x0 -> x1, blocking collectives: none -> 20.2 us  [on_device(): lax.all_to_all(gb, 'pair', split_axis=0, concat_axis=0, tiled=True)]
    ppermute x17 -> x12, waiting for transfers between devices: 49.1 us -> 31.4 us  [exchange(): return lax.ppermute(value, axis, [(d, d ^ bit) for d in range(size)])]
  transfers between devices with their start and end apart: 25 -> 19, of which waited for: 17 -> 16; matrix products, arithmetic and copies ran while one was open for 5% -> 3% of each run, Pallas kernels for 33% -> 8%
where the time goes in v3:
time: 805 us; the launch traced here: 789 us
  Pallas kernels  457 us (57%)
  waiting for transfers between devices  181 us (22%)
  blocking collectives  41.5 us (5%)
  other arithmetic  38.1 us (5%)
  local copies, waits for them, and re-layouts  27.7 us (3%)
  between operations  22.5 us (3%)
  starting transfers between devices  21.3 us (3%)
    pallas_call x1, Pallas kernels, column_pass(): pl.pallas_call(functools.partial(column_kernel, heads), grid=(cols // cb,...  202 us
    all_gather x3, waiting for transfers between devices, gather_rows(): lax.all_gather(pair_act[0, m * rows:(m + 1) * rows], 'pair', axis=0, tile...  134 us
    pallas_call x3, Pallas kernels, operands(): pl.pallas_call(functools.partial(operand_kernel, cols), grid=(x.shape[0]...  94.8 us
    pallas_call x1, Pallas kernels, back_pass(): pl.pallas_call(back_kernel, grid=(cols // cb,), in_specs=[col(n, c)] * 3...  43.5 us
    pallas_call x1, Pallas kernels, tri_grads(): pl.pallas_call(tri_grads_kernel, grid=(n // rows,), in_specs=[row(n, c),...  43.3 us
    pallas_call x1, Pallas kernels, operand_grads(): pl.pallas_call(operand_grads_kernel, grid=(half // g,), in_specs=[pl.Bloc...  38.3 us
    ppermute x12, waiting for transfers between devices, exchange(): return lax.ppermute(value, axis, [(d, d ^ bit) for d in range(size)])  31.4 us
    pallas_call x1, Pallas kernels, afters(): pl.pallas_call(functools.partial(after_kernel, heads), grid=(cols // cb,)...  21.6 us
  transfers between devices with their start and end apart: 19, of which 16 were waited for; matrix products, arithmetic and copies ran while one was open for 3% of the time, Pallas kernels for 8%

profile of v3, /device:TPU:0, one launch (start us, length us, event | category | flops | bytes accessed | tf_op | source)
XLA Modules:
  0.0 789.5 jit_solution(18232432894246706702)
XLA Ops:
  7.2 4.6 fusion.24
  14.0 21.3 %all_gather.16 = bf16[128,2953]{1,0:T(8,128)(2,1)S(1)} all-gather(bf16[32,2953]{1,0:T(8,128)(2,1)S(1)} %concatenate.35), channel_id=1, replica_groups=mesh['item'=4,'pair'=8] {'item'}, dimensions={0}, use_global_device_ids=true | all-gather | bytes 944960 | tf_op jit(solution)/shard_map/all_gather | solution.py:569
  37.6 49.4 %all-gather.13.cloned.1.call-done = bf16[1,128,384,128]{3,2,0,1:T(8,128)(2,1)} async-done(((bf16[1,16,384,128]{3,2,0,1:T(8,128)(2,1)}), bf16[1,128,384,128]{3,2,0,1:T(8,128)(2,1)}) %all-gather.13.cloned.1.call-update) | async-done | bytes 12582928 | tf_op jit(solution)/shard_map/all_gather | solution.py:581
  86.9 31.6 %operands.3 = (bf16[64,384,384]{2,1,0:T(8,128)(2,1)}, bf16[64,384,128]{2,1,0:T(8,128)(2,1)}, bf16[384,384,128]{2,1,0:T(8,128)(2,1)}, bf16[384,128,128]{2,1,0:T(8,128)(2,1)}, bf16[48,384,128]{2,1,0:T(8,128)(2,1)}) custom-call(s32[2]{0:T(128)} %pad_add_fusion.off_ref, bf16[128,384,128]{2,1,0:T(8,128)(2,1)} %bitcast.126, ...), custom_call_target="tpu_custom_call" | custom-call | flops 3221225472 | bytes 37748736 | tf_op jit(solution)/shard_map/operands/pallas_call | solution.py:313
  118.5 42.5 %all-gather.11.cloned.1.call-done = bf16[1,128,384,128]{3,2,0,1:T(8,128)(2,1)} async-done(((bf16[1,16,384,128]{3,2,0,1:T(8,128)(2,1)}), bf16[1,128,384,128]{3,2,0,1:T(8,128)(2,1)}) %all-gather.11.cloned.1.call-update) | async-done | bytes 12582928 | tf_op jit(solution)/shard_map/all_gather | solution.py:581
  161.0 31.6 %operands.4 = (bf16[64,384,384]{2,1,0:T(8,128)(2,1)}, bf16[64,384,128]{2,1,0:T(8,128)(2,1)}, bf16[384,384,128]{2,1,0:T(8,128)(2,1)}, bf16[384,128,128]{2,1,0:T(8,128)(2,1)}, bf16[48,384,128]{2,1,0:T(8,128)(2,1)}) custom-call(s32[2]{0:T(128)} %pad_add_fusion.off_ref, ...), custom_call_target="tpu_custom_call", output_to_operand_aliasing={{0}: (4, {}), {1}: (5, {}), {2}: (6, {}), {3}: (7, {}), {4}... | custom-call | flops 3221225472 | bytes 37748736 | tf_op jit(solution)/shard_map/operands/pallas_call | solution.py:313
  192.6 42.5 %all-gather.9.cloned.1.call-done = bf16[1,128,384,128]{3,2,0,1:T(8,128)(2,1)} async-done(((bf16[1,16,384,128]{3,2,0,1:T(8,128)(2,1)}), bf16[1,128,384,128]{3,2,0,1:T(8,128)(2,1)}) %all-gather.9.cloned.1.call-update) | async-done | bytes 12582928 | tf_op jit(solution)/shard_map/all_gather | solution.py:581
  235.1 31.6 %operands.5 = (bf16[64,384,384]{2,1,0:T(8,128)(2,1)}, bf16[64,384,128]{2,1,0:T(8,128)(2,1)}, bf16[384,384,128]{2,1,0:T(8,128)(2,1)}, bf16[384,128,128]{2,1,0:T(8,128)(2,1)}, bf16[48,384,128]{2,1,0:T(8,128)(2,1)}) custom-call(s32[2]{0:T(128)} %pad_add_fusion.off_ref, ...), custom_call_target="tpu_custom_call", output_to_operand_aliasing={{0}: (4, {}), {1}: (5, {}), {2}: (6, {}), {3}: (7, {}), {4}... | custom-call | flops 3221225472 | bytes 37748736 | tf_op jit(solution)/shard_map/operands/pallas_call | solution.py:313
  266.7 13.7 %products.1 = (bf16[48,64,384]{2,1,0:T(8,128)(2,1)}, bf16[48,64,384]{2,1,0:T(8,128)(2,1)}) custom-call(bf16[64,384,384]{2,1,0:T(8,128)(2,1)} %get-tuple-element.77.left_ref, bf16[64,384,128]{2,1,0:T(8,128)(2,1)} %get-tuple-element.78.right_ref), custom_call_target="tpu_custom_call" | custom-call | flops 2415919104 | bytes 37748736 | tf_op jit(solution)/shard_map/products/pallas_call | solution.py:348
  286.5 21.6 %afters.1 = (f32[48,384,128]{2,1,0:T(8,128)}, f32[48,1,1536]{2,1,0:T(1,128)}) custom-call(bf16[48,384,128]{2,1,0:T(8,128)(2,1)} %get-tuple-element.76.xc_ref, bf16[48,64,384]{2,1,0:T(8,128)(2,1)} %get-tuple-element.79.mine_ref, bf16[48,64,384]{2,1,0:T(8,128)(2,1)} %copy-done, bf16[128,128]{1,0:T(8,128)(2,1)} %copy.231.w4_ref, ...), custom_call_target="tpu_custom_call" | custom-call | flops 2415919104 | bytes 23592960 | tf_op jit(solution)/shard_map/afters/pallas_call | solution.py:397
  311.4 3.4 all-to-all-start
  317.6 2.9 all-to-all-done
  323.7 10.4 %all-gather.15.cloned.1.call-done = bf16[384,1,1536]{2,0,1:T(8,128)(2,1)} async-done(((bf16[48,1,1536]{2,0,1:T(8,128)(2,1)}), bf16[384,1,1536]{2,0,1:T(8,128)(2,1)}) %all-gather.15.cloned.1.call-update) | async-done | bytes 1179664 | tf_op jit(solution)/shard_map/all_gather | solution.py:697
  334.0 201.9 %columns.1 = (f32[48,384,128]{2,1,0:T(8,128)}, f32[48,384,128]{2,1,0:T(8,128)}, bf16[384,1536]{1,0:T(8,128)(2,1)}, f32[128,256]{1,0:T(8,128)}, f32[256,128]{1,0:...) custom-call(f32[48,384,128]{2,1,0:T(8,128)} %get-tuple-element.81.after_ref, ...), custom_call_target="tpu_custom_call" | custom-call | flops 43486543872 | bytes 37748736 | tf_op jit(solution)/shard_map/columns/pallas_call | solution.py:214
  536.0 20.2 %all_to_all.24 = bf16[8,48,1536]{2,1,0:T(8,128)(2,1)S(1)} all-to-all(bf16[8,48,1536]{2,1,0:T(8,128)(2,1)} %bitcast.133), channel_id=1, replica_groups=mesh['item'=4,'pair'=8] {'pair'}, dimensions={0} | all-to-all | bytes 2359296 | tf_op jit(solution)/shard_map/all_to_all | solution.py:706
  557.4 43.5 %back.1 = (bf16[48,64,384]{2,1,0:T(8,128)(2,1)}, bf16[48,64,384]{2,1,0:T(8,128)(2,1)}, f32[16,128]{1,0:T(8,128)}, f32[128,128]{1,0:T(8,128)}, f32[128,128]{1,0:T(8,128)}, /*index=5*/f32[8,128]{1,0:T(8,128)}) custom-call(f32[48,384,128]{2,1,0:T(8,128)} %get-tuple-element.81.after_ref, f32[48,384,128]{2,1,0:T(8,128)} %get-tuple-element.90.gx_ref, ...), custom_call_target="tpu_custom_call" | custom-call | flops 4831838208 | bytes 56623104 | tf_op jit(solution)/shard_map/back/pallas_call | solution.py:463
  608.9 38.3 %operand_grads.1 = (bf16[384,64,384]{2,1,0:T(8,128)(2,1)}, bf16[384,64,128]{2,1,0:T(8,128)(2,1)}) custom-call(bf16[64,384,384]{2,1,0:T(8,128)(2,1)} %get-tuple-element.77.left_ref, bf16[64,384,128]{2,1,0:T(8,128)(2,1)} %get-tuple-element.78.right_ref, bf16[48,64,384]{2,1,0:T(8,128)(2,1)} %get-tuple-element.93.gm_ref, bf16[48,64,384]{2,1,0:T(8,128)(2,1)} %copy-done.1), custom_call_target="tpu_custom_call" | custom-call | flops 4831838208 | bytes 75497472 | tf_op jit(solution)/shard_map/operand_grads/pallas_call | solution.py:502
  647.2 43.3 %tri_grads.1 = (f32[128,128]{1,0:T(8,128)}, f32[128,128]{1,0:T(8,128)}) custom-call(bf16[384,384,128]{2,1,0:T(8,128)(2,1)} %get-tuple-element.88.n_ref, bf16[384,128,128]{2,1,0:T(8,128)(2,1)} %get-tuple-element.89.nc_ref, bf16[384,64,384]{2,1,0:T(8,128)(2,1)} %get-tuple-element.95.gl_ref, bf16[384,64,128]{2,1,0:T(8,128)(2,1)} %get-tuple-element.96.gr_ref, ...), custom_call_target="tpu_custom_call" | custom-call | flops 19327352832 | bytes 150994944 | tf_op jit(solution)/shard_map/tri_grads/pallas_call | solution.py:552
  700.1 15.4 %collective-permute-done.7 = bf16[64,2445]{1,0:T(8,128)(2,1)S(1)} collective-permute-done((bf16[64,2445]{1,0:T(8,128)(2,1)S(1)}, bf16[64,2445]{1,0:T(8,128)(2,1)S(1)}, u32[]{:S(2)}, u32[]{:S(2)}) %collective-permute-start.7) | collective-permute-done | bytes 312992 | tf_op jit(solution)/shard_map/ppermute | solution.py:593
  716.3 5.1 collective-permute-done.8
  730.7 2.7 collective-permute-start.2
  742.1 2.6 collective-permute-done.5
  759.7 2.8 collective-permute-start.12
  764.1 4.0 collective-permute-start.13
  (230 shorter events, 80.0 us)
Async XLA Ops:
  7.2 79.7 %all-gather.13.cloned.1.call-start = ((), (), s32[]{:S(2)}) async-start(), calls=%async_computation.4 | async-start | bytes 14155776 | tf_op jit(solution)/shard_map/all_gather | solution.py:581
  12.0 149.0 %all-gather.11.cloned.1.call-start = ((), (), s32[]{:S(2)}) async-start(), calls=%async_computation.3 | async-start | bytes 14155776 | tf_op jit(solution)/shard_map/all_gather | solution.py:581
  12.7 222.3 %all-gather.9.cloned.1.call-start = ((), (), s32[]{:S(2)}) async-start(), calls=%async_computation.2 | async-start | bytes 14155776 | tf_op jit(solution)/shard_map/all_gather | solution.py:581
  13.5 320.6 %all-gather.15.cloned.1.call-start = ((), (), s32[]{:S(2)}) async-start(), calls=%async_computation.5 | async-start | bytes 1327104 | tf_op jit(solution)/shard_map/all_gather | solution.py:697
  280.4 4.7 collective-permute-start
  311.4 9.1 %all-to-all-start = ((f32[8,1,4608]{2,1,0:T(1,128)}), f32[8,1,4608]{2,1,0:T(1,128)S(1)}, u32[]{:S(2)}, u32[]{:S(2)}) async-start(f32[8,1,4608]{2,1,0:T(1,128)} %reshape.296), calls=%async_computation | async-start | bytes 294912 | tf_op jit(solution)/shard_map/all_to_all | solution.py:668
  600.9 6.6 collective-permute-start.6
  697.6 80.5 %copy-start.3 = (f32[1,32,1024]{2,1,0:T(8,128)S(1)}, f32[1,32,1024]{2,1,0:T(8,128)}, u32[]{:S(2)}) copy-start(f32[1,32,1024]{2,1,0:T(8,128)} %param.37) | copy-start | bytes 393220
  697.6 80.5 %copy-start.13 = (f32[1,32,1024]{2,1,0:T(8,128)S(1)}, f32[1,32,1024]{2,1,0:T(8,128)}, u32[]{:S(2)}) copy-start(f32[1,32,1024]{2,1,0:T(8,128)} %param.45) | copy-start | bytes 393220
  697.6 80.5 %copy-start.14 = (f32[1,32,1024]{2,1,0:T(8,128)S(1)}, f32[1,32,1024]{2,1,0:T(8,128)}, u32[]{:S(2)}) copy-start(f32[1,32,1024]{2,1,0:T(8,128)} %param.53) | copy-start | bytes 393220
  697.6 18.0 %collective-permute-start.7 = (bf16[64,2445]{1,0:T(8,128)(2,1)S(1)}, bf16[64,2445]{1,0:T(8,128)(2,1)S(1)}, u32[]{:S(2)}, u32[]{:S(2)}) collective-permute-start(bf16[64,2445]{1,0:T(8,128)(2,1)S(1)} %dynamic-slice_convert_fusion), channel_id=1, source_target_pairs={{0,16},{8,24},{16,0},{24,8},{1,17},{9,25},{17,1},{25,9},{2,18},{10... | collective-permute-start | bytes 938888 | tf_op jit(solution)/shard_map/ppermute | solution.py:593
  700.1 80.1 %copy-start.31 = (f32[1,32,128]{2,1,0:T(8,128)S(1)}, f32[1,32,128]{2,1,0:T(8,128)}, u32[]{:S(2)}) copy-start(f32[1,32,128]{2,1,0:T(8,128)} %param.49) | copy-start | bytes 49156
  700.1 80.1 %copy-start.32 = (f32[1,32,128]{2,1,0:T(8,128)S(1)}, f32[1,32,128]{2,1,0:T(8,128)}, u32[]{:S(2)}) copy-start(f32[1,32,128]{2,1,0:T(8,128)} %param.41) | copy-start | bytes 49156
  715.7 5.7 collective-permute-start.8
  721.4 2.3 collective-permute-start.9
  723.8 10.2 %collective-permute-start.10 = (f32[32,2445]{1,0:T(8,128)S(1)}, f32[32,2445]{1,0:T(8,128)S(1)}, u32[]{:S(2)}, u32[]{:S(2)}) collective-permute-start(f32[32,2445]{1,0:T(8,128)S(1)} %add.279), channel_id=1, source_target_pairs={{0,2},{1,3},{2,0},{3,1},{4,6},{5,7},{6,4},{7,5},{8,10},{9,11},{10,... | collective-permute-start | bytes 938888 | tf_op jit(solution)/shard_map/ppermute | solution.py:593
  725.8 3.5 collective-permute-start.1
  730.7 4.4 collective-permute-start.2
  734.0 11.3 %collective-permute-start.11 = (f32[32,2445]{1,0:T(8,128)S(1)}, f32[32,2445]{1,0:T(8,128)S(1)}, u32[]{:S(2)}, u32[]{:S(2)}) collective-permute-start(f32[32,2445]{1,0:T(8,128)S(1)} %add.280), channel_id=1, source_target_pairs={{0,4},{1,5},{2,6},{3,7},{4,0},{5,1},{6,2},{7,3},{8,12},{9,13},{10,... | collective-permute-start | bytes 938888 | tf_op jit(solution)/shard_map/ppermute | solution.py:593
  736.5 1.1 collective-permute-start.3
  737.6 3.5 collective-permute-start.4
  741.2 3.5 collective-permute-start.5
  759.7 3.7 collective-permute-start.12
  764.1 4.6 collective-permute-start.13
  (32 other events, 1373.2 us)
Sparse Core Ops, SparseCore 0:
  12.1 74.8 all-gather.12
  88.8 72.1 all-gather.10
  162.9 72.1 all-gather.8
  309.9 24.0 all-gather.14

commit v4 on v3

--- a/solution.py
+++ b/solution.py
@@ -256,10 +256,10 @@
 
 
 def operand_kernel(cols, off_ref, x_ref, wl_ref, wr_ref, *refs):
-    left_ref, right_ref, n_ref, nc_ref, xc_ref, lscr, rscr, nscr, xscr, cscr = refs[-10:]
+    keep_l, keep_r, send_l, send_r, n_ref, nc_ref, xc_ref, xs_ref, lscr, rscr, nscr, xscr, cscr = refs[-13:]
     rows, n, c = x_ref.shape
-    half = wl_ref.shape[0] // 2
     wide = nc_ref.shape[1]
+    half = c // 2
     own = off_ref[0]
     other = off_ref[1]
     for k in range(rows):
@@ -270,92 +270,108 @@
         nscr[k] = nrm
         xscr[k] = x
         p = nt(wl_ref[...], low)
-        spread(lscr, k, half, rows, p[:half] * sigm(p[half:]))
+        spread(lscr, k, c, rows, p[:c] * sigm(p[c:]))
+    blank = [jnp.zeros((wide - 2 * cols, c), F32)] if wide > 2 * cols else []
     for k in range(rows):
-        near = [nscr[k, pl.ds(own, cols), :], nscr[k, pl.ds(other, cols), :]]
-        if wide > 2 * cols:
-            near.append(jnp.zeros((wide - 2 * cols, c), F32))
-        near = jnp.concatenate(near, axis=0).astype(BF)
+        mine, theirs = nscr[k, pl.ds(own, cols), :], nscr[k, pl.ds(other, cols), :]
+        near = jnp.concatenate([mine, theirs] + blank, axis=0).astype(BF)
         nc_ref[k] = near
-        p = nt(wr_ref[...], near)
+        turned = jnp.concatenate([theirs, mine] + blank, axis=0).astype(BF)
+        p = nt(wr_ref[:c], near)
         spread(rscr, k, half, rows, p[:half] * sigm(p[half:]))
+        p = nt(wr_ref[c:], turned)
+        spread(rscr, half * rows + k, half, rows, p[:half] * sigm(p[half:]))
         cscr[pl.ds(k, cols, stride=rows), :] = xscr[k, pl.ds(own, cols), :]
-    left_ref[...] = joined(lscr).astype(BF).reshape(left_ref.shape)
-    right_ref[...] = joined(rscr).astype(BF).reshape(right_ref.shape)
-    xc_ref[...] = cscr[...].astype(BF).reshape(xc_ref.shape)
-
-
-def operands(offs, x, wl, wr, cols, place, bufs):
-    n, c = x.shape[1], x.shape[2]
-    half = wl.shape[0] // 2
+        cscr[pl.ds(cols * rows + k, cols, stride=rows), :] = xscr[k, pl.ds(other, cols), :]
+    for scr, keep, send in ((lscr, keep_l, send_l), (rscr, keep_r, send_r)):
+        cut = half * rows
+        keep[...] = joined(scr, slice(0, cut)).astype(BF).reshape(keep.shape)
+        send[...] = joined(scr, slice(cut, None)).astype(BF).reshape(send.shape)
+    xc_ref[...] = cscr[:cols * rows].astype(BF).reshape(xc_ref.shape)
+    xs_ref[...] = cscr[cols * rows:].astype(BF).reshape(xs_ref.shape)
+
+
+def operands(offs, x, wl, wr, cols, start, total, bufs):
+    count, n, c = x.shape
+    half = c // 2
     wide = padded(2 * cols)
     g = GROUP
+    at = start // g
     shapes = [
-        ((half, n, n), (half, g, n), lambda b: (0, place(b), 0)),
-        ((half, n, wide), (half, g, wide), lambda b: (0, place(b), 0)),
-        ((n, n, c), (g, n, c), lambda b: (place(b), 0, 0)),
-        ((n, wide, c), (g, wide, c), lambda b: (place(b), 0, 0)),
-        ((cols, n, c), (cols, g, c), lambda b: (0, place(b), 0)),
+        ((half, count, n), (half, g, n), lambda b, o: (0, b, 0)),
+        ((half, count, wide), (half, g, wide), lambda b, o: (0, b, 0)),
+        ((half, count, n), (half, g, n), lambda b, o: (0, b, 0)),
+        ((half, count, wide), (half, g, wide), lambda b, o: (0, b, 0)),
+        ((total, n, c), (g, n, c), lambda b, o: (at + b, 0, 0)),
+        ((total, wide, c), (g, wide, c), lambda b, o: (at + b, 0, 0)),
+        ((cols, total, c), (cols, g, c), lambda b, o: (0, o[2 + at + b], 0)),
+        ((cols, total, c), (cols, g, c), lambda b, o: (0, o[2 + at + b], 0)),
     ]
-    full = lambda v: pl.BlockSpec(v.shape, lambda b: (0,) * v.ndim)
-    ins = [offs, x, wl, wr]
-    specs = [
-        pl.BlockSpec(memory_space=pltpu.SMEM),
-        pl.BlockSpec((g, n, c), lambda b: (b, 0, 0)),
-        full(wl),
-        full(wr),
-    ]
+    full = lambda v: pl.BlockSpec(v.shape, lambda b, o: (0,) * v.ndim)
+    ins = [x, wl, wr]
+    specs = [pl.BlockSpec((g, n, c), lambda b, o: (b, 0, 0)), full(wl), full(wr)]
     alias = {}
     if bufs is not None:
-        alias = {4 + i: i for i in range(5)}
+        alias = {4 + i: 4 + i for i in range(4)}
         ins += list(bufs)
-        specs += [pl.BlockSpec(memory_space=pl.ANY)] * 5
-    return pl.pallas_call(
+        specs += [pl.BlockSpec(memory_space=pl.ANY)] * 4
+    got = pl.pallas_call(
         functools.partial(operand_kernel, cols),
-        grid=(x.shape[0] // g,),
-        in_specs=specs,
-        out_specs=[pl.BlockSpec(b, m) for _, b, m in shapes],
+        grid_spec=pltpu.PrefetchScalarGridSpec(
+            num_scalar_prefetch=1,
+            grid=(count // g,),
+            in_specs=specs,
+            out_specs=[pl.BlockSpec(b, m) for _, b, m in shapes],
+            scratch_shapes=[
+                pltpu.VMEM((n // 128, c * g, 128), F32),
+                pltpu.VMEM((wide // 128, c * g, 128), F32),
+                pltpu.VMEM((g, n, c), F32),
+                pltpu.VMEM((g, n, c), F32),
+                pltpu.VMEM((2 * cols * g, c), F32),
+            ],
+        ),
         out_shape=[jax.ShapeDtypeStruct(s, BF) for s, _, _ in shapes],
-        scratch_shapes=[
-            pltpu.VMEM((n // 128, half * g, 128), F32),
-            pltpu.VMEM((wide // 128, half * g, 128), F32),
-            pltpu.VMEM((g, n, c), F32),
-            pltpu.VMEM((g, n, c), F32),
-            pltpu.VMEM((cols * g, c), F32),
-        ],
         input_output_aliases=alias,
-        compiler_params=pltpu.CompilerParams(vmem_limit_bytes=56 << 20),
-        cost_estimate=cost(4 * x.shape[0] * n * c * 2 * half, 6 * x.shape[0] * n * c, x.shape[0] * n * half),
+        compiler_params=pltpu.CompilerParams(vmem_limit_bytes=60 << 20),
+        cost_estimate=cost(8 * count * n * c * c, 8 * count * n * c, count * n * c),
         name="operands",
-    )(*ins)
-
-
-def product_kernel(left_ref, right_ref, mine_ref, theirs_ref, scr):
-    g = left_ref.shape[0]
+    )(offs, *ins)
+    return got[:2], got[2:4], got[4:]
+
+
+def product_kernel(groups, *refs):
+    lefts, rights = refs[:groups], refs[groups:2 * groups]
+    mine_ref, theirs_ref, scr = refs[2 * groups:]
+    g = lefts[0].shape[0]
     cols = mine_ref.shape[0]
     for e in range(g):
-        part = lax.dot_general(right_ref[e], left_ref[e], (((0,), (0,)), ((), ())), preferred_element_type=F32)
+        part = lax.dot_general(
+            jnp.concatenate([r[e] for r in rights], axis=0),
+            jnp.concatenate([r[e] for r in lefts], axis=0),
+            (((0,), (0,)), ((), ())),
+            preferred_element_type=F32,
+        )
         spread(scr, e, 2 * cols, g, part[: 2 * cols])
     mine_ref[...] = joined(scr, slice(0, cols * g)).astype(mine_ref.dtype).reshape(mine_ref.shape)
     theirs_ref[...] = joined(scr, slice(cols * g, None)).astype(theirs_ref.dtype).reshape(theirs_ref.shape)
 
 
-def products(left, right, cols):
-    half, n, _ = left.shape
-    wide = right.shape[2]
+def products(lefts, rights, cols):
+    half, _, n = lefts[0].shape
+    wide = rights[0].shape[2]
     g = GROUP
     out = jax.ShapeDtypeStruct((cols, half, n), BF)
     return pl.pallas_call(
-        product_kernel,
+        functools.partial(product_kernel, len(lefts)),
         grid=(half // g,),
-        in_specs=[pl.BlockSpec((g, n, n), lambda b: (b, 0, 0)), pl.BlockSpec((g, n, wide), lambda b: (b, 0, 0))],
+        in_specs=[pl.BlockSpec((g,) + v.shape[1:], lambda b: (b, 0, 0)) for v in lefts + rights],
         out_specs=[pl.BlockSpec((cols, g, n), lambda b: (0, b, 0))] * 2,
         out_shape=[out, out],
         scratch_shapes=[pltpu.VMEM((n // 128, 2 * cols * g, 128), F32)],
         compiler_params=pltpu.CompilerParams(vmem_limit_bytes=56 << 20),
         cost_estimate=cost(2 * half * n * n * wide, 4 * half * n * n),
         name="products",
-    )(left, right)
+    )(*lefts, *rights)
 
 
 def batch(count, most):
@@ -372,9 +388,19 @@
     )
 
 
-def after_kernel(heads, xc_ref, mine_ref, theirs_ref, w4_ref, wout_ref, wb_ref, vec_ref, after_ref, bias_ref):
+def after_kernel(heads, core_ref, xm_ref, xo_ref, mine_ref, theirs_ref, w4_ref, wout_ref, wb_ref, vec_ref,
+                 after_ref, bias_ref, xc_ref):
     cb, n, c = xc_ref.shape
-    x = xc_ref[...].astype(F32).reshape(cb * n, c)
+    first = core_ref[0] == 0
+    span = core_ref.shape[0]
+    parts = []
+    for b in range(cb):
+        near, far = xm_ref[b].astype(F32), xo_ref[b].astype(F32)
+        low, high = jnp.where(first, near, far), jnp.where(first, far, near)
+        for r in range(0, n // 2, span):
+            parts += [low[r:r + span], high[r:r + span]]
+    x = jnp.concatenate(parts, axis=0)
+    xc_ref[...] = x.astype(BF).reshape(xc_ref.shape)
     n0, _ = norm(x)
     gate = sigm(nn(n0.astype(BF), w4_ref[...]))
     nc, _ = norm(product_rows(mine_ref, theirs_ref))
@@ -388,8 +414,9 @@
             bias_ref[b, :, h * n:(h + 1) * n] = bias[h:h + 1, b * n:(b + 1) * n]
 
 
-def afters(xc, mine, theirs, w4, wout, wb, vec, heads):
-    cols, n, c = xc.shape
+def afters(core, xm, xo, mine, theirs, w4, wout, wb, vec, heads):
+    cols, rows, c = xm.shape
+    n = 2 * rows
     half = mine.shape[1]
     cb = batch(cols, AFTER_BATCH)
     full = lambda v: pl.BlockSpec(v.shape, lambda b: (0,) * v.ndim)
@@ -397,13 +424,18 @@
     return pl.pallas_call(
         functools.partial(after_kernel, heads),
         grid=(cols // cb,),
-        in_specs=[col(n, c), col(half, n), col(half, n), full(w4), full(wout), full(wb), full(vec)],
-        out_specs=[col(n, c), col(1, heads * n)],
-        out_shape=[jax.ShapeDtypeStruct((cols, n, c), F32), jax.ShapeDtypeStruct((cols, 1, heads * n), F32)],
+        in_specs=[pl.BlockSpec(memory_space=pltpu.SMEM), col(rows, c), col(rows, c), col(half, n), col(half, n)]
+        + [full(v) for v in (w4, wout, wb, vec)],
+        out_specs=[col(n, c), col(1, heads * n), col(n, c)],
+        out_shape=[
+            jax.ShapeDtypeStruct((cols, n, c), F32),
+            jax.ShapeDtypeStruct((cols, 1, heads * n), F32),
+            jax.ShapeDtypeStruct((cols, n, c), BF),
+        ],
         compiler_params=pltpu.CompilerParams(vmem_limit_bytes=56 << 20),
         cost_estimate=cost(8 * cols * n * c * c, 10 * cols * n * c, cols * n * c),
         name="afters",
-    )(xc, mine, theirs, w4, wout, wb, vec)
+    )(core, xm, xo, mine, theirs, w4, wout, wb, vec)
 
 
 def back_kernel(after_ref, gx_ref, gmid_ref, gb_ref, xc_ref, mine_ref, theirs_ref, w4_ref, wout_ref, wb_ref, vec_ref,
@@ -474,47 +506,58 @@
     )(after, gx, gmid, gb, xc, mine, theirs, w4, wout, wb, vec)
 
 
-def operand_grads_kernel(left_ref, right_ref, gm_ref, gt_ref, gl_ref, gr_ref, scr, lscr, rscr):
-    g, n, _ = left_ref.shape
+def operand_grads_kernel(groups, *refs):
+    sets = [refs[groups * s:groups * (s + 1)] for s in range(4)]
+    gm_ref, gt_ref, gl_keep, gr_keep, gl_send, gr_send, scr, lscr, rscr = refs[4 * groups:]
+    g, _, n = sets[0][0].shape
+    wide = sets[2][0].shape[2]
     cols = gm_ref.shape[0]
-    wide = right_ref.shape[2]
+    rows = gl_keep.shape[0]
     gm = gm_ref[...].astype(F32).reshape(cols * g, n)
     gt = gt_ref[...].astype(F32).reshape(cols * g, n)
     for t in range(n // 128):
         scr[t, : cols * g] = gm[:, t * 128 : (t + 1) * 128]
         scr[t, cols * g :] = gt[:, t * 128 : (t + 1) * 128]
-    for e in range(g):
-        gp = jnp.concatenate([scr[t, pl.ds(e, 2 * cols, stride=g), :] for t in range(n // 128)], axis=1)
-        if wide > 2 * cols:
-            gp = jnp.concatenate([gp, jnp.zeros((wide - 2 * cols, n), F32)], axis=0)
-        gp = gp.astype(BF)
-        spread(rscr, e, n, g, nt(left_ref[e], gp))
-        spread(lscr, e, n, g, nn(right_ref[e], gp))
-    gl_ref[...] = joined(lscr).astype(BF).reshape(gl_ref.shape)
-    gr_ref[...] = joined(rscr).astype(BF).reshape(gr_ref.shape)
-
-
-def operand_grads(left, right, gmine, gtheirs):
-    half, n, _ = left.shape
-    wide = right.shape[2]
+    blank = [jnp.zeros((wide - 2 * cols, n), F32)] if wide > 2 * cols else []
+    fetch = lambda at: jnp.concatenate([scr[t, pl.ds(at, cols, stride=g), :] for t in range(n // 128)], axis=1)
+    for part, (gl_ref, gr_ref) in enumerate(((gl_keep, gr_keep), (gl_send, gr_send))):
+        for e in range(g):
+            pieces = [fetch(e), fetch(cols * g + e)]
+            gp = jnp.concatenate(pieces + blank, axis=0).astype(BF)
+            seen = gp if part == 0 else jnp.concatenate(pieces[::-1] + blank, axis=0).astype(BF)
+            left = jnp.concatenate([r[e] for r in sets[part]], axis=0)
+            right = jnp.concatenate([r[e] for r in sets[2 + part]], axis=0)
+            spread(rscr, e, rows, g, nt(left, seen))
+            spread(lscr, e, rows, g, nn(right, gp))
+        gl_ref[...] = joined(lscr).astype(BF).reshape(gl_ref.shape)
+        gr_ref[...] = joined(rscr).astype(BF).reshape(gr_ref.shape)
+
+
+def operand_grads(keep_l, recv_l, keep_r, recv_r, gmine, gtheirs):
+    half, _, n = keep_l[0].shape
+    wide = keep_r[0].shape[2]
+    rows = sum(v.shape[1] for v in keep_l)
     cols = gmine.shape[0]
     g = GROUP
+    ins = keep_l + recv_l + keep_r + recv_r
+    left = pl.BlockSpec((rows, g, n), lambda b: (0, b, 0))
+    right = pl.BlockSpec((rows, g, wide), lambda b: (0, b, 0))
     return pl.pallas_call(
-        operand_grads_kernel,
+        functools.partial(operand_grads_kernel, len(keep_l)),
         grid=(half // g,),
-        in_specs=[pl.BlockSpec((g, n, n), lambda b: (b, 0, 0)), pl.BlockSpec((g, n, wide), lambda b: (b, 0, 0))]
+        in_specs=[pl.BlockSpec((g,) + v.shape[1:], lambda b: (b, 0, 0)) for v in ins]
         + [pl.BlockSpec((cols, g, n), lambda b: (0, b, 0))] * 2,
-        out_specs=[pl.BlockSpec((n, g, n), lambda b: (0, b, 0)), pl.BlockSpec((n, g, wide), lambda b: (0, b, 0))],
-        out_shape=[jax.ShapeDtypeStruct((n, half, n), BF), jax.ShapeDtypeStruct((n, half, wide), BF)],
+        out_specs=[left, right] * 2,
+        out_shape=[jax.ShapeDtypeStruct((rows, half, n), BF), jax.ShapeDtypeStruct((rows, half, wide), BF)] * 2,
         scratch_shapes=[
             pltpu.VMEM((n // 128, 2 * cols * g, 128), F32),
-            pltpu.VMEM((n // 128, n * g, 128), F32),
-            pltpu.VMEM((wide // 128, n * g, 128), F32),
+            pltpu.VMEM((n // 128, rows * g, 128), F32),
+            pltpu.VMEM((wide // 128, rows * g, 128), F32),
         ],
         compiler_params=pltpu.CompilerParams(vmem_limit_bytes=60 << 20),
         cost_estimate=cost(4 * half * n * n * wide, 8 * half * n * n),
         name="operand_grads",
-    )(left, right, gmine, gtheirs)
+    )(*ins, gmine, gtheirs)
 
 
 def tri_grads_kernel(n_ref, nc_ref, gl_ref, gr_ref, wl_ref, wr_ref, al_ref, ar_ref, lg, rg):
@@ -542,22 +585,22 @@
 
 
 def tri_grads(nrm, near, gl, gr, wl, wr):
-    n, _, c = nrm.shape
+    count, n, c = nrm.shape
     half = gl.shape[1]
     wide = near.shape[1]
-    rows = 24
+    rows = batch(count, 24)
     full = lambda v: pl.BlockSpec(v.shape, lambda b: (0,) * v.ndim)
     row = lambda a, b: pl.BlockSpec((rows, a, b), lambda k: (k, 0, 0))
     out = jax.ShapeDtypeStruct((2 * half, c), F32)
     return pl.pallas_call(
         tri_grads_kernel,
-        grid=(n // rows,),
+        grid=(count // rows,),
         in_specs=[row(n, c), row(wide, c), row(half, n), row(half, wide), full(wl), full(wr)],
         out_specs=[pl.BlockSpec(out.shape, lambda k: (0, 0))] * 2,
         out_shape=[out] * 2,
         scratch_shapes=[pltpu.VMEM((2*half, rows*n), BF), pltpu.VMEM((2*half, rows*wide), BF)],
         compiler_params=pltpu.CompilerParams(vmem_limit_bytes=56 << 20),
-        cost_estimate=cost(8 * n * n * c * c, 8 * n * n * c, n * n * half),
+        cost_estimate=cost(8 * count * n * c * c, 8 * count * n * c, count * n * half),
         name="tri_grads",
     )(nrm, near, gl, gr, wl, wr)
 
@@ -575,12 +618,32 @@
     return tri, tri_out, attn, bias, outp, expand, shr.reshape(-1, shrink.shape[2]), vec.T
 
 
-def gather_rows(pair_act, pieces):
-    rows = pair_act.shape[1] // pieces
-    return [
-        lax.all_gather(pair_act[0, m * rows : (m + 1) * rows], "pair", axis=0, tiled=True)
-        for m in range(pieces)
-    ]
+def gather_rows(rows):
+    size = lax.axis_size("pair")
+    here = lax.axis_index("pair")
+    count = rows.shape[0]
+    if size != 8 or count % 48:
+        sets = [list(range(c, size, 2)) for c in range(2)]
+        return [lax.all_gather(rows, "pair", axis=0, tiled=True, axis_index_groups=sets)], jnp.arange(
+            size // 2 * count // GROUP
+        )
+    stages = 3
+    step = count // stages
+    per = step // GROUP
+    x = [rows[s * step : (s + 1) * step] for s in range(stages)]
+    spot = lambda device, s: [device // 2 * (stages * per) + s * per + u for u in range(per)]
+    groups, places = [rows], [p for s in range(stages) for p in spot(here, s)]
+    late = []
+    for s in range(stages):
+        side, above = exchange(x[s], "pair", 2), exchange(x[s], "pair", 4)
+        if s + 1 < stages:
+            x[s + 1], side, above = lax.optimization_barrier((x[s + 1], side, above))
+        groups.append(jnp.concatenate([side, above] + late))
+        places += spot(here ^ 2, s) + spot(here ^ 4, s) + (spot(here ^ 6, s - 1) if late else [])
+        late = [exchange(side[: step // 2], "pair", 4), exchange(above[step // 2 :], "pair", 2)]
+    groups.append(jnp.concatenate(late))
+    places += spot(here ^ 6, stages - 1)
+    return groups, jnp.stack(places)
 
 
 def swap_cores(value):
@@ -657,8 +720,7 @@
     heads = bias_proj.shape[2]
     here = lax.axis_index("pair")
     core = here % 2
-    pieces = 3 if cols % (3 * GROUP) == 0 else 1
-    gathered = gather_rows(pair_act, pieces)
+    groups, places = gather_rows(pair_act[0])
     weight = gather_weights(
         tri_proj, tri_out, attention_proj, bias_proj, output_proj, expand_proj, shrink_proj, vectors
     )
@@ -670,30 +732,34 @@
     )
 
     scaled = (tri_w.astype(F32) * vec[0][:, None]).astype(BF).T
-    halves = [
-        lax.dynamic_slice_in_dim(scaled, width * s + half * core, half, 0) for s in range(4)
-    ]
-    w_left = jnp.concatenate(halves[:2])
-    w_right = jnp.concatenate(halves[2:])
+    tri_half = lambda s, c: lax.dynamic_slice_in_dim(scaled, width * s + half * c, half, 0)
+    near_w = [tri_half(s, core) for s in range(4)]
+    far_w = [tri_half(s, 1 - core) for s in range(4)]
+    w_left = jnp.concatenate([near_w[0], far_w[0], near_w[1], far_w[1]])
+    w_right = jnp.concatenate([near_w[2], near_w[3], far_w[2], far_w[3]])
     w_gate = scaled[4 * width :].T
     wout = jnp.roll(tri_out_w, -half * core, axis=0)
     gain_c = jnp.roll(vec[1], -half * core)
     vec8 = jnp.concatenate([vec[:1], gain_c[None], vec[2:], jnp.zeros((3, width), F32)])
     wb = jnp.concatenate([pairbias_w.T, jnp.zeros((16 - heads, width), BF)])
 
-    offs = jnp.stack([here * cols, (here + 1 - 2 * core) * cols]).astype(jnp.int32)
-    span = cols // pieces // GROUP
-    bufs = None
-    for m in range(pieces):
-        if pieces == 1:
-            place = lambda b: b
-        else:
-            place = lambda b, m=m: (b // span) * (span * pieces) + m * span + b % span
-        bufs = operands(offs, gathered[m], w_left, w_right, cols, place, bufs)
-    left, right, nrm, near, xc = bufs
-    mine, send = products(left, right, cols)
+    offs = jnp.concatenate(
+        [jnp.stack([here * cols, (here + 1 - 2 * core) * cols]), places]
+    ).astype(jnp.int32)
+    keep, recv, bufs, start = [], [], None, 0
+    for rows in groups:
+        mine, sent, bufs = operands(offs, rows, w_left, w_right, cols, start, tokens // 2, bufs)
+        keep.append(mine)
+        recv.append([swap_cores(v) for v in sent])
+        start += rows.shape[0]
+    nrm, near, xm, xs = bufs
+    xo = swap_cores(xs)
+    keep_l, keep_r = [v[0] for v in keep], [v[1] for v in keep]
+    recv_l, recv_r = [v[0] for v in recv], [v[1] for v in recv]
+    mine, send = products(keep_l + recv_l, keep_r + recv_r, cols)
     theirs = swap_cores(send)
-    after_c, bias_part = afters(xc, mine, theirs, w_gate, wout, wb, vec8, heads)
+    cores = jnp.full((cols,), core, jnp.int32)
+    after_c, bias_part, xc = afters(cores, xm, xo, mine, theirs, w_gate, wout, wb, vec8, heads)
     bias_full = lax.all_gather(bias_part[:, 0].astype(BF), "pair", axis=0, tiled=True)
     hidden = expand_w.shape[1] // 2
     expand_mix = (
@@ -710,16 +776,18 @@
         w_gate, wout, wb, vec8,
     )
     gtheirs = swap_cores(gsend)
-    gl, gr = operand_grads(left, right, gmine, gtheirs)
-    al, ar = tri_grads(nrm, near, gl, gr, w_left, w_right)
-
-    def halfway(part):
-        zero = jnp.zeros_like(part)
-        return [jnp.where(core == 0, part, zero), jnp.where(core == 1, part, zero)]
-
-    a_tri = jnp.concatenate(
-        halfway(al[:half]) + halfway(al[half:]) + halfway(ar[:half]) + halfway(ar[half:]) + [gw4.T]
-    ).T
+    gl, gr, gl_sent, gr_sent = operand_grads(keep_l, recv_l, keep_r, recv_r, gmine, gtheirs)
+    gl_far, gr_far = swap_cores(gl_sent), swap_cores(gr_sent)
+    w_l = [jnp.concatenate([w[0], w[1]]) for w in (near_w, far_w)]
+    w_r = [jnp.concatenate([w[2], w[3]]) for w in (near_w, far_w)]
+    near_a = tri_grads(nrm, near, gl, gr, w_l[0], w_r[0])
+    far_a = tri_grads(nrm, near, gl_far, gr_far, w_l[1], w_r[1])
+    a_tri = []
+    for near_part, far_part in zip(near_a, far_a):
+        for s in range(2):
+            parts = [p[s * half : (s + 1) * half] for p in (near_part, far_part)]
+            a_tri += [jnp.where(core == 0, parts[0], parts[1]), jnp.where(core == 0, parts[1], parts[0])]
+    a_tri = jnp.concatenate(a_tri + [gw4.T]).T
     g_read = small[0] + jnp.sum(svec[0][:, None] * shrink_w.astype(F32), axis=0)
     g_vec = jnp.stack(
         [

time: 805 us -> 789 us (0.980)
  waiting for transfers between devices: 181 us -> 119 us
  other arithmetic: 38.1 us -> 59.9 us
  starting transfers between devices: 21.3 us -> 41.5 us
  local copies, waits for them, and re-layouts: 27.7 us -> 43.5 us
    all_gather x3 -> x0, waiting for transfers between devices: 134 us -> none  [gather_rows(): lax.all_gather(pair_act[0, m * rows:(m + 1) * rows], 'pair', axis=0, tile...]
    ppermute x12 -> x24, waiting for transfers between devices: 31.4 us -> 96.8 us  [exchange(): return lax.ppermute(value, axis, [(d, d ^ bit) for d in range(size)])]
    concatenate x2 -> x10, other arithmetic: 1.24 us -> 20.3 us  [the longest x3 14.2 us: gather_rows(): groups.append(jnp.concatenate([side, above] + late))]
    ppermute x12 -> x24, starting transfers between devices: 17.4 us -> 33.8 us  [exchange(): return lax.ppermute(value, axis, [(d, d ^ bit) for d in range(size)])]
    ppermute x2 -> x15, waiting for transfers between devices: 0.81 us -> 9.14 us  [swap_cores(): return lax.ppermute(value, 'pair', [(d, d ^ 1) for d in range(size)])]
    slice x1 -> x7, local copies, waits for them, and re-layouts: 4.63 us -> 12.8 us  [the longest x3 5.13 us: gather_rows(): above[step // 2:]]
    pallas_call x6 -> x9, Pallas kernels: 190 us -> 185 us  [the longest x5 84.3 us: operands(): pl.pallas_call(functools.partial(operand_kernel, cols), grid_spec=pltpu.P...]
  transfers between devices with their start and end apart: 19 -> 41, of which waited for: 16 -> 20; matrix products, arithmetic and copies ran while one was open for 3% -> 8% of each run, Pallas kernels for 8% -> 16%
where the time goes in v4:
time: 789 us; the launch traced here: 779 us
  Pallas kernels  452 us (57%)
  waiting for transfers between devices  119 us (15%)
  other arithmetic  59.9 us (8%)
  local copies, waits for them, and re-layouts  43.5 us (6%)
  starting transfers between devices  41.5 us (5%)
  blocking collectives  39.5 us (5%)
  between operations  23.4 us (3%)
    pallas_call x1, Pallas kernels, column_pass(): pl.pallas_call(functools.partial(column_kernel, heads), grid=(cols // cb,...  202 us
    ppermute x24, waiting for transfers between devices, exchange(): return lax.ppermute(value, axis, [(d, d ^ bit) for d in range(size)])  96.8 us
    pallas_call x5, Pallas kernels, operands(): pl.pallas_call(functools.partial(operand_kernel, cols), grid_spec=pltpu.P...  84.3 us
    pallas_call x2, Pallas kernels, tri_grads(): pl.pallas_call(tri_grads_kernel, grid=(count // rows,), in_specs=[row(n,...  46.3 us
    pallas_call x1, Pallas kernels, back_pass(): pl.pallas_call(back_kernel, grid=(cols // cb,), in_specs=[col(n, c)] * 3...  43.4 us
    pallas_call x1, Pallas kernels, operand_grads(): pl.pallas_call(functools.partial(operand_grads_kernel, len(keep_l)), grid...  40.7 us
    ppermute x24, starting transfers between devices, exchange(): return lax.ppermute(value, axis, [(d, d ^ bit) for d in range(size)])  33.8 us
    pallas_call x1, Pallas kernels, afters(): pl.pallas_call(functools.partial(after_kernel, heads), grid=(cols // cb,)...  21.9 us
  transfers between devices with their start and end apart: 41, of which 20 were waited for; matrix products, arithmetic and copies ran while one was open for 8% of the time, Pallas kernels for 16%

profile of v4, /device:TPU:0, one launch (start us, length us, event | category | flops | bytes accessed | tf_op | source)
XLA Modules:
  0.0 779.3 jit_solution(1973532199537640466)
XLA Ops:
  7.3 4.6 slice_bitcast_fusion
  16.7 32.7 %collective-permute-done = bf16[16,384,128]{2,1,0:T(8,128)(2,1)} collective-permute-done((bf16[16,384,128]{2,1,0:T(8,128)(2,1)S(1)}, bf16[16,384,128]{2,1,0:T(8,128)(2,1)}, u32[]{:S(2)}, u32[]{:S(2)}) %collective-permute-start) | collective-permute-done | bytes 1572896 | tf_op jit(solution)/shard_map/ppermute | solution.py:656
  53.7 19.3 %all_gather.6 = bf16[128,2953]{1,0:T(8,128)(2,1)S(1)} all-gather(bf16[32,2953]{1,0:T(8,128)(2,1)S(1)} %concatenate.64), channel_id=1, replica_groups=mesh['item'=4,'pair'=8] {'item'}, dimensions={0}, use_global_device_ids=true | all-gather | bytes 944960 | tf_op jit(solution)/shard_map/all_gather | solution.py:612
  77.1 11.2 %collective-permute-done.2 = bf16[16,384,128]{2,1,0:T(8,128)(2,1)S(1)} collective-permute-done((bf16[16,384,128]{2,1,0:T(8,128)(2,1)}, bf16[16,384,128]{2,1,0:T(8,128)(2,1)S(1)}, u32[]{:S(2)}, u32[]{:S(2)}) %collective-permute-start.2) | collective-permute-done | bytes 1572896 | tf_op jit(solution)/shard_map/ppermute | solution.py:656
  95.0 20.0 %operands.5 = (bf16[64,48,384]{2,1,0:T(8,128)(2,1)}, bf16[64,48,128]{2,1,0:T(8,128)(2,1)}, bf16[64,48,384]{2,1,0:T(8,128)(2,1)}, bf16[64,48,128]{2,1,0:T(8,128)(...) custom-call(s32[14]{0:T(128)} %concatenate.62.off_ref, ...), custom_call_target="tpu_custom_call" | custom-call | flops 2415919104 | bytes 18874368 | tf_op jit(solution)/shard_map/operands/pallas_call | solution.py:318
  125.0 14.7 %operands.6 = (bf16[64,32,384]{2,1,0:T(8,128)(2,1)}, bf16[64,32,128]{2,1,0:T(8,128)(2,1)}, bf16[64,32,384]{2,1,0:T(8,128)(2,1)}, bf16[64,32,128]{2,1,0:T(8,128)(...) custom-call(s32[14]{0:T(128)} %concatenate.62.off_ref, ...), custom_call_target="tpu_custom_call", output_to_operand_aliasing={{4}: (4, {}), {5}: (5, {}), {6}: (6, {}), {7}: (7, {})} | custom-call | flops 1610612736 | bytes 12582912 | tf_op jit(solution)/shard_map/operands/pallas_call | solution.py:318
  142.9 5.5 pad_maximum_fusion.1.x_ref
  148.9 20.2 %operands.7 = (bf16[64,48,384]{2,1,0:T(8,128)(2,1)}, bf16[64,48,128]{2,1,0:T(8,128)(2,1)}, bf16[64,48,384]{2,1,0:T(8,128)(2,1)}, bf16[64,48,128]{2,1,0:T(8,128)(...) custom-call(s32[14]{0:T(128)} %concatenate.62.off_ref, ...), custom_call_target="tpu_custom_call", output_to_operand_aliasing={{4}: (4, {}), {5}: (5, {}), {6}: (6, {}), {7}: (7, {})} | custom-call | flops 2415919104 | bytes 18874368 | tf_op jit(solution)/shard_map/operands/pallas_call | solution.py:318
  172.1 4.8 pad_maximum_fusion.x_ref
  176.9 20.3 %operands.8 = (bf16[64,48,384]{2,1,0:T(8,128)(2,1)}, bf16[64,48,128]{2,1,0:T(8,128)(2,1)}, bf16[64,48,384]{2,1,0:T(8,128)(2,1)}, bf16[64,48,128]{2,1,0:T(8,128)(...) custom-call(s32[14]{0:T(128)} %concatenate.62.off_ref, ...), custom_call_target="tpu_custom_call", output_to_operand_aliasing={{4}: (4, {}), {5}: (5, {}), {6}: (6, {}), {7}: (7, {})} | custom-call | flops 2415919104 | bytes 18874368 | tf_op jit(solution)/shard_map/operands/pallas_call | solution.py:318
  199.6 17.8 %collective-permute-done.5 = bf16[8,384,128]{2,1,0:T(8,128)(2,1)S(1)} collective-permute-done((bf16[8,384,128]{2,1,0:T(8,128)(2,1)S(1)}, bf16[8,384,128]{2,1,0:T(8,128)(2,1)S(1)}, u32[]{:S(2)}, u32[]{:S(2)}) %collective-permute-start.5) | collective-permute-done | bytes 786464 | tf_op jit(solution)/shard_map/ppermute | solution.py:656
  219.9 9.1 %operands.9 = (bf16[64,16,384]{2,1,0:T(8,128)(2,1)}, bf16[64,16,128]{2,1,0:T(8,128)(2,1)}, bf16[64,16,384]{2,1,0:T(8,128)(2,1)}, bf16[64,16,128]{2,1,0:T(8,128)(...) custom-call(s32[14]{0:T(128)} %concatenate.62.off_ref, ...), custom_call_target="tpu_custom_call", output_to_operand_aliasing={{4}: (4, {}), {5}: (5, {}), {6}: (6, {}), {7}: (7, {})} | custom-call | flops 805306368 | bytes 6291456 | tf_op jit(solution)/shard_map/operands/pallas_call | solution.py:318
  235.6 13.5 %products.1 = (bf16[48,64,384]{2,1,0:T(8,128)(2,1)}, bf16[48,64,384]{2,1,0:T(8,128)(2,1)}) custom-call(bf16[64,48,384]{2,1,0:T(8,128)(2,1)} %get-tuple-element.126.refs_0_, bf16[64,32,384]{2,1,0:T(8,128)(2,1)} %get-tuple-element.127.refs_1_, bf16[64,48,384]{2,1,0:T(8,128)(2,1)} %get-tuple-element.128.refs_2_, ...), custom_call_target="tpu_custom_call" | custom-call | flops 2415919104 | bytes 37748736 | tf_op jit(solution)/shard_map/products/pallas_call | solution.py:364
  256.6 21.9 %afters.1 = (f32[48,384,128]{2,1,0:T(8,128)}, f32[48,1,1536]{2,1,0:T(1,128)}, bf16[48,384,128]{2,1,0:T(8,128)(2,1)}) custom-call(s32[48]{0:T(128)} %broadcast_in_dim.8.core_ref, bf16[48,192,128]{2,1,0:T(8,128)(2,1)} %get-tuple-element.124.xm_ref, bf16[48,192,128]{2,1,0:T(8,128)(2,1)} %collective-permute-done.12.xo_ref, ...), custom_call_target="tpu_custom_call" | custom-call | flops 2415919104 | bytes 23592960 | tf_op jit(solution)/shard_map/afters/pallas_call | solution.py:424
  295.6 10.3 %all-gather.3.cloned.1.call-done = bf16[384,1,1536]{2,0,1:T(8,128)(2,1)} async-done(((bf16[48,1,1536]{2,0,1:T(8,128)(2,1)}), bf16[384,1,1536]{2,0,1:T(8,128)(2,1)}) %all-gather.3.cloned.1.call-update) | async-done | bytes 1179664 | tf_op jit(solution)/shard_map/all_gather | solution.py:763
  305.9 202.1 %columns.1 = (f32[48,384,128]{2,1,0:T(8,128)}, f32[48,384,128]{2,1,0:T(8,128)}, bf16[384,1536]{1,0:T(8,128)(2,1)}, f32[128,256]{1,0:T(8,128)}, f32[256,128]{1,0:...) custom-call(f32[48,384,128]{2,1,0:T(8,128)} %get-tuple-element.148.after_ref, ...), custom_call_target="tpu_custom_call" | custom-call | flops 43486543872 | bytes 37748736 | tf_op jit(solution)/shard_map/columns/pallas_call | solution.py:214
  508.0 20.2 %all_to_all.24 = bf16[8,48,1536]{2,1,0:T(8,128)(2,1)S(1)} all-to-all(bf16[8,48,1536]{2,1,0:T(8,128)(2,1)} %bitcast.153), channel_id=1, replica_groups=mesh['item'=4,'pair'=8] {'pair'}, dimensions={0} | all-to-all | bytes 2359296 | tf_op jit(solution)/shard_map/all_to_all | solution.py:772
  529.5 43.4 %back.1 = (bf16[48,64,384]{2,1,0:T(8,128)(2,1)}, bf16[48,64,384]{2,1,0:T(8,128)(2,1)}, f32[16,128]{1,0:T(8,128)}, f32[128,128]{1,0:T(8,128)}, f32[128,128]{1,0:T(8,128)}, /*index=5*/f32[8,128]{1,0:T(8,128)}) custom-call(f32[48,384,128]{2,1,0:T(8,128)} %get-tuple-element.148.after_ref, f32[48,384,128]{2,1,0:T(8,128)} %get-tuple-element.157.gx_ref, ...), custom_call_target="tpu_custom_call" | custom-call | flops 4831838208 | bytes 56623104 | tf_op jit(solution)/shard_map/back/pallas_call | solution.py:495
  573.0 4.7 collective-permute-done.29.refs_21_
  579.2 40.7 %operand_grads.1 = (bf16[192,64,384]{2,1,0:T(8,128)(2,1)}, bf16[192,64,128]{2,1,0:T(8,128)(2,1)}, bf16[192,64,384]{2,1,0:T(8,128)(2,1)}, bf16[192,64,128]{2,1,0:T(8,128)(2,1)}) custom-call(bf16[64,48,384]{2,1,0:T(8,128)(2,1)} %get-tuple-element.126.refs_0_, bf16[64,32,384]{2,1,0:T(8,128)(2,1)} %get-tuple-element.127.refs_1_, ...), custom_call_target="tpu_custom_call" | custom-call | flops 4831838208 | bytes 75497472 | tf_op jit(solution)/shard_map/operand_grads/pallas_call | solution.py:545
  633.7 23.3 %tri_grads.2 = (f32[128,128]{1,0:T(8,128)}, f32[128,128]{1,0:T(8,128)}) custom-call(bf16[192,384,128]{2,1,0:T(8,128)(2,1)} %get-tuple-element.155.n_ref, bf16[192,128,128]{2,1,0:T(8,128)(2,1)} %get-tuple-element.156.nc_ref, bf16[192,64,384]{2,1,0:T(8,128)(2,1)} %get-tuple-element.163.gl_ref, bf16[192,64,128]{2,1,0:T(8,128)(2,1)} %get-tuple-element.164.gr_ref, ...), custom_call_target="tpu_custom_call" | custom-call | flops 9663676416 | bytes 75497472 | tf_op jit(solution)/shard_map/tri_grads/pallas_call | solution.py:595
  658.6 23.0 %tri_grads.3 = (f32[128,128]{1,0:T(8,128)}, f32[128,128]{1,0:T(8,128)}) custom-call(bf16[192,384,128]{2,1,0:T(8,128)(2,1)} %get-tuple-element.155.n_ref, bf16[192,128,128]{2,1,0:T(8,128)(2,1)} %get-tuple-element.156.nc_ref, bf16[192,64,384]{2,1,0:T(8,128)(2,1)} %collective-permute-done.30.gl_ref, bf16[192,64,128]{2,1,0:T(8,128)(2,1)} %copy-done.6, ...), custom_call_target="tpu_custom_call" | custom-call | flops 9663676416 | bytes 75497472 | tf_op jit(solution)/shard_map/tri_grads/pallas_call | solution.py:595
  691.3 15.2 %collective-permute-done.32 = bf16[64,2445]{1,0:T(8,128)(2,1)S(1)} collective-permute-done((bf16[64,2445]{1,0:T(8,128)(2,1)S(1)}, bf16[64,2445]{1,0:T(8,128)(2,1)S(1)}, u32[]{:S(2)}, u32[]{:S(2)}) %collective-permute-start.32) | collective-permute-done | bytes 312992 | tf_op jit(solution)/shard_map/ppermute | solution.py:656
  707.2 4.8 collective-permute-done.33
  (369 shorter events, 152.3 us)
Async XLA Ops:
  7.3 298.6 %all-gather.3.cloned.1.call-start = ((), (), s32[]{:S(2)}) async-start(), calls=%async_computation.2 | async-start | bytes 1327104 | tf_op jit(solution)/shard_map/all_gather | solution.py:763
  11.9 37.4 %collective-permute-start = (bf16[16,384,128]{2,1,0:T(8,128)(2,1)S(1)}, bf16[16,384,128]{2,1,0:T(8,128)(2,1)}, u32[]{:S(2)}, u32[]{:S(2)}) collective-permute-start(bf16[16,384,128]{2,1,0:T(8,128)(2,1)S(1)} %get-tuple-element.364), channel_id=1, source_target_pairs={{0,2},{1,3},{2,0},{3,1},{4,6},{5,7},{6,4},{7,5},{8,10},{9,11},{10,... | collective-permute-start | bytes 4718600 | tf_op jit(solution)/shard_map/ppermute | solution.py:656
  14.9 35.9 %collective-permute-start.1 = (bf16[16,384,128]{2,1,0:T(8,128)(2,1)S(1)}, bf16[16,384,128]{2,1,0:T(8,128)(2,1)S(1)}, u32[]{:S(2)}, u32[]{:S(2)}) collective-permute-start(bf16[16,384,128]{2,1,0:T(8,128)(2,1)S(1)} %get-tuple-element.364), channel_id=1, source_target_pairs={{0,4},{1,5},{2,6},{3,7},{4,0},{5,1},{6,2},{7,3},{8,12},{9,13},{10,... | collective-permute-start | bytes 4718600 | tf_op jit(solution)/shard_map/ppermute | solution.py:656
  50.7 37.5 %collective-permute-start.2 = (bf16[16,384,128]{2,1,0:T(8,128)(2,1)}, bf16[16,384,128]{2,1,0:T(8,128)(2,1)S(1)}, u32[]{:S(2)}, u32[]{:S(2)}) collective-permute-start(bf16[16,384,128]{2,1,0:T(8,128)(2,1)} %get-tuple-element.102), channel_id=1, source_target_pairs={{0,2},{1,3},{2,0},{3,1},{4,6},{5,7},{6,4},{7,5},{8,10},{9,11},{10,... | collective-permute-start | bytes 4718600 | tf_op jit(solution)/shard_map/ppermute | solution.py:656
  51.1 37.2 %collective-permute-start.3 = (bf16[16,384,128]{2,1,0:T(8,128)(2,1)}, bf16[16,384,128]{2,1,0:T(8,128)(2,1)}, u32[]{:S(2)}, u32[]{:S(2)}) collective-permute-start(bf16[16,384,128]{2,1,0:T(8,128)(2,1)} %get-tuple-element.102), channel_id=1, source_target_pairs={{0,4},{1,5},{2,6},{3,7},{4,0},{5,1},{6,2},{7,3},{8,12},{9,13},{10,... | collective-permute-start | bytes 4718600 | tf_op jit(solution)/shard_map/ppermute | solution.py:656
  75.7 47.8 %collective-permute-start.11 = (bf16[8,384,128]{2,1,0:T(8,128)(2,1)}, bf16[8,384,128]{2,1,0:T(8,128)(2,1)}, u32[]{:S(2)}, u32[]{:S(2)}) collective-permute-start(bf16[8,384,128]{2,1,0:T(8,128)(2,1)} %slice.196), channel_id=1, source_target_pairs={{0,2},{1,3},{2,0},{3,1},{4,6},{5,7},{6,4},{7,5},{8,10},{9,11},{10,... | collective-permute-start | bytes 2359304 | tf_op jit(solution)/shard_map/ppermute | solution.py:656
  88.3 60.1 %collective-permute-start.6 = (bf16[16,384,128]{2,1,0:T(8,128)(2,1)}, bf16[16,384,128]{2,1,0:T(8,128)(2,1)}, u32[]{:S(2)}, u32[]{:S(2)}) collective-permute-start(bf16[16,384,128]{2,1,0:T(8,128)(2,1)} %get-tuple-element.103), channel_id=1, source_target_pairs={{0,4},{1,5},{2,6},{3,7},{4,0},{5,1},{6,2},{7,3},{8,12},{9,13},{10,... | collective-permute-start | bytes 4718600 | tf_op jit(solution)/shard_map/ppermute | solution.py:656
  89.9 81.9 %collective-permute-start.4 = (bf16[16,384,128]{2,1,0:T(8,128)(2,1)}, bf16[16,384,128]{2,1,0:T(8,128)(2,1)S(1)}, u32[]{:S(2)}, u32[]{:S(2)}) collective-permute-start(bf16[16,384,128]{2,1,0:T(8,128)(2,1)} %get-tuple-element.103), channel_id=1, source_target_pairs={{0,2},{1,3},{2,0},{3,1},{4,6},{5,7},{6,4},{7,5},{8,10},{9,11},{10,... | collective-permute-start | bytes 4718600 | tf_op jit(solution)/shard_map/ppermute | solution.py:656
  93.3 49.5 %collective-permute-start.10 = (bf16[8,384,128]{2,1,0:T(8,128)(2,1)}, bf16[8,384,128]{2,1,0:T(8,128)(2,1)}, u32[]{:S(2)}, u32[]{:S(2)}) collective-permute-start(bf16[8,384,128]{2,1,0:T(8,128)(2,1)} %slice.195), channel_id=1, source_target_pairs={{0,4},{1,5},{2,6},{3,7},{4,0},{5,1},{6,2},{7,3},{8,12},{9,13},{10,... | collective-permute-start | bytes 2359304 | tf_op jit(solution)/shard_map/ppermute | solution.py:656
  120.8 50.4 %collective-permute-start.9 = (bf16[8,384,128]{2,1,0:T(8,128)(2,1)}, bf16[8,384,128]{2,1,0:T(8,128)(2,1)}, u32[]{:S(2)}, u32[]{:S(2)}) collective-permute-start(bf16[8,384,128]{2,1,0:T(8,128)(2,1)} %slice.194), channel_id=1, source_target_pairs={{0,2},{1,3},{2,0},{3,1},{4,6},{5,7},{6,4},{7,5},{8,10},{9,11},{10,... | collective-permute-start | bytes 2359304 | tf_op jit(solution)/shard_map/ppermute | solution.py:656
  123.4 47.8 %collective-permute-start.8 = (bf16[8,384,128]{2,1,0:T(8,128)(2,1)}, bf16[8,384,128]{2,1,0:T(8,128)(2,1)}, u32[]{:S(2)}, u32[]{:S(2)}) collective-permute-start(bf16[8,384,128]{2,1,0:T(8,128)(2,1)} %slice.193), channel_id=1, source_target_pairs={{0,4},{1,5},{2,6},{3,7},{4,0},{5,1},{6,2},{7,3},{8,12},{9,13},{10,... | collective-permute-start | bytes 2359304 | tf_op jit(solution)/shard_map/ppermute | solution.py:656
  142.8 86.2 %collective-permute-start.13 = (bf16[64,48,384]{2,1,0:T(8,128)(2,1)}, bf16[64,48,384]{2,1,0:T(8,128)(2,1)S(1)}, u32[]{:S(2)}, u32[]{:S(2)}) collective-permute-start(bf16[64,48,384]{2,1,0:T(8,128)(2,1)} %get-tuple-element.131), channel_id=1, source_target_pairs={{0,1},{1,0},{2,3},{3,2},{4,5},{5,4},{6,7},{7,6},{8,9},{9,8},{10,11... | collective-permute-start | bytes 7077896 | tf_op jit(solution)/shard_map/ppermute | solution.py:651
  148.4 48.8 %collective-permute-start.18 = (bf16[64,48,128]{2,1,0:T(8,128)(2,1)}, bf16[64,48,128]{2,1,0:T(8,128)(2,1)}, u32[]{:S(2)}, u32[]{:S(2)}) collective-permute-start(bf16[64,48,128]{2,1,0:T(8,128)(2,1)} %get-tuple-element.141), channel_id=1, source_target_pairs={{0,1},{1,0},{2,3},{3,2},{4,5},{5,4},{6,7},{7,6},{8,9},{9,8},{10,11... | collective-permute-start | bytes 2359304 | tf_op jit(solution)/shard_map/ppermute | solution.py:651
  171.2 26.1 %collective-permute-start.19 = (bf16[64,32,128]{2,1,0:T(8,128)(2,1)}, bf16[64,32,128]{2,1,0:T(8,128)(2,1)}, u32[]{:S(2)}, u32[]{:S(2)}) collective-permute-start(bf16[64,32,128]{2,1,0:T(8,128)(2,1)} %get-tuple-element.142), channel_id=1, source_target_pairs={{0,1},{1,0},{2,3},{3,2},{4,5},{5,4},{6,7},{7,6},{8,9},{9,8},{10,11... | collective-permute-start | bytes 1572872 | tf_op jit(solution)/shard_map/ppermute | solution.py:651
  171.3 58.9 %collective-permute-start.15 = (bf16[64,48,384]{2,1,0:T(8,128)(2,1)}, bf16[64,48,384]{2,1,0:T(8,128)(2,1)}, u32[]{:S(2)}, u32[]{:S(2)}) collective-permute-start(bf16[64,48,384]{2,1,0:T(8,128)(2,1)} %get-tuple-element.133), channel_id=1, source_target_pairs={{0,1},{1,0},{2,3},{3,2},{4,5},{5,4},{6,7},{7,6},{8,9},{9,8},{10,11... | collective-permute-start | bytes 7077896 | tf_op jit(solution)/shard_map/ppermute | solution.py:651
  171.8 26.1 %collective-permute-start.7 = (bf16[8,384,128]{2,1,0:T(8,128)(2,1)}, bf16[8,384,128]{2,1,0:T(8,128)(2,1)}, u32[]{:S(2)}, u32[]{:S(2)}) collective-permute-start(bf16[8,384,128]{2,1,0:T(8,128)(2,1)} %slice.236), channel_id=1, source_target_pairs={{0,2},{1,3},{2,0},{3,1},{4,6},{5,7},{6,4},{7,5},{8,10},{9,11},{10,... | collective-permute-start | bytes 2359304 | tf_op jit(solution)/shard_map/ppermute | solution.py:656
  197.2 32.4 %collective-permute-start.14 = (bf16[64,32,384]{2,1,0:T(8,128)(2,1)}, bf16[64,32,384]{2,1,0:T(8,128)(2,1)}, u32[]{:S(2)}, u32[]{:S(2)}) collective-permute-start(bf16[64,32,384]{2,1,0:T(8,128)(2,1)} %get-tuple-element.132), channel_id=1, source_target_pairs={{0,1},{1,0},{2,3},{3,2},{4,5},{5,4},{6,7},{7,6},{8,9},{9,8},{10,11... | collective-permute-start | bytes 4718600 | tf_op jit(solution)/shard_map/ppermute | solution.py:651
  197.3 37.3 %collective-permute-start.16 = (bf16[64,48,384]{2,1,0:T(8,128)(2,1)}, bf16[64,48,384]{2,1,0:T(8,128)(2,1)}, u32[]{:S(2)}, u32[]{:S(2)}) collective-permute-start(bf16[64,48,384]{2,1,0:T(8,128)(2,1)} %get-tuple-element.134), channel_id=1, source_target_pairs={{0,1},{1,0},{2,3},{3,2},{4,5},{5,4},{6,7},{7,6},{8,9},{9,8},{10,11... | collective-permute-start | bytes 7077896 | tf_op jit(solution)/shard_map/ppermute | solution.py:651
  197.9 19.6 %collective-permute-start.5 = (bf16[8,384,128]{2,1,0:T(8,128)(2,1)S(1)}, bf16[8,384,128]{2,1,0:T(8,128)(2,1)S(1)}, u32[]{:S(2)}, u32[]{:S(2)}) collective-permute-start(bf16[8,384,128]{2,1,0:T(8,128)(2,1)S(1)} %slice.235), channel_id=1, source_target_pairs={{0,4},{1,5},{2,6},{3,7},{4,0},{5,1},{6,2},{7,3},{8,12},{9,13},{10,... | collective-permute-start | bytes 2359304 | tf_op jit(solution)/shard_map/ppermute | solution.py:656
  217.5 12.2 %collective-permute-start.20 = (bf16[64,48,128]{2,1,0:T(8,128)(2,1)}, bf16[64,48,128]{2,1,0:T(8,128)(2,1)S(1)}, u32[]{:S(2)}, u32[]{:S(2)}) collective-permute-start(bf16[64,48,128]{2,1,0:T(8,128)(2,1)} %get-tuple-element.143), channel_id=1, source_target_pairs={{0,1},{1,0},{2,3},{3,2},{4,5},{5,4},{6,7},{7,6},{8,9},{9,8},{10,11... | collective-permute-start | bytes 2359304 | tf_op jit(solution)/shard_map/ppermute | solution.py:651
  230.1 25.0 %collective-permute-start.12 = (bf16[48,192,128]{2,1,0:T(8,128)(2,1)}, bf16[48,192,128]{2,1,0:T(8,128)(2,1)}, u32[]{:S(2)}, u32[]{:S(2)}) collective-permute-start(bf16[48,192,128]{2,1,0:T(8,128)(2,1)} %get-tuple-element.125), channel_id=1, source_target_pairs={{0,1},{1,0},{2,3},{3,2},{4,5},{5,4},{6,7},{7,6},{8,9},{9,8},{10,11... | collective-permute-start | bytes 7077896 | tf_op jit(solution)/shard_map/ppermute | solution.py:651
  619.8 37.2 %collective-permute-start.30 = (bf16[192,64,384]{2,1,0:T(8,128)(2,1)}, bf16[192,64,384]{2,1,0:T(8,128)(2,1)}, u32[]{:S(2)}, u32[]{:S(2)}) collective-permute-start(bf16[192,64,384]{2,1,0:T(8,128)(2,1)} %get-tuple-element.166), channel_id=1, source_target_pairs={{0,1},{1,0},{2,3},{3,2},{4,5},{5,4},{6,7},{7,6},{8,9},{9,8},{10,11... | collective-permute-start | bytes 28311560 | tf_op jit(solution)/shard_map/ppermute | solution.py:651
  620.0 36.9 %collective-permute-start.31 = (bf16[192,64,128]{2,1,0:T(8,128)(2,1)}, bf16[192,64,128]{2,1,0:T(8,128)(2,1)S(1)}, u32[]{:S(2)}, u32[]{:S(2)}) collective-permute-start(bf16[192,64,128]{2,1,0:T(8,128)(2,1)} %get-tuple-element.167), channel_id=1, source_target_pairs={{0,1},{1,0},{2,3},{3,2},{4,5},{5,4},{6,7},{7,6},{8,9},{9,8},{10,11... | collective-permute-start | bytes 9437192 | tf_op jit(solution)/shard_map/ppermute | solution.py:651
  688.8 17.7 %collective-permute-start.32 = (bf16[64,2445]{1,0:T(8,128)(2,1)S(1)}, bf16[64,2445]{1,0:T(8,128)(2,1)S(1)}, u32[]{:S(2)}, u32[]{:S(2)}) collective-permute-start(bf16[64,2445]{1,0:T(8,128)(2,1)S(1)} %dynamic-slice_convert_fusion), channel_id=1, source_target_pairs={{0,16},{8,24},{16,0},{24,8},{1,17},{9,25},{17,1},{25,9},{2,18},{10... | collective-permute-start | bytes 938888 | tf_op jit(solution)/shard_map/ppermute | solution.py:656
  (95 other events, 2229.2 us)
Sparse Core Ops, SparseCore 0:
  280.4 25.4 all-gather.2

commit v5 on v4

--- a/solution.py
+++ b/solution.py
@@ -116,17 +116,17 @@
     t = (n4 * g4).astype(BF)
     f = we_ref.shape[1] // 2
     racc = mid * wr
-    for q in range(f // 128):
-        u = nn(t, we_ref[:, q * 256:(q + 1) * 256])
-        a, b = u[:, :128], u[:, 128:]
-        zc = z_ref[:, q * 128:(q + 1) * 128]
-        sig = sigm(a)
-        silu = a * sig
-        h_low = (silu * b).astype(BF)
-        hv[:, q * 128:(q + 1) * 128] = h_low
-        racc += h_low.astype(F32) * zc
-        cu[:, q * 256:q * 256 + 128] = (zc * b * (sig + silu - silu * sig)).astype(BF)
-        cu[:, q * 256 + 128:(q + 1) * 256] = (zc * silu).astype(BF)
+    u = nn(t, we_ref[...])
+    a, b = u[:, :f], u[:, f:]
+    sig = sigm(a)
+    silu = a * sig
+    h_low = (silu * b).astype(BF)
+    hv[...] = h_low
+    part = h_low.astype(F32) * z_ref[...]
+    for q in range(f // c):
+        racc += part[:, q * c:(q + 1) * c]
+    cu[:, :f] = (z_ref[...] * b * (sig + silu - silu * sig)).astype(BF)
+    cu[:, f:] = (z_ref[...] * silu).astype(BF)
     readout = jnp.sum(racc, axis=-1, keepdims=True)
     spot = lax.broadcasted_iota(jnp.int32, tgt_ref.shape, 1)
     pick = lambda ref: jnp.concatenate(
@@ -256,7 +256,7 @@
 
 
 def operand_kernel(cols, off_ref, x_ref, wl_ref, wr_ref, *refs):
-    keep_l, keep_r, send_l, send_r, n_ref, nc_ref, xc_ref, xs_ref, lscr, rscr, nscr, xscr, cscr = refs[-13:]
+    keep_ref, send_ref, n_ref, nc_ref, xc_ref, xs_ref, lscr, rscr, nscr, xscr, cscr = refs[-11:]
     rows, n, c = x_ref.shape
     wide = nc_ref.shape[1]
     half = c // 2
@@ -283,10 +283,10 @@
         spread(rscr, half * rows + k, half, rows, p[:half] * sigm(p[half:]))
         cscr[pl.ds(k, cols, stride=rows), :] = xscr[k, pl.ds(own, cols), :]
         cscr[pl.ds(cols * rows + k, cols, stride=rows), :] = xscr[k, pl.ds(other, cols), :]
-    for scr, keep, send in ((lscr, keep_l, send_l), (rscr, keep_r, send_r)):
-        cut = half * rows
-        keep[...] = joined(scr, slice(0, cut)).astype(BF).reshape(keep.shape)
-        send[...] = joined(scr, slice(cut, None)).astype(BF).reshape(send.shape)
+    cut = half * rows
+    for ref, span in ((keep_ref, slice(0, cut)), (send_ref, slice(cut, None))):
+        both = jnp.concatenate([joined(lscr, span), joined(rscr, span)], axis=1)
+        ref[...] = both.astype(BF).reshape(ref.shape)
     xc_ref[...] = cscr[:cols * rows].astype(BF).reshape(xc_ref.shape)
     xs_ref[...] = cscr[cols * rows:].astype(BF).reshape(xs_ref.shape)
 
@@ -298,21 +298,19 @@
     g = GROUP
     at = start // g
     shapes = [
-        ((half, count, n), (half, g, n), lambda b, o: (0, b, 0)),
-        ((half, count, wide), (half, g, wide), lambda b, o: (0, b, 0)),
-        ((half, count, n), (half, g, n), lambda b, o: (0, b, 0)),
-        ((half, count, wide), (half, g, wide), lambda b, o: (0, b, 0)),
+        ((half, count, n + wide), (half, g, n + wide), lambda b, o: (0, b, 0)),
+        ((half, count, n + wide), (half, g, n + wide), lambda b, o: (0, b, 0)),
         ((total, n, c), (g, n, c), lambda b, o: (at + b, 0, 0)),
         ((total, wide, c), (g, wide, c), lambda b, o: (at + b, 0, 0)),
-        ((cols, total, c), (cols, g, c), lambda b, o: (0, o[2 + at + b], 0)),
-        ((cols, total, c), (cols, g, c), lambda b, o: (0, o[2 + at + b], 0)),
+        ((cols, total, c), (cols, g, c), lambda b, o: (0, o[2 + b], 0)),
+        ((cols, total, c), (cols, g, c), lambda b, o: (0, o[2 + b], 0)),
     ]
     full = lambda v: pl.BlockSpec(v.shape, lambda b, o: (0,) * v.ndim)
     ins = [x, wl, wr]
     specs = [pl.BlockSpec((g, n, c), lambda b, o: (b, 0, 0)), full(wl), full(wr)]
     alias = {}
     if bufs is not None:
-        alias = {4 + i: 4 + i for i in range(4)}
+        alias = {4 + i: 2 + i for i in range(4)}
         ins += list(bufs)
         specs += [pl.BlockSpec(memory_space=pl.ANY)] * 4
     got = pl.pallas_call(
@@ -333,45 +331,42 @@
         out_shape=[jax.ShapeDtypeStruct(s, BF) for s, _, _ in shapes],
         input_output_aliases=alias,
         compiler_params=pltpu.CompilerParams(vmem_limit_bytes=60 << 20),
-        cost_estimate=cost(8 * count * n * c * c, 8 * count * n * c, count * n * c),
+        cost_estimate=cost(3e9 * count, 8 * count * n * c),
         name="operands",
     )(offs, *ins)
-    return got[:2], got[2:4], got[4:]
+    return got[0], got[1], got[2:]
 
 
 def product_kernel(groups, *refs):
-    lefts, rights = refs[:groups], refs[groups:2 * groups]
-    mine_ref, theirs_ref, scr = refs[2 * groups:]
-    g = lefts[0].shape[0]
-    cols = mine_ref.shape[0]
+    mine_ref, theirs_ref, scr = refs[groups:]
+    g = refs[0].shape[0]
+    cols, _, n = mine_ref.shape
     for e in range(g):
+        both = jnp.concatenate([r[e] for r in refs[:groups]], axis=0)
         part = lax.dot_general(
-            jnp.concatenate([r[e] for r in rights], axis=0),
-            jnp.concatenate([r[e] for r in lefts], axis=0),
-            (((0,), (0,)), ((), ())),
-            preferred_element_type=F32,
+            both[:, n:], both[:, :n], (((0,), (0,)), ((), ())), preferred_element_type=F32
         )
         spread(scr, e, 2 * cols, g, part[: 2 * cols])
     mine_ref[...] = joined(scr, slice(0, cols * g)).astype(mine_ref.dtype).reshape(mine_ref.shape)
     theirs_ref[...] = joined(scr, slice(cols * g, None)).astype(theirs_ref.dtype).reshape(theirs_ref.shape)
 
 
-def products(lefts, rights, cols):
-    half, _, n = lefts[0].shape
-    wide = rights[0].shape[2]
+def products(sets, cols, n):
+    half, _, wide = sets[0].shape
+    wide -= n
     g = GROUP
     out = jax.ShapeDtypeStruct((cols, half, n), BF)
     return pl.pallas_call(
-        functools.partial(product_kernel, len(lefts)),
+        functools.partial(product_kernel, len(sets)),
         grid=(half // g,),
-        in_specs=[pl.BlockSpec((g,) + v.shape[1:], lambda b: (b, 0, 0)) for v in lefts + rights],
+        in_specs=[pl.BlockSpec((g,) + v.shape[1:], lambda b: (b, 0, 0)) for v in sets],
         out_specs=[pl.BlockSpec((cols, g, n), lambda b: (0, b, 0))] * 2,
         out_shape=[out, out],
         scratch_shapes=[pltpu.VMEM((n // 128, 2 * cols * g, 128), F32)],
         compiler_params=pltpu.CompilerParams(vmem_limit_bytes=56 << 20),
         cost_estimate=cost(2 * half * n * n * wide, 4 * half * n * n),
         name="products",
-    )(*lefts, *rights)
+    )(*sets)
 
 
 def batch(count, most):
@@ -389,7 +384,7 @@
 
 
 def after_kernel(heads, core_ref, xm_ref, xo_ref, mine_ref, theirs_ref, w4_ref, wout_ref, wb_ref, vec_ref,
-                 after_ref, bias_ref, xc_ref):
+                 after_ref, bias_ref, xc_ref, bscr):
     cb, n, c = xc_ref.shape
     first = core_ref[0] == 0
     span = core_ref.shape[0]
@@ -411,7 +406,12 @@
     bias = nt(wb_ref[...], (n3 * vec_ref[2:3, :]).astype(BF))
     for b in range(cb):
         for h in range(heads):
-            bias_ref[b, :, h * n:(h + 1) * n] = bias[h:h + 1, b * n:(b + 1) * n]
+            at = pl.program_id(0) * cb + b
+            bscr[pl.ds(at, 1), h * n:(h + 1) * n] = bias[h:h + 1, b * n:(b + 1) * n]
+
+    @pl.when(pl.program_id(0) == pl.num_programs(0) - 1)
+    def _():
+        bias_ref[...] = bscr[...].astype(BF)
 
 
 def afters(core, xm, xo, mine, theirs, w4, wout, wb, vec, heads):
@@ -426,12 +426,13 @@
         grid=(cols // cb,),
         in_specs=[pl.BlockSpec(memory_space=pltpu.SMEM), col(rows, c), col(rows, c), col(half, n), col(half, n)]
         + [full(v) for v in (w4, wout, wb, vec)],
-        out_specs=[col(n, c), col(1, heads * n), col(n, c)],
+        out_specs=[col(n, c), pl.BlockSpec((cols, heads * n), lambda j: (0, 0)), col(n, c)],
         out_shape=[
             jax.ShapeDtypeStruct((cols, n, c), F32),
-            jax.ShapeDtypeStruct((cols, 1, heads * n), F32),
+            jax.ShapeDtypeStruct((cols, heads * n), BF),
             jax.ShapeDtypeStruct((cols, n, c), BF),
         ],
+        scratch_shapes=[pltpu.VMEM((cols, heads * n), F32)],
         compiler_params=pltpu.CompilerParams(vmem_limit_bytes=56 << 20),
         cost_estimate=cost(8 * cols * n * c * c, 10 * cols * n * c, cols * n * c),
         name="afters",
@@ -507,12 +508,11 @@
 
 
 def operand_grads_kernel(groups, *refs):
-    sets = [refs[groups * s:groups * (s + 1)] for s in range(4)]
-    gm_ref, gt_ref, gl_keep, gr_keep, gl_send, gr_send, scr, lscr, rscr = refs[4 * groups:]
-    g, _, n = sets[0][0].shape
-    wide = sets[2][0].shape[2]
-    cols = gm_ref.shape[0]
-    rows = gl_keep.shape[0]
+    sets = [refs[:groups], refs[groups:2 * groups]]
+    gm_ref, gt_ref, keep_ref, send_ref, scr, lscr, rscr = refs[2 * groups:]
+    cols, g, n = gm_ref.shape
+    rows = keep_ref.shape[0]
+    wide = keep_ref.shape[2] - n
     gm = gm_ref[...].astype(F32).reshape(cols * g, n)
     gt = gt_ref[...].astype(F32).reshape(cols * g, n)
     for t in range(n // 128):
@@ -520,35 +520,32 @@
         scr[t, cols * g :] = gt[:, t * 128 : (t + 1) * 128]
     blank = [jnp.zeros((wide - 2 * cols, n), F32)] if wide > 2 * cols else []
     fetch = lambda at: jnp.concatenate([scr[t, pl.ds(at, cols, stride=g), :] for t in range(n // 128)], axis=1)
-    for part, (gl_ref, gr_ref) in enumerate(((gl_keep, gr_keep), (gl_send, gr_send))):
+    for part, out_ref in enumerate((keep_ref, send_ref)):
         for e in range(g):
             pieces = [fetch(e), fetch(cols * g + e)]
             gp = jnp.concatenate(pieces + blank, axis=0).astype(BF)
             seen = gp if part == 0 else jnp.concatenate(pieces[::-1] + blank, axis=0).astype(BF)
-            left = jnp.concatenate([r[e] for r in sets[part]], axis=0)
-            right = jnp.concatenate([r[e] for r in sets[2 + part]], axis=0)
-            spread(rscr, e, rows, g, nt(left, seen))
-            spread(lscr, e, rows, g, nn(right, gp))
-        gl_ref[...] = joined(lscr).astype(BF).reshape(gl_ref.shape)
-        gr_ref[...] = joined(rscr).astype(BF).reshape(gr_ref.shape)
-
-
-def operand_grads(keep_l, recv_l, keep_r, recv_r, gmine, gtheirs):
-    half, _, n = keep_l[0].shape
-    wide = keep_r[0].shape[2]
-    rows = sum(v.shape[1] for v in keep_l)
-    cols = gmine.shape[0]
+            both = jnp.concatenate([r[e] for r in sets[part]], axis=0)
+            spread(rscr, e, rows, g, nt(both[:, :n], seen))
+            spread(lscr, e, rows, g, nn(both[:, n:], gp))
+        both = jnp.concatenate([joined(lscr), joined(rscr)], axis=1)
+        out_ref[...] = both.astype(BF).reshape(out_ref.shape)
+
+
+def operand_grads(keep, recv, gmine, gtheirs):
+    half, _, lanes = keep[0].shape
+    rows = sum(v.shape[1] for v in keep)
+    cols, _, n = gmine.shape
+    wide = lanes - n
     g = GROUP
-    ins = keep_l + recv_l + keep_r + recv_r
-    left = pl.BlockSpec((rows, g, n), lambda b: (0, b, 0))
-    right = pl.BlockSpec((rows, g, wide), lambda b: (0, b, 0))
+    out = jax.ShapeDtypeStruct((rows, half, lanes), BF)
     return pl.pallas_call(
-        functools.partial(operand_grads_kernel, len(keep_l)),
+        functools.partial(operand_grads_kernel, len(keep)),
         grid=(half // g,),
-        in_specs=[pl.BlockSpec((g,) + v.shape[1:], lambda b: (b, 0, 0)) for v in ins]
+        in_specs=[pl.BlockSpec((g,) + v.shape[1:], lambda b: (b, 0, 0)) for v in keep + recv]
         + [pl.BlockSpec((cols, g, n), lambda b: (0, b, 0))] * 2,
-        out_specs=[left, right] * 2,
-        out_shape=[jax.ShapeDtypeStruct((rows, half, n), BF), jax.ShapeDtypeStruct((rows, half, wide), BF)] * 2,
+        out_specs=[pl.BlockSpec((rows, g, lanes), lambda b: (0, b, 0))] * 2,
+        out_shape=[out, out],
         scratch_shapes=[
             pltpu.VMEM((n // 128, 2 * cols * g, 128), F32),
             pltpu.VMEM((n // 128, rows * g, 128), F32),
@@ -557,36 +554,36 @@
         compiler_params=pltpu.CompilerParams(vmem_limit_bytes=60 << 20),
         cost_estimate=cost(4 * half * n * n * wide, 8 * half * n * n),
         name="operand_grads",
-    )(*ins, gmine, gtheirs)
-
-
-def tri_grads_kernel(n_ref, nc_ref, gl_ref, gr_ref, wl_ref, wr_ref, al_ref, ar_ref, lg, rg):
+    )(*keep, *recv, gmine, gtheirs)
+
+
+def tri_grads_kernel(n_ref, nc_ref, g_ref, wl_ref, wr_ref, al_ref, ar_ref, lg, rg):
     @pl.when(pl.program_id(0) == 0)
     def _():
         al_ref[...] = jnp.zeros_like(al_ref)
         ar_ref[...] = jnp.zeros_like(ar_ref)
     rows, n, c = n_ref.shape
     wide = nc_ref.shape[1]
-    half = gl_ref.shape[1]
+    half = g_ref.shape[1]
     def one(low, grad, w):
         p = nt(w, low)
         s = sigm(p[half:])
         first = grad.astype(F32) * s
         return first.astype(BF), (first * p[:half] * (1.0 - s)).astype(BF)
     for k in range(rows):
-        a, b = one(n_ref[k], gl_ref[k], wl_ref[...])
+        a, b = one(n_ref[k], g_ref[k, :, :n], wl_ref[...])
         lg[:half, k*n:(k+1)*n] = a
         lg[half:, k*n:(k+1)*n] = b
-        a, b = one(nc_ref[k], gr_ref[k], wr_ref[...])
+        a, b = one(nc_ref[k], g_ref[k, :, n:], wr_ref[...])
         rg[:half, k*wide:(k+1)*wide] = a
         rg[half:, k*wide:(k+1)*wide] = b
     al_ref[...] += nn(lg[...], n_ref[...].reshape(rows*n, c))
     ar_ref[...] += nn(rg[...], nc_ref[...].reshape(rows*wide, c))
 
 
-def tri_grads(nrm, near, gl, gr, wl, wr):
+def tri_grads(nrm, near, grad, wl, wr):
     count, n, c = nrm.shape
-    half = gl.shape[1]
+    half = grad.shape[1]
     wide = near.shape[1]
     rows = batch(count, 24)
     full = lambda v: pl.BlockSpec(v.shape, lambda b: (0,) * v.ndim)
@@ -595,21 +592,65 @@
     return pl.pallas_call(
         tri_grads_kernel,
         grid=(count // rows,),
-        in_specs=[row(n, c), row(wide, c), row(half, n), row(half, wide), full(wl), full(wr)],
+        in_specs=[row(n, c), row(wide, c), row(half, n + wide), full(wl), full(wr)],
         out_specs=[pl.BlockSpec(out.shape, lambda k: (0, 0))] * 2,
         out_shape=[out] * 2,
         scratch_shapes=[pltpu.VMEM((2*half, rows*n), BF), pltpu.VMEM((2*half, rows*wide), BF)],
         compiler_params=pltpu.CompilerParams(vmem_limit_bytes=56 << 20),
         cost_estimate=cost(8 * count * n * c * c, 8 * count * n * c, count * n * half),
         name="tri_grads",
-    )(nrm, near, gl, gr, wl, wr)
+    )(nrm, near, grad, wl, wr)
+
+
+def adam_kernel(scale_ref, sum_ref, shrink_ref, bias_ref, vec_ref, *refs):
+    masters, firsts, seconds = refs[:8], refs[8:16], refs[16:24]
+    new_masters, new_firsts, new_seconds = refs[24:32], refs[32:40], refs[40:]
+    at = [0]
+
+    def take(ref):
+        at[0] += ref.shape[-1]
+        return sum_ref[:, at[0] - ref.shape[-1] : at[0]]
+
+    grads = {slot: take(masters[slot]) for slot in (2, 4, 5, 1, 0)}
+    grads.update({3: bias_ref[...], 6: shrink_ref[...], 7: vec_ref[...]})
+    for slot in range(8):
+        whole = (lambda ref: ref[...]) if slot == 7 else (lambda ref: ref[0])
+        clipped = grads[slot] * scale_ref[0]
+        master = whole(masters[slot])
+        moment = beta_first * whole(firsts[slot]) + (1 - beta_first) * clipped
+        square = beta_second * whole(seconds[slot]) + (1 - beta_second) * clipped * clipped
+        stride = (
+            moment
+            / (1 - beta_first**STEP)
+            / (jnp.sqrt(square / (1 - beta_second**STEP)) + adam_epsilon)
+        )
+        rate = vector_rate if slot == 7 else learn_rate
+        fresh = (master - rate * (stride + weight_decay * master), moment, square)
+        for refs_out, value in zip((new_masters, new_firsts, new_seconds), fresh):
+            if slot == 7:
+                refs_out[slot][...] = value
+            else:
+                refs_out[slot][0] = value
+
+
+def adam(scale, total, shrink, bias, vec, masters, firsts, seconds):
+    ins = [total, shrink, bias, vec, *masters, *firsts, *seconds]
+    vmem = pl.BlockSpec(memory_space=pltpu.VMEM)
+    return pl.pallas_call(
+        adam_kernel,
+        in_specs=[pl.BlockSpec(memory_space=pltpu.SMEM)] + [vmem] * len(ins),
+        out_specs=[vmem] * 24,
+        out_shape=[jax.ShapeDtypeStruct(v.shape, F32) for v in [*masters, *firsts, *seconds]],
+        compiler_params=pltpu.CompilerParams(vmem_limit_bytes=40 << 20),
+        name="adam",
+    )(scale, *ins)
 
 
 def gather_weights(tri, tri_out, attn, bias, outp, expand, shrink, vectors):
     rows = tri.shape[1]
     pieces = [tri[0], tri_out[0], attn[0], outp[0], expand[0], shrink[0].reshape(rows, -1), bias[0], vectors.T]
     widths = [p.shape[1] for p in pieces]
-    packed = lax.all_gather(jnp.concatenate([p.astype(BF) for p in pieces], axis=1), "item", axis=0, tiled=True)
+    packed = jnp.concatenate(all_item(jnp.concatenate([p.astype(BF) for p in pieces], axis=1)))
     got, at = [], 0
     for w in widths:
         got.append(packed[:, at : at + w])
@@ -618,32 +659,42 @@
     return tri, tri_out, attn, bias, outp, expand, shr.reshape(-1, shrink.shape[2]), vec.T
 
 
-def gather_rows(rows):
-    size = lax.axis_size("pair")
+def project_rows(rows, project, size, first):
     here = lax.axis_index("pair")
     count = rows.shape[0]
     if size != 8 or count % 48:
         sets = [list(range(c, size, 2)) for c in range(2)]
-        return [lax.all_gather(rows, "pair", axis=0, tiled=True, axis_index_groups=sets)], jnp.arange(
-            size // 2 * count // GROUP
-        )
+        got = lax.all_gather(rows, "pair", axis=0, tiled=True, axis_index_groups=sets)
+        return [project(got, list(range(got.shape[0] // GROUP)))], first
     stages = 3
     step = count // stages
     per = step // GROUP
-    x = [rows[s * step : (s + 1) * step] for s in range(stages)]
+    x = [rows[s * step : (s + 1) * step] for s in range(stages)] + [None]
     spot = lambda device, s: [device // 2 * (stages * per) + s * per + u for u in range(per)]
-    groups, places = [rows], [p for s in range(stages) for p in spot(here, s)]
-    late = []
+    send = lambda value: [exchange(value, "pair", 2), exchange(value, "pair", 4)]
+    near, late = send(x[0]), []
+    done = [project(rows, [p for s in range(stages) for p in spot(here, s)])]
     for s in range(stages):
-        side, above = exchange(x[s], "pair", 2), exchange(x[s], "pair", 4)
+        waits = [x[s + 1], near, late, done[-1][0]]
+        if s == 1:
+            waits.append(first)
+        if s:
+            waits.append(done[-2][1])
+        held = lax.optimization_barrier(tuple(waits))
+        following, near, arrived, done[-1][0] = held[:4]
+        if s == 1:
+            first = held[4]
+        if s:
+            done[-2][1] = held[-1]
+        late = [exchange(near[0][: step // 2], "pair", 4), exchange(near[1][step // 2 :], "pair", 2)]
+        places = spot(here ^ 2, s) + spot(here ^ 4, s) + (spot(here ^ 6, s - 1) if arrived else [])
+        group = jnp.concatenate(near + arrived)
         if s + 1 < stages:
-            x[s + 1], side, above = lax.optimization_barrier((x[s + 1], side, above))
-        groups.append(jnp.concatenate([side, above] + late))
-        places += spot(here ^ 2, s) + spot(here ^ 4, s) + (spot(here ^ 6, s - 1) if late else [])
-        late = [exchange(side[: step // 2], "pair", 4), exchange(above[step // 2 :], "pair", 2)]
-    groups.append(jnp.concatenate(late))
-    places += spot(here ^ 6, stages - 1)
-    return groups, jnp.stack(places)
+            near = send(following)
+        done.append(project(group, places))
+    late, done[-1][0], done[-2][1] = lax.optimization_barrier((late, done[-1][0], done[-2][1]))
+    done.append(project(jnp.concatenate(late), spot(here ^ 6, stages - 1)))
+    return done, first
 
 
 def swap_cores(value):
@@ -664,24 +715,29 @@
     return value
 
 
-def sum_all(value):
-    return sum_axis(sum_axis(value, "item"), "pair")
-
-
-def sum_shards(parts):
+def sum_item(part, beside=()):
+    bit = lax.axis_size("item") // 2
+    here = lax.axis_index("item")
+    beside = list(beside)
+    while bit:
+        upper = (here // bit) % 2
+        rows = part.shape[0] // 2
+        kept = lax.dynamic_slice_in_dim(part, upper * rows, rows, 0)
+        sent = lax.dynamic_slice_in_dim(part, (1 - upper) * rows, rows, 0)
+        got = exchange(sent.astype(BF), "item", bit)
+        if beside:
+            work = beside.pop(0)
+            got, work[0] = lax.optimization_barrier((got, work[0]))
+        part = kept + got.astype(F32)
+        bit //= 2
+    return part
+
+
+def all_item(value):
     size = lax.axis_size("item")
     here = lax.axis_index("item")
-    bit = size // 2
-    while bit:
-        upper = (here // bit) % 2
-        kept, sent = [], []
-        for part in parts:
-            rows = part.shape[0] // 2
-            kept.append(lax.dynamic_slice_in_dim(part, upper * rows, rows, 0))
-            sent.append(lax.dynamic_slice_in_dim(part, (1 - upper) * rows, rows, 0))
-        parts = [k + exchange(s.astype(BF), "item", bit).astype(F32) for k, s in zip(kept, sent)]
-        bit //= 2
-    return [sum_axis(part, "pair") for part in parts]
+    got = jnp.stack([value] + [exchange(value, "item", bit) for bit in range(1, size)])
+    return [lax.dynamic_index_in_dim(got, here ^ t, 0, keepdims=False) for t in range(size)]
 
 
 def on_device(
@@ -720,16 +776,16 @@
     heads = bias_proj.shape[2]
     here = lax.axis_index("pair")
     core = here % 2
-    groups, places = gather_rows(pair_act[0])
     weight = gather_weights(
         tri_proj, tri_out, attention_proj, bias_proj, output_proj, expand_proj, shrink_proj, vectors
     )
     tri_w, tri_out_w, project_w, pairbias_w, output_w, expand_w, shrink_w, vector_low = weight
     vec = vector_low.astype(F32)
     weighting_rows = pair_mask.astype(F32)
-    both = lax.all_to_all(
-        jnp.concatenate([targets, weighting_rows]), "pair", split_axis=2, concat_axis=1, tiled=True
-    )
+    both = lax.all_gather(
+        jnp.concatenate([targets, weighting_rows]), "pair", axis=1, tiled=True
+    )
+    both = lax.dynamic_slice_in_dim(both, here * cols, cols, 2)
 
     scaled = (tri_w.astype(F32) * vec[0][:, None]).astype(BF).T
     tri_half = lambda s, c: lax.dynamic_slice_in_dim(scaled, width * s + half * c, half, 0)
@@ -743,101 +799,100 @@
     vec8 = jnp.concatenate([vec[:1], gain_c[None], vec[2:], jnp.zeros((3, width), F32)])
     wb = jnp.concatenate([pairbias_w.T, jnp.zeros((16 - heads, width), BF)])
 
-    offs = jnp.concatenate(
-        [jnp.stack([here * cols, (here + 1 - 2 * core) * cols]), places]
-    ).astype(jnp.int32)
-    keep, recv, bufs, start = [], [], None, 0
-    for rows in groups:
-        mine, sent, bufs = operands(offs, rows, w_left, w_right, cols, start, tokens // 2, bufs)
-        keep.append(mine)
-        recv.append([swap_cores(v) for v in sent])
-        start += rows.shape[0]
+    state = {"bufs": None, "start": 0}
+
+    def project(rows, places):
+        offs = jnp.stack([here * cols, (here + 1 - 2 * core) * cols, *places]).astype(jnp.int32)
+        mine, sent, state["bufs"] = operands(
+            offs, rows, w_left, w_right, cols, state["start"], tokens // 2, state["bufs"]
+        )
+        state["start"] += rows.shape[0]
+        return [mine, swap_cores(sent)]
+
+    done, both = project_rows(pair_act[0], project, lax.axis_size("pair"), both)
+    keep, recv = [v[0] for v in done], [v[1] for v in done]
+    bufs = state["bufs"]
     nrm, near, xm, xs = bufs
     xo = swap_cores(xs)
-    keep_l, keep_r = [v[0] for v in keep], [v[1] for v in keep]
-    recv_l, recv_r = [v[0] for v in recv], [v[1] for v in recv]
-    mine, send = products(keep_l + recv_l, keep_r + recv_r, cols)
+    mine, send = products(keep + recv, cols, tokens)
     theirs = swap_cores(send)
     cores = jnp.full((cols,), core, jnp.int32)
     after_c, bias_part, xc = afters(cores, xm, xo, mine, theirs, w_gate, wout, wb, vec8, heads)
-    bias_full = lax.all_gather(bias_part[:, 0].astype(BF), "pair", axis=0, tiled=True)
+    bias_full = lax.all_gather(bias_part, "pair", axis=0, tiled=True)
     hidden = expand_w.shape[1] // 2
-    expand_mix = (
-        expand_w.reshape(width, 2, hidden // 128, 128).swapaxes(1, 2).reshape(width, 2 * hidden)
-    )
     z = jnp.sum(shrink_w.astype(F32) * vec[4], axis=1)[None]
     gx, gmid, gb, gkv_w, gqg_w, gow, gew, svec, small = column_pass(
-        after_c, both[0], both[1], bias_full, project_w, project_w.T, output_w, expand_mix, vec8, z
+        after_c, both[0], both[1], bias_full, project_w, project_w.T, output_w, expand_w, vec8, z
     )
     bias_cols = lax.all_to_all(gb, "pair", split_axis=0, concat_axis=0, tiled=True)
-    scalars = sum_all(jnp.stack([jnp.sum(small[2]), jnp.sum(weighting_rows)]))
     gmine, gsend, gwb, gwout, gw4, small2 = back_pass(
         after_c, gx, gmid, bias_cols.reshape(-1, cols, heads, tokens), xc, mine, theirs,
         w_gate, wout, wb, vec8,
     )
+    early = jnp.concatenate(
+            [
+                gqg_w[:width].T,
+                gkv_w,
+                gqg_w[width:].T,
+                gow,
+                gew,
+                jnp.roll(gwout, half * core, axis=0),
+                gw4 * vec[0][:, None],
+                gwb[:heads].T,
+                jnp.roll(small2[1], half * core)[:, None],
+                small2[0][:, None],
+                small[1][:, None],
+                (small[0] + jnp.sum(svec[0][:, None] * shrink_w.astype(F32), axis=0))[:, None],
+                svec.reshape(width, -1),
+            ],
+            axis=1,
+        )
     gtheirs = swap_cores(gsend)
-    gl, gr, gl_sent, gr_sent = operand_grads(keep_l, recv_l, keep_r, recv_r, gmine, gtheirs)
-    gl_far, gr_far = swap_cores(gl_sent), swap_cores(gr_sent)
+    grad_keep, grad_sent = operand_grads(keep, recv, gmine, gtheirs)
+    grad_far = swap_cores(grad_sent)
     w_l = [jnp.concatenate([w[0], w[1]]) for w in (near_w, far_w)]
     w_r = [jnp.concatenate([w[2], w[3]]) for w in (near_w, far_w)]
-    near_a = tri_grads(nrm, near, gl, gr, w_l[0], w_r[0])
-    far_a = tri_grads(nrm, near, gl_far, gr_far, w_l[1], w_r[1])
+    near_a = list(tri_grads(nrm, near, grad_keep, w_l[0], w_r[0]))
+    far_a = list(tri_grads(nrm, near, grad_far, w_l[1], w_r[1]))
+    early = sum_item(early, (near_a, far_a))
     a_tri = []
     for near_part, far_part in zip(near_a, far_a):
         for s in range(2):
             parts = [p[s * half : (s + 1) * half] for p in (near_part, far_part)]
             a_tri += [jnp.where(core == 0, parts[0], parts[1]), jnp.where(core == 0, parts[1], parts[0])]
     a_tri = jnp.concatenate(a_tri + [gw4.T]).T
-    g_read = small[0] + jnp.sum(svec[0][:, None] * shrink_w.astype(F32), axis=0)
-    g_vec = jnp.stack(
-        [
-            jnp.sum(a_tri * tri_w.astype(F32), axis=1),
-            jnp.roll(small2[1], half * core),
-            small2[0],
-            small[1],
-            g_read,
-        ]
-    )
-    (total,) = sum_shards(
-        [
-            jnp.concatenate(
-                [
-                    gqg_w[:width].T,
-                    gkv_w,
-                    gqg_w[width:].T,
-                    gow,
-                    gew,
-                    a_tri * vec[0][:, None],
-                    jnp.roll(gwout, half * core, axis=0),
-                    svec.reshape(width, -1),
-                    gwb[:heads].T,
-                    g_vec.T,
-                ],
-                axis=1,
-            )
-        ]
-    )
-    loss_sum, count = scalars[0], scalars[1]
-    widths = (4 * width, width, 2 * hidden, 5 * width, width, svec.shape[1] // width, heads)
-    cuts = []
-    for w in widths:
-        cuts.append(total[:, :w])
-        total = total[:, w:]
-    shards = [
-        cuts[3],
-        cuts[4],
-        cuts[0],
-        cuts[6],
-        cuts[1],
-        cuts[2].reshape(-1, hidden // 128, 2, 128).swapaxes(1, 2).reshape(-1, 2 * hidden),
-        cuts[5].reshape(-1, 1) * vec[4][None, :],
-        total.T,
-    ]
-    shards = [s / count for s in shards]
-    squares = sum_axis(sum(jnp.sum(s * s) for s in shards), "item")
-    grad_norm = jnp.sqrt(squares)
+    g_gain = jnp.sum(a_tri * tri_w.astype(F32), axis=1)[:, None]
+    late = sum_item(jnp.concatenate([a_tri[:, : 4 * width] * vec[0][:, None], g_gain], axis=1))
+    cut = 8 * width + 2 * hidden - width
+    joint = sum_axis(
+        jnp.concatenate(
+            [
+                early[:, : cut - width],
+                late[:, : 4 * width],
+                early[:, cut - width :],
+                late[:, 4 * width :],
+                jnp.pad(jnp.stack([jnp.sum(small[2]), jnp.sum(weighting_rows)]), (0, late.shape[0] - 2))[:, None],
+            ],
+            axis=1,
+        ),
+        "pair",
+    )
+    total = joint[:, : cut + 4 * width]
+    rest = joint[:, cut + 4 * width :]
+    g_bias, g_vec, g_svec = rest[:, :heads], rest[:, heads : heads + 4], rest[:, heads + 4 : -2]
+    g_gain = rest[:, -2:-1]
+    g_vec = jnp.concatenate([g_gain, g_vec], axis=1).T
+    g_shrink = g_svec.reshape(-1, 1) * vec[4][None, :]
+    squares = (
+        jnp.sum(total * total)
+        + jnp.sum(g_bias * g_bias)
+        + jnp.sum(g_vec * g_vec)
+        + jnp.sum(g_svec * g_svec) * jnp.sum(vec[4] * vec[4])
+    )
+    sums = sum(all_item(jnp.stack([squares, rest[0, -1], rest[1, -1]])))
+    loss_sum, count = sums[1], sums[2]
+    grad_norm = jnp.sqrt(sums[0]) / count
     factor = jnp.minimum(1.0, clip_limit / (grad_norm + 1e-06))
-    shards = [s[None] for s in shards[:7]] + shards[7:]
     masters = (
         tri_proj,
         tri_out,
@@ -868,23 +923,10 @@
         second_shrink,
         second_vectors,
     )
-    rates = (learn_rate,) * 7 + (vector_rate,)
-    new_masters, new_firsts, new_seconds = ([], [], [])
-    for master, grad, first, second, rate in zip(masters, shards, firsts, seconds, rates):
-        clipped = grad * factor
-        moment = beta_first * first + (1 - beta_first) * clipped
-        square = beta_second * second + (1 - beta_second) * clipped * clipped
-        stride = (
-            moment
-            / (1 - beta_first**STEP)
-            / (jnp.sqrt(square / (1 - beta_second**STEP)) + adam_epsilon)
-        )
-        new_masters.append(master - rate * (stride + weight_decay * master))
-        new_firsts.append(moment)
-        new_seconds.append(square)
-    return (
-        (loss_sum, count, grad_norm) + tuple(new_masters) + tuple(new_firsts) + tuple(new_seconds)
-    )
+    outs = adam(
+        (factor / count)[None], total, g_shrink, g_bias, g_vec, masters, firsts, seconds
+    )
+    return (loss_sum, count, grad_norm) + tuple(outs)
 
 
 def solution(mesh):

time: 789 us -> 755 us (0.957)
  blocking collectives: 39.5 us -> 20.2 us
  starting transfers between devices: 41.5 us -> 32.3 us
    all_gather x1 -> x0, blocking collectives: 19.3 us -> none  [gather_weights(): lax.all_gather(jnp.concatenate([p.astype(BF) for p in pieces], axis=1), '...]
    all_gather x1 -> x2, waiting for transfers between devices: 10.3 us -> 17.9 us  [the longest x1 17.9 us: on_device(): bias_full = lax.all_gather(bias_part, 'pair', axis=0, tiled=True)]
    ppermute x24 -> x25, waiting for transfers between devices: 96.8 us -> 91.5 us  [exchange(): return lax.ppermute(value, axis, [(d, d ^ bit) for d in range(size)])]
    slice x10 -> x17, local copies, waits for them, and re-layouts: 14.9 us -> 19 us  [the longest x3 6.31 us: project_rows(): near[0][:step // 2]]
    ppermute x24 -> x25, starting transfers between devices: 33.8 us -> 30.8 us  [exchange(): return lax.ppermute(value, axis, [(d, d ^ bit) for d in range(size)])]
    concatenate x5 -> x6, other arithmetic: 16.6 us -> 18.8 us  [the longest x3 15.1 us: project_rows(): group = jnp.concatenate(near + arrived)]
    pallas_call x2 -> x3, Pallas kernels: 54.1 us -> 55.2 us  [the longest x1 40.3 us: operand_grads(): pl.pallas_call(functools.partial(operand_grads_kernel, len(keep)), grid=(...]
  transfers between devices with their start and end apart: 41 -> 36, of which waited for: 20 -> 15; matrix products, arithmetic and copies ran while one was open for 8% -> 9% of each run, Pallas kernels for 16% -> 19%
where the time goes in v5:
time: 755 us; the launch traced here: 750 us
  Pallas kernels  452 us (60%)
  waiting for transfers between devices  118 us (16%)
  other arithmetic  56.1 us (7%)
  local copies, waits for them, and re-layouts  48.6 us (6%)
  starting transfers between devices  32.3 us (4%)
  between operations  22.4 us (3%)
  blocking collectives  20.2 us (3%)
    pallas_call x1, Pallas kernels, column_pass(): pl.pallas_call(functools.partial(column_kernel, heads), grid=(cols // cb,...  201 us
    ppermute x25, waiting for transfers between devices, exchange(): return lax.ppermute(value, axis, [(d, d ^ bit) for d in range(size)])  91.5 us
    pallas_call x5, Pallas kernels, operands(): pl.pallas_call(functools.partial(operand_kernel, cols), grid_spec=pltpu.P...  84.5 us
    pallas_call x2, Pallas kernels, tri_grads(): pl.pallas_call(tri_grads_kernel, grid=(count // rows,), in_specs=[row(n,...  46.2 us
    pallas_call x1, Pallas kernels, back_pass(): pl.pallas_call(back_kernel, grid=(cols // cb,), in_specs=[col(n, c)] * 3...  43.4 us
    pallas_call x1, Pallas kernels, operand_grads(): pl.pallas_call(functools.partial(operand_grads_kernel, len(keep)), grid=(...  40.3 us
    ppermute x25, starting transfers between devices, exchange(): return lax.ppermute(value, axis, [(d, d ^ bit) for d in range(size)])  30.8 us
    pallas_call x1, Pallas kernels, afters(): pl.pallas_call(functools.partial(after_kernel, heads), grid=(cols // cb,)...  22.3 us
  transfers between devices with their start and end apart: 36, of which 15 were waited for; matrix products, arithmetic and copies ran while one was open for 9% of the time, Pallas kernels for 19%

profile of v5, /device:TPU:0, one launch (start us, length us, event | category | flops | bytes accessed | tf_op | source)
XLA Modules:
  0.0 749.7 jit_solution(16036434871076948399)
XLA Ops:
  13.2 5.1 collective-permute-start.4
  40.6 20.1 %operands.5 = (bf16[64,48,512]{2,1,0:T(8,128)(2,1)}, bf16[64,48,512]{2,1,0:T(8,128)(2,1)}, bf16[192,384,128]{2,1,0:T(8,128)(2,1)}, bf16[192,128,128]{2,1,0:T(8,1...) custom-call(s32[5]{0:T(128)} %stack.117.off_ref, bf16[48,384,128]{2,1,0:T(8,128)(2,1)} %bitcast.148, ...), custom_call_target="tpu_custom_call" | custom-call | flops 143999991808 | bytes 18874368 | tf_op jit(solution)/shard_map/operands/pallas_call | solution.py:316
  77.6 14.6 %operands.6 = (bf16[64,32,512]{2,1,0:T(8,128)(2,1)}, bf16[64,32,512]{2,1,0:T(8,128)(2,1)}, bf16[192,384,128]{2,1,0:T(8,128)(2,1)}, bf16[192,128,128]{2,1,0:T(8,1...) custom-call(s32[4]{0:T(128)} %pad_add_fusion.1.off_ref, ...), custom_call_target="tpu_custom_call", output_to_operand_aliasing={{2}: (4, {}), {3}: (5, {}), {4}: (6, {}), {5}: (7, {})} | custom-call | flops 96000000000 | bytes 12582912 | tf_op jit(solution)/shard_map/operands/pallas_call | solution.py:316
  94.3 31.0 %collective-permute-done.8 = bf16[8,384,128]{2,1,0:T(8,128)(2,1)} collective-permute-done((bf16[8,384,128]{2,1,0:T(8,128)(2,1)}, bf16[8,384,128]{2,1,0:T(8,128)(2,1)}, u32[]{:S(2)}, u32[]{:S(2)}) %collective-permute-start.8) | collective-permute-done | bytes 786464 | tf_op jit(solution)/shard_map/ppermute | solution.py:707
  133.7 5.6 pad_maximum_fusion.x_ref
  139.3 20.2 %operands.7 = (bf16[64,48,512]{2,1,0:T(8,128)(2,1)}, bf16[64,48,512]{2,1,0:T(8,128)(2,1)}, bf16[192,384,128]{2,1,0:T(8,128)(2,1)}, bf16[192,128,128]{2,1,0:T(8,1...) custom-call(s32[5]{0:T(128)} %stack.129.off_ref, ...), custom_call_target="tpu_custom_call", output_to_operand_aliasing={{2}: (4, {}), {3}: (5, {}), {4}: (6, {}), {5}: (7, {})} | custom-call | flops 143999991808 | bytes 18874368 | tf_op jit(solution)/shard_map/operands/pallas_call | solution.py:316
  159.6 20.9 %collective-permute-done.13 = bf16[8,384,128]{2,1,0:T(8,128)(2,1)} collective-permute-done((bf16[8,384,128]{2,1,0:T(8,128)(2,1)}, bf16[8,384,128]{2,1,0:T(8,128)(2,1)}, u32[]{:S(2)}, u32[]{:S(2)}) %collective-permute-start.13) | collective-permute-done | bytes 786464 | tf_op jit(solution)/shard_map/ppermute | solution.py:707
  186.7 5.6 pad_maximum_fusion.1.x_ref
  192.4 20.3 %operands.8 = (bf16[64,48,512]{2,1,0:T(8,128)(2,1)}, bf16[64,48,512]{2,1,0:T(8,128)(2,1)}, bf16[192,384,128]{2,1,0:T(8,128)(2,1)}, bf16[192,128,128]{2,1,0:T(8,1...) custom-call(s32[5]{0:T(128)} %stack.133.off_ref, ...), custom_call_target="tpu_custom_call", output_to_operand_aliasing={{2}: (4, {}), {3}: (5, {}), {4}: (6, {}), {5}: (7, {})} | custom-call | flops 143999991808 | bytes 18874368 | tf_op jit(solution)/shard_map/operands/pallas_call | solution.py:316
  215.5 9.2 %operands.9 = (bf16[64,16,512]{2,1,0:T(8,128)(2,1)}, bf16[64,16,512]{2,1,0:T(8,128)(2,1)}, bf16[192,384,128]{2,1,0:T(8,128)(2,1)}, bf16[192,128,128]{2,1,0:T(8,1...) custom-call(s32[3]{0:T(128)} %pad_add_fusion.off_ref, ...), custom_call_target="tpu_custom_call", output_to_operand_aliasing={{2}: (4, {}), {3}: (5, {}), {4}: (6, {}), {5}: (7, {})} | custom-call | flops 48000000000 | bytes 6291456 | tf_op jit(solution)/shard_map/operands/pallas_call | solution.py:316
  230.9 13.7 %products.1 = (bf16[48,64,384]{2,1,0:T(8,128)(2,1)}, bf16[48,64,384]{2,1,0:T(8,128)(2,1)}) custom-call(bf16[64,48,512]{2,1,0:T(8,128)(2,1)} %get-tuple-element.173.refs_0_, bf16[64,32,512]{2,1,0:T(8,128)(2,1)} %get-tuple-element.174.refs_1_, bf16[64,48,512]{2,1,0:T(8,128)(2,1)} %get-tuple-element.175.refs_2_, ...), custom_call_target="tpu_custom_call" | custom-call | flops 2415919104 | bytes 37748736 | tf_op jit(solution)/shard_map/products/pallas_call | solution.py:359
  250.0 22.3 %afters.1 = (f32[48,384,128]{2,1,0:T(8,128)}, bf16[48,1536]{1,0:T(8,128)(2,1)}, bf16[48,384,128]{2,1,0:T(8,128)(2,1)}) custom-call(s32[48]{0:T(128)} %broadcast_in_dim.26.core_ref, bf16[48,192,128]{2,1,0:T(8,128)(2,1)} %get-tuple-element.171.xm_ref, bf16[48,192,128]{2,1,0:T(8,128)(2,1)} %collective-permute-done.18.xo_ref, ...), custom_call_target="tpu_custom_call" | custom-call | flops 2415919104 | bytes 23592960 | tf_op jit(solution)/shard_map/afters/pallas_call | solution.py:424
  278.9 17.9 %all-gather.5.cloned.1.call-done.bias_ref = bf16[384,1536]{1,0:T(8,128)(2,1)} async-done(((bf16[48,1536]{1,0:T(8,128)(2,1)}), bf16[384,1536]{1,0:T(8,128)(2,1)}) %all-gather.5.cloned.1.call-update) | async-done | bytes 1179664 | tf_op jit(solution)/shard_map/all_gather | solution.py:821
  296.7 200.6 %columns.1 = (f32[48,384,128]{2,1,0:T(8,128)}, f32[48,384,128]{2,1,0:T(8,128)}, bf16[384,1536]{1,0:T(8,128)(2,1)}, f32[128,256]{1,0:T(8,128)}, f32[256,128]{1,0:...) custom-call(f32[48,384,128]{2,1,0:T(8,128)} %get-tuple-element.185.after_ref, ...), custom_call_target="tpu_custom_call" | custom-call | flops 43486543872 | bytes 37748736 | tf_op jit(solution)/shard_map/columns/pallas_call | solution.py:214
  497.3 20.2 %all_to_all.9 = bf16[8,48,1536]{2,1,0:T(8,128)(2,1)S(1)} all-to-all(bf16[8,48,1536]{2,1,0:T(8,128)(2,1)} %bitcast.150), channel_id=1, replica_groups=mesh['item'=4,'pair'=8] {'pair'}, dimensions={0} | all-to-all | bytes 2359296 | tf_op jit(solution)/shard_map/all_to_all | solution.py:827
  518.7 43.4 %back.1 = (bf16[48,64,384]{2,1,0:T(8,128)(2,1)}, bf16[48,64,384]{2,1,0:T(8,128)(2,1)}, f32[16,128]{1,0:T(8,128)}, f32[128,128]{1,0:T(8,128)}, f32[128,128]{1,0:T(8,128)}, /*index=5*/f32[8,128]{1,0:T(8,128)}) custom-call(f32[48,384,128]{2,1,0:T(8,128)} %get-tuple-element.185.after_ref, f32[48,384,128]{2,1,0:T(8,128)} %get-tuple-element.192.gx_ref, ...), custom_call_target="tpu_custom_call" | custom-call | flops 4831838208 | bytes 56623104 | tf_op jit(solution)/shard_map/back/pallas_call | solution.py:496
  562.2 4.7 collective-permute-done.23.refs_11_
  568.5 40.3 %operand_grads.1 = (bf16[192,64,512]{2,1,0:T(8,128)(2,1)}, bf16[192,64,512]{2,1,0:T(8,128)(2,1)}) custom-call(bf16[64,48,512]{2,1,0:T(8,128)(2,1)} %get-tuple-element.173.refs_0_, bf16[64,32,512]{2,1,0:T(8,128)(2,1)} %get-tuple-element.174.refs_1_, bf16[64,48,512]{2,1,0:T(8,128)(2,1)} %get-tuple-element.175.refs_2_, ...), custom_call_target="tpu_custom_call" | custom-call | flops 4831838208 | bytes 75497472 | tf_op jit(solution)/shard_map/operand_grads/pallas_call | solution.py:542
  621.0 23.2 %tri_grads.2 = (f32[128,128]{1,0:T(8,128)}, f32[128,128]{1,0:T(8,128)}) custom-call(bf16[192,384,128]{2,1,0:T(8,128)(2,1)} %get-tuple-element.202.n_ref, bf16[192,128,128]{2,1,0:T(8,128)(2,1)} %get-tuple-element.203.nc_ref, bf16[192,64,512]{2,1,0:T(8,128)(2,1)} %get-tuple-element.206.g_ref, bf16[128,128]{1,0:T(8,128)(2,1)} %pad_maximum_fusion.12.wl_ref, ...), custom_call_target="tpu_custom_call" | custom-call | flops 9663676416 | bytes 75497472 | tf_op jit(solution)/shard_map/tri_grads/pallas_call | solution.py:592
  646.4 23.0 %tri_grads.3 = (f32[128,128]{1,0:T(8,128)}, f32[128,128]{1,0:T(8,128)}) custom-call(bf16[192,384,128]{2,1,0:T(8,128)(2,1)} %get-tuple-element.202.n_ref, bf16[192,128,128]{2,1,0:T(8,128)(2,1)} %get-tuple-element.203.nc_ref, bf16[192,64,512]{2,1,0:T(8,128)(2,1)} %collective-permute-done.25.g_ref, bf16[128,128]{1,0:T(8,128)(2,1)} %pad_maximum_fusion.14.wl_ref, ...), custom_call_target="tpu_custom_call" | custom-call | flops 9663676416 | bytes 75497472 | tf_op jit(solution)/shard_map/tri_grads/pallas_call | solution.py:592
  679.0 5.8 collective-permute-done.26
  685.5 5.0 collective-permute-done.27
  696.9 9.2 %collective-permute-done.29 = f32[32,2446]{1,0:T(8,128)S(1)} collective-permute-done((f32[32,2446]{1,0:T(8,128)S(1)}, f32[32,2446]{1,0:T(8,128)S(1)}, u32[]{:S(2)}, u32[]{:S(2)}) %collective-permute-start.29) | collective-permute-done | bytes 313120 | tf_op jit(solution)/shard_map/ppermute | solution.py:707
  711.6 6.8 collective-permute-done.30
  (365 shorter events, 138.4 us)
Async XLA Ops:
  7.2 85.0 %all-gather.3.cloned.1.call-start = ((), (), s32[]{:S(2)}) async-start(), calls=%async_computation.1 | async-start | bytes 1327104 | tf_op jit(solution)/shard_map/all_gather | solution.py:785
  13.2 17.5 %collective-permute-start.4 = (bf16[32,2953]{1,0:T(8,128)(2,1)S(1)}, bf16[32,2953]{1,0:T(8,128)(2,1)S(1)}, u32[]{:S(2)}, u32[]{:S(2)}) collective-permute-start(bf16[32,2953]{1,0:T(8,128)(2,1)S(1)} %concatenate.71), channel_id=1, source_target_pairs={{0,24},{8,16},{16,8},{24,0},{1,25},{9,17},{17,9},{25,1},{2,26},{10... | collective-permute-start | bytes 566984 | tf_op jit(solution)/shard_map/ppermute | solution.py:707
  18.3 16.7 %collective-permute-start.3 = (bf16[32,2953]{1,0:T(8,128)(2,1)S(1)}, bf16[32,2953]{1,0:T(8,128)(2,1)S(1)}, u32[]{:S(2)}, u32[]{:S(2)}) collective-permute-start(bf16[32,2953]{1,0:T(8,128)(2,1)S(1)} %concatenate.71), channel_id=1, source_target_pairs={{0,16},{8,24},{16,0},{24,8},{1,17},{9,25},{17,1},{25,9},{2,18},{10... | collective-permute-start | bytes 566984 | tf_op jit(solution)/shard_map/ppermute | solution.py:707
  18.3 16.7 %collective-permute-start.2 = (bf16[32,2953]{1,0:T(8,128)(2,1)S(1)}, bf16[32,2953]{1,0:T(8,128)(2,1)S(1)}, u32[]{:S(2)}, u32[]{:S(2)}) collective-permute-start(bf16[32,2953]{1,0:T(8,128)(2,1)S(1)} %concatenate.71), channel_id=1, source_target_pairs={{0,8},{8,0},{16,24},{24,16},{1,9},{9,1},{17,25},{25,17},{2,10},{10... | collective-permute-start | bytes 566984 | tf_op jit(solution)/shard_map/ppermute | solution.py:707
  23.6 40.6 %collective-permute-start.1 = (bf16[16,384,128]{2,1,0:T(8,128)(2,1)}, bf16[16,384,128]{2,1,0:T(8,128)(2,1)}, u32[]{:S(2)}, u32[]{:S(2)}) collective-permute-start(bf16[16,384,128]{2,1,0:T(8,128)(2,1)} %get-tuple-element.350), channel_id=1, source_target_pairs={{0,4},{1,5},{2,6},{3,7},{4,0},{5,1},{6,2},{7,3},{8,12},{9,13},{10,... | collective-permute-start | bytes 4718600 | tf_op jit(solution)/shard_map/ppermute | solution.py:707
  25.3 40.2 %collective-permute-start = (bf16[16,384,128]{2,1,0:T(8,128)(2,1)}, bf16[16,384,128]{2,1,0:T(8,128)(2,1)}, u32[]{:S(2)}, u32[]{:S(2)}) collective-permute-start(bf16[16,384,128]{2,1,0:T(8,128)(2,1)} %get-tuple-element.350), channel_id=1, source_target_pairs={{0,2},{1,3},{2,0},{3,1},{4,6},{5,7},{6,4},{7,5},{8,10},{9,11},{10,... | collective-permute-start | bytes 4718600 | tf_op jit(solution)/shard_map/ppermute | solution.py:707
  27.5 269.2 %all-gather.5.cloned.1.call-start = ((), (), s32[]{:S(2)}) async-start(), calls=%async_computation.2 | async-start | bytes 1327104 | tf_op jit(solution)/shard_map/all_gather | solution.py:821
  60.7 64.6 %collective-permute-start.9 = (bf16[64,48,512]{2,1,0:T(8,128)(2,1)}, bf16[64,48,512]{2,1,0:T(8,128)(2,1)S(1)}, u32[]{:S(2)}, u32[]{:S(2)}) collective-permute-start(bf16[64,48,512]{2,1,0:T(8,128)(2,1)} %get-tuple-element.143), channel_id=1, source_target_pairs={{0,1},{1,0},{2,3},{3,2},{4,5},{5,4},{6,7},{7,6},{8,9},{9,8},{10,11... | collective-permute-start | bytes 9437192 | tf_op jit(solution)/shard_map/ppermute | solution.py:702
  73.5 51.8 %collective-permute-start.6 = (bf16[16,384,128]{2,1,0:T(8,128)(2,1)}, bf16[16,384,128]{2,1,0:T(8,128)(2,1)}, u32[]{:S(2)}, u32[]{:S(2)}) collective-permute-start(bf16[16,384,128]{2,1,0:T(8,128)(2,1)} %get-tuple-element.135), channel_id=1, source_target_pairs={{0,4},{1,5},{2,6},{3,7},{4,0},{5,1},{6,2},{7,3},{8,12},{9,13},{10,... | collective-permute-start | bytes 4718600 | tf_op jit(solution)/shard_map/ppermute | solution.py:707
  74.0 51.3 %collective-permute-start.5 = (bf16[16,384,128]{2,1,0:T(8,128)(2,1)}, bf16[16,384,128]{2,1,0:T(8,128)(2,1)}, u32[]{:S(2)}, u32[]{:S(2)}) collective-permute-start(bf16[16,384,128]{2,1,0:T(8,128)(2,1)} %get-tuple-element.135), channel_id=1, source_target_pairs={{0,2},{1,3},{2,0},{3,1},{4,6},{5,7},{6,4},{7,5},{8,10},{9,11},{10,... | collective-permute-start | bytes 4718600 | tf_op jit(solution)/shard_map/ppermute | solution.py:707
  75.5 49.8 %collective-permute-start.8 = (bf16[8,384,128]{2,1,0:T(8,128)(2,1)}, bf16[8,384,128]{2,1,0:T(8,128)(2,1)}, u32[]{:S(2)}, u32[]{:S(2)}) collective-permute-start(bf16[8,384,128]{2,1,0:T(8,128)(2,1)} %slice.200), channel_id=1, source_target_pairs={{0,2},{1,3},{2,0},{3,1},{4,6},{5,7},{6,4},{7,5},{8,10},{9,11},{10,... | collective-permute-start | bytes 2359304 | tf_op jit(solution)/shard_map/ppermute | solution.py:707
  76.0 49.2 %collective-permute-start.7 = (bf16[8,384,128]{2,1,0:T(8,128)(2,1)}, bf16[8,384,128]{2,1,0:T(8,128)(2,1)}, u32[]{:S(2)}, u32[]{:S(2)}) collective-permute-start(bf16[8,384,128]{2,1,0:T(8,128)(2,1)} %slice.199), channel_id=1, source_target_pairs={{0,4},{1,5},{2,6},{3,7},{4,0},{5,1},{6,2},{7,3},{8,12},{9,13},{10,... | collective-permute-start | bytes 2359304 | tf_op jit(solution)/shard_map/ppermute | solution.py:707
  125.3 34.2 %collective-permute-start.14 = (bf16[64,32,512]{2,1,0:T(8,128)(2,1)}, bf16[64,32,512]{2,1,0:T(8,128)(2,1)}, u32[]{:S(2)}, u32[]{:S(2)}) collective-permute-start(bf16[64,32,512]{2,1,0:T(8,128)(2,1)} %get-tuple-element.154), channel_id=1, source_target_pairs={{0,1},{1,0},{2,3},{3,2},{4,5},{5,4},{6,7},{7,6},{8,9},{9,8},{10,11... | collective-permute-start | bytes 6291464 | tf_op jit(solution)/shard_map/ppermute | solution.py:702
  125.3 55.1 %collective-permute-start.11 = (bf16[16,384,128]{2,1,0:T(8,128)(2,1)}, bf16[16,384,128]{2,1,0:T(8,128)(2,1)}, u32[]{:S(2)}, u32[]{:S(2)}) collective-permute-start(bf16[16,384,128]{2,1,0:T(8,128)(2,1)} %get-tuple-element.144), channel_id=1, source_target_pairs={{0,4},{1,5},{2,6},{3,7},{4,0},{5,1},{6,2},{7,3},{8,12},{9,13},{10,... | collective-permute-start | bytes 4718600 | tf_op jit(solution)/shard_map/ppermute | solution.py:707
  126.8 53.7 %collective-permute-start.10 = (bf16[16,384,128]{2,1,0:T(8,128)(2,1)}, bf16[16,384,128]{2,1,0:T(8,128)(2,1)}, u32[]{:S(2)}, u32[]{:S(2)}) collective-permute-start(bf16[16,384,128]{2,1,0:T(8,128)(2,1)} %get-tuple-element.144), channel_id=1, source_target_pairs={{0,2},{1,3},{2,0},{3,1},{4,6},{5,7},{6,4},{7,5},{8,10},{9,11},{10,... | collective-permute-start | bytes 4718600 | tf_op jit(solution)/shard_map/ppermute | solution.py:707
  132.5 48.0 %collective-permute-start.13 = (bf16[8,384,128]{2,1,0:T(8,128)(2,1)}, bf16[8,384,128]{2,1,0:T(8,128)(2,1)}, u32[]{:S(2)}, u32[]{:S(2)}) collective-permute-start(bf16[8,384,128]{2,1,0:T(8,128)(2,1)} %slice.202), channel_id=1, source_target_pairs={{0,2},{1,3},{2,0},{3,1},{4,6},{5,7},{6,4},{7,5},{8,10},{9,11},{10,... | collective-permute-start | bytes 2359304 | tf_op jit(solution)/shard_map/ppermute | solution.py:707
  133.0 47.4 %collective-permute-start.12 = (bf16[8,384,128]{2,1,0:T(8,128)(2,1)}, bf16[8,384,128]{2,1,0:T(8,128)(2,1)}, u32[]{:S(2)}, u32[]{:S(2)}) collective-permute-start(bf16[8,384,128]{2,1,0:T(8,128)(2,1)} %slice.201), channel_id=1, source_target_pairs={{0,4},{1,5},{2,6},{3,7},{4,0},{5,1},{6,2},{7,3},{8,12},{9,13},{10,... | collective-permute-start | bytes 2359304 | tf_op jit(solution)/shard_map/ppermute | solution.py:707
  159.5 53.3 %collective-permute-start.17 = (bf16[64,48,512]{2,1,0:T(8,128)(2,1)}, bf16[64,48,512]{2,1,0:T(8,128)(2,1)}, u32[]{:S(2)}, u32[]{:S(2)}) collective-permute-start(bf16[64,48,512]{2,1,0:T(8,128)(2,1)} %get-tuple-element.164), channel_id=1, source_target_pairs={{0,1},{1,0},{2,3},{3,2},{4,5},{5,4},{6,7},{7,6},{8,9},{9,8},{10,11... | collective-permute-start | bytes 9437192 | tf_op jit(solution)/shard_map/ppermute | solution.py:702
  184.7 28.1 %collective-permute-start.16 = (bf16[8,384,128]{2,1,0:T(8,128)(2,1)}, bf16[8,384,128]{2,1,0:T(8,128)(2,1)}, u32[]{:S(2)}, u32[]{:S(2)}) collective-permute-start(bf16[8,384,128]{2,1,0:T(8,128)(2,1)} %slice.204), channel_id=1, source_target_pairs={{0,2},{1,3},{2,0},{3,1},{4,6},{5,7},{6,4},{7,5},{8,10},{9,11},{10,... | collective-permute-start | bytes 2359304 | tf_op jit(solution)/shard_map/ppermute | solution.py:707
  186.2 26.6 %collective-permute-start.15 = (bf16[8,384,128]{2,1,0:T(8,128)(2,1)}, bf16[8,384,128]{2,1,0:T(8,128)(2,1)}, u32[]{:S(2)}, u32[]{:S(2)}) collective-permute-start(bf16[8,384,128]{2,1,0:T(8,128)(2,1)} %slice.203), channel_id=1, source_target_pairs={{0,4},{1,5},{2,6},{3,7},{4,0},{5,1},{6,2},{7,3},{8,12},{9,13},{10,... | collective-permute-start | bytes 2359304 | tf_op jit(solution)/shard_map/ppermute | solution.py:707
  225.1 24.1 %collective-permute-start.18 = (bf16[48,192,128]{2,1,0:T(8,128)(2,1)}, bf16[48,192,128]{2,1,0:T(8,128)(2,1)}, u32[]{:S(2)}, u32[]{:S(2)}) collective-permute-start(bf16[48,192,128]{2,1,0:T(8,128)(2,1)} %get-tuple-element.172), channel_id=1, source_target_pairs={{0,1},{1,0},{2,3},{3,2},{4,5},{5,4},{6,7},{7,6},{8,9},{9,8},{10,11... | collective-permute-start | bytes 7077896 | tf_op jit(solution)/shard_map/ppermute | solution.py:702
  608.9 37.5 %collective-permute-start.25 = (bf16[192,64,512]{2,1,0:T(8,128)(2,1)}, bf16[192,64,512]{2,1,0:T(8,128)(2,1)}, u32[]{:S(2)}, u32[]{:S(2)}) collective-permute-start(bf16[192,64,512]{2,1,0:T(8,128)(2,1)} %get-tuple-element.209), channel_id=1, source_target_pairs={{0,1},{1,0},{2,3},{3,2},{4,5},{5,4},{6,7},{7,6},{8,9},{9,8},{10,11... | collective-permute-start | bytes 37748744 | tf_op jit(solution)/shard_map/ppermute | solution.py:702
  618.5 25.7 %collective-permute-start.22 = (bf16[64,1932]{0,1:T(8,128)(2,1)S(1)}, bf16[64,1932]{0,1:T(8,128)(2,1)S(1)}, u32[]{:S(2)}, u32[]{:S(2)}) collective-permute-start(bf16[64,1932]{0,1:T(8,128)(2,1)S(1)} %dynamic-slice_convert_fusion.1), channel_id=1, source_target_pairs={{0,16},{8,24},{16,0},{24,8},{1,17},{9,25},{17,1},{25,9},{2,18},{10... | collective-permute-start | bytes 741896 | tf_op jit(solution)/shard_map/ppermute | solution.py:707
  644.8 24.5 %collective-permute-start.24 = (bf16[32,1932]{0,1:T(8,128)(2,1)S(1)}, bf16[32,1932]{0,1:T(8,128)(2,1)S(1)}, u32[]{:S(2)}, u32[]{:S(2)}) collective-permute-start(bf16[32,1932]{0,1:T(8,128)(2,1)S(1)} %dynamic-slice_convert_fusion), channel_id=1, source_target_pairs={{0,8},{8,0},{16,24},{24,16},{1,9},{9,1},{17,25},{25,17},{2,10},{10... | collective-permute-start | bytes 370952 | tf_op jit(solution)/shard_map/ppermute | solution.py:707
  (88 other events, 1323.3 us)
Sparse Core Ops, SparseCore 0:
  27.6 28.4 all-gather.2
  272.4 24.2 all-gather.4

commit v6 on v5

--- a/solution.py
+++ b/solution.py
@@ -238,8 +238,8 @@
 
 
 GROUP = 16
-AFTER_BATCH = 4
-BACK_BATCH = 4
+AFTER_BATCH = 6
+BACK_BATCH = 6
 
 
 def spread(scr, start, count, stride, value):
@@ -255,9 +255,22 @@
     return -(-count // 128) * 128
 
 
-def operand_kernel(cols, off_ref, x_ref, wl_ref, wr_ref, *refs):
-    keep_ref, send_ref, n_ref, nc_ref, xc_ref, xs_ref, lscr, rscr, nscr, xscr, cscr = refs[-11:]
-    rows, n, c = x_ref.shape
+def operand_kernel(cols, sizes, off_ref, *refs):
+    x_refs, (wl_ref, wr_ref) = refs[: len(sizes)], refs[len(sizes) : len(sizes) + 2]
+    keep_ref, send_ref, n_ref, nc_ref, xc_ref, xs_ref, lscr, rscr, nscr, xscr, cscr, block = refs[-12:]
+    rows, n, c = n_ref.shape
+    if len(sizes) == 1:
+        x_ref = x_refs[0]
+    else:
+        x_ref = block
+        at = 0
+        for size, ref in zip(sizes, x_refs):
+
+            @pl.when(pl.program_id(0) == at // rows)
+            def _(ref=ref, first=at % rows, size=size):
+                block[first : first + size] = ref[...]
+
+            at += size
     wide = nc_ref.shape[1]
     half = c // 2
     own = off_ref[0]
@@ -291,8 +304,9 @@
     xs_ref[...] = cscr[cols * rows:].astype(BF).reshape(xs_ref.shape)
 
 
-def operands(offs, x, wl, wr, cols, start, total, bufs):
-    count, n, c = x.shape
+def operands(offs, parts, wl, wr, cols, start, total, bufs):
+    n, c = parts[0].shape[1:]
+    count = sum(p.shape[0] for p in parts)
     half = c // 2
     wide = padded(2 * cols)
     g = GROUP
@@ -306,15 +320,16 @@
         ((cols, total, c), (cols, g, c), lambda b, o: (0, o[2 + b], 0)),
     ]
     full = lambda v: pl.BlockSpec(v.shape, lambda b, o: (0,) * v.ndim)
-    ins = [x, wl, wr]
-    specs = [pl.BlockSpec((g, n, c), lambda b, o: (b, 0, 0)), full(wl), full(wr)]
+    ins = [*parts, wl, wr]
+    rows = [pl.BlockSpec((g, n, c), lambda b, o: (b, 0, 0))] if len(parts) == 1 else [full(p) for p in parts]
+    specs = rows + [full(wl), full(wr)]
     alias = {}
     if bufs is not None:
-        alias = {4 + i: 2 + i for i in range(4)}
+        alias = {1 + len(ins) + i: 2 + i for i in range(4)}
         ins += list(bufs)
         specs += [pl.BlockSpec(memory_space=pl.ANY)] * 4
     got = pl.pallas_call(
-        functools.partial(operand_kernel, cols),
+        functools.partial(operand_kernel, cols, tuple(p.shape[0] for p in parts)),
         grid_spec=pltpu.PrefetchScalarGridSpec(
             num_scalar_prefetch=1,
             grid=(count // g,),
@@ -326,6 +341,7 @@
                 pltpu.VMEM((g, n, c), F32),
                 pltpu.VMEM((g, n, c), F32),
                 pltpu.VMEM((2 * cols * g, c), F32),
+                pltpu.VMEM((g, n, c), BF),
             ],
         ),
         out_shape=[jax.ShapeDtypeStruct(s, BF) for s, _, _ in shapes],
@@ -665,7 +681,7 @@
     if size != 8 or count % 48:
         sets = [list(range(c, size, 2)) for c in range(2)]
         got = lax.all_gather(rows, "pair", axis=0, tiled=True, axis_index_groups=sets)
-        return [project(got, list(range(got.shape[0] // GROUP)))], first
+        return [project([got], list(range(got.shape[0] // GROUP)))], first
     stages = 3
     step = count // stages
     per = step // GROUP
@@ -673,7 +689,7 @@
     spot = lambda device, s: [device // 2 * (stages * per) + s * per + u for u in range(per)]
     send = lambda value: [exchange(value, "pair", 2), exchange(value, "pair", 4)]
     near, late = send(x[0]), []
-    done = [project(rows, [p for s in range(stages) for p in spot(here, s)])]
+    done = [project([rows], [p for s in range(stages) for p in spot(here, s)])]
     for s in range(stages):
         waits = [x[s + 1], near, late, done[-1][0]]
         if s == 1:
@@ -688,12 +704,12 @@
             done[-2][1] = held[-1]
         late = [exchange(near[0][: step // 2], "pair", 4), exchange(near[1][step // 2 :], "pair", 2)]
         places = spot(here ^ 2, s) + spot(here ^ 4, s) + (spot(here ^ 6, s - 1) if arrived else [])
-        group = jnp.concatenate(near + arrived)
+        group = list(near) + list(arrived)
         if s + 1 < stages:
             near = send(following)
         done.append(project(group, places))
     late, done[-1][0], done[-2][1] = lax.optimization_barrier((late, done[-1][0], done[-2][1]))
-    done.append(project(jnp.concatenate(late), spot(here ^ 6, stages - 1)))
+    done.append(project(list(late), spot(here ^ 6, stages - 1)))
     return done, first
 
 
@@ -806,7 +822,7 @@
         mine, sent, state["bufs"] = operands(
             offs, rows, w_left, w_right, cols, state["start"], tokens // 2, state["bufs"]
         )
-        state["start"] += rows.shape[0]
+        state["start"] += sum(r.shape[0] for r in rows)
         return [mine, swap_cores(sent)]
 
     done, both = project_rows(pair_act[0], project, lax.axis_size("pair"), both)

time: 755 us -> 736 us (0.975)
  other arithmetic: 56.1 us -> 38.3 us
    concatenate x4 -> x0, other arithmetic: 17.8 us -> none  [the longest x3 15.1 us: project_rows(): group = jnp.concatenate(near + arrived)]
  transfers between devices with their start and end apart: 36 -> 36, of which waited for: 15 -> 15; matrix products, arithmetic and copies ran while one was open for 9% -> 7% of each run, Pallas kernels for 19% -> 20%
where the time goes in v6:
time: 736 us; the launch traced here: 731 us
  Pallas kernels  454 us (62%)
  waiting for transfers between devices  117 us (16%)
  local copies, waits for them, and re-layouts  46.5 us (6%)
  other arithmetic  38.3 us (5%)
  starting transfers between devices  32.6 us (4%)
  between operations  22.5 us (3%)
  blocking collectives  20.2 us (3%)
    pallas_call x1, Pallas kernels, column_pass(): pl.pallas_call(functools.partial(column_kernel, heads), grid=(cols // cb,...  201 us
    ppermute x25, waiting for transfers between devices, exchange(): return lax.ppermute(value, axis, [(d, d ^ bit) for d in range(size)])  91.3 us
    pallas_call x5, Pallas kernels, operands(): pl.pallas_call(functools.partial(operand_kernel, cols, tuple((p.shape[0]...  87.8 us
    pallas_call x2, Pallas kernels, tri_grads(): pl.pallas_call(tri_grads_kernel, grid=(count // rows,), in_specs=[row(n,...  46 us
    pallas_call x1, Pallas kernels, back_pass(): pl.pallas_call(back_kernel, grid=(cols // cb,), in_specs=[col(n, c)] * 3...  42.5 us
    pallas_call x1, Pallas kernels, operand_grads(): pl.pallas_call(functools.partial(operand_grads_kernel, len(keep)), grid=(...  40.5 us
    ppermute x25, starting transfers between devices, exchange(): return lax.ppermute(value, axis, [(d, d ^ bit) for d in range(size)])  31.1 us
    pallas_call x1, Pallas kernels, afters(): pl.pallas_call(functools.partial(after_kernel, heads), grid=(cols // cb,)...  21.5 us
  transfers between devices with their start and end apart: 36, of which 15 were waited for; matrix products, arithmetic and copies ran while one was open for 7% of the time, Pallas kernels for 20%

profile of v6, /device:TPU:0, one launch (start us, length us, event | category | flops | bytes accessed | tf_op | source)
XLA Modules:
  0.0 731.1 jit_solution(11311732162238192056)
XLA Ops:
  13.2 5.1 collective-permute-start.4
  19.0 4.7 slice_bitcast_fusion
  30.6 4.4 collective-permute-done.3
  40.6 20.1 %operands.5 = (bf16[64,48,512]{2,1,0:T(8,128)(2,1)}, bf16[64,48,512]{2,1,0:T(8,128)(2,1)}, bf16[192,384,128]{2,1,0:T(8,128)(2,1)}, bf16[192,128,128]{2,1,0:T(8,1...) custom-call(s32[5]{0:T(128)} %stack.117.off_ref, bf16[48,384,128]{2,1,0:T(8,128)(2,1)} %bitcast.148, ...), custom_call_target="tpu_custom_call" | custom-call | flops 143999991808 | bytes 18874368 | tf_op jit(solution)/shard_map/operands/pallas_call | solution.py:331
  73.7 15.3 %operands.6 = (bf16[64,32,512]{2,1,0:T(8,128)(2,1)}, bf16[64,32,512]{2,1,0:T(8,128)(2,1)}, bf16[192,384,128]{2,1,0:T(8,128)(2,1)}, bf16[192,128,128]{2,1,0:T(8,1...) custom-call(s32[4]{0:T(128)} %pad_add_fusion.1.off_ref, ...), custom_call_target="tpu_custom_call", output_to_operand_aliasing={{2}: (5, {}), {3}: (6, {}), {4}: (7, {}), {5}: (8, {})} | custom-call | flops 96000000000 | bytes 12582912 | tf_op jit(solution)/shard_map/operands/pallas_call | solution.py:331
  91.0 26.2 %collective-permute-done.8.refs_3_ = bf16[8,384,128]{2,1,0:T(8,128)(2,1)} collective-permute-done((bf16[8,384,128]{2,1,0:T(8,128)(2,1)}, bf16[8,384,128]{2,1,0:T(8,128)(2,1)}, u32[]{:S(2)}, u32[]{:S(2)}) %collective-permute-start.8) | collective-permute-done | bytes 786464 | tf_op jit(solution)/shard_map/ppermute | solution.py:723
  125.6 21.2 %operands.7 = (bf16[64,48,512]{2,1,0:T(8,128)(2,1)}, bf16[64,48,512]{2,1,0:T(8,128)(2,1)}, bf16[192,384,128]{2,1,0:T(8,128)(2,1)}, bf16[192,128,128]{2,1,0:T(8,1...) custom-call(s32[5]{0:T(128)} %stack.129.off_ref, ...), custom_call_target="tpu_custom_call", output_to_operand_aliasing={{2}: (7, {}), {3}: (8, {}), {4}: (9, {}), {5}: (10, {})} | custom-call | flops 143999991808 | bytes 18874368 | tf_op jit(solution)/shard_map/operands/pallas_call | solution.py:331
  147.0 25.5 %collective-permute-done.13.refs_3_ = bf16[8,384,128]{2,1,0:T(8,128)(2,1)} collective-permute-done((bf16[8,384,128]{2,1,0:T(8,128)(2,1)}, bf16[8,384,128]{2,1,0:T(8,128)(2,1)}, u32[]{:S(2)}, u32[]{:S(2)}) %collective-permute-start.13) | collective-permute-done | bytes 786464 | tf_op jit(solution)/shard_map/ppermute | solution.py:723
  177.8 21.4 %operands.8 = (bf16[64,48,512]{2,1,0:T(8,128)(2,1)}, bf16[64,48,512]{2,1,0:T(8,128)(2,1)}, bf16[192,384,128]{2,1,0:T(8,128)(2,1)}, bf16[192,128,128]{2,1,0:T(8,1...) custom-call(s32[5]{0:T(128)} %stack.133.off_ref, ...), custom_call_target="tpu_custom_call", output_to_operand_aliasing={{2}: (7, {}), {3}: (8, {}), {4}: (9, {}), {5}: (10, {})} | custom-call | flops 143999991808 | bytes 18874368 | tf_op jit(solution)/shard_map/operands/pallas_call | solution.py:331
  199.4 9.7 %operands.9 = (bf16[64,16,512]{2,1,0:T(8,128)(2,1)}, bf16[64,16,512]{2,1,0:T(8,128)(2,1)}, bf16[192,384,128]{2,1,0:T(8,128)(2,1)}, bf16[192,128,128]{2,1,0:T(8,1...) custom-call(s32[3]{0:T(128)} %pad_add_fusion.off_ref, ...), custom_call_target="tpu_custom_call", output_to_operand_aliasing={{2}: (5, {}), {3}: (6, {}), {4}: (7, {}), {5}: (8, {})} | custom-call | flops 48000000000 | bytes 6291456 | tf_op jit(solution)/shard_map/operands/pallas_call | solution.py:331
  213.9 13.6 %products.1 = (bf16[48,64,384]{2,1,0:T(8,128)(2,1)}, bf16[48,64,384]{2,1,0:T(8,128)(2,1)}) custom-call(bf16[64,48,512]{2,1,0:T(8,128)(2,1)} %get-tuple-element.173.refs_0_, bf16[64,32,512]{2,1,0:T(8,128)(2,1)} %get-tuple-element.174.refs_1_, bf16[64,48,512]{2,1,0:T(8,128)(2,1)} %get-tuple-element.175.refs_2_, ...), custom_call_target="tpu_custom_call" | custom-call | flops 2415919104 | bytes 37748736 | tf_op jit(solution)/shard_map/products/pallas_call | solution.py:375
  233.0 21.5 %afters.1 = (f32[48,384,128]{2,1,0:T(8,128)}, bf16[48,1536]{1,0:T(8,128)(2,1)}, bf16[48,384,128]{2,1,0:T(8,128)(2,1)}) custom-call(s32[48]{0:T(128)} %broadcast_in_dim.26.core_ref, bf16[48,192,128]{2,1,0:T(8,128)(2,1)} %get-tuple-element.171.xm_ref, bf16[48,192,128]{2,1,0:T(8,128)(2,1)} %collective-permute-done.18.xo_ref, ...), custom_call_target="tpu_custom_call" | custom-call | flops 2415919104 | bytes 23592960 | tf_op jit(solution)/shard_map/afters/pallas_call | solution.py:440
  261.1 17.8 %all-gather.5.cloned.1.call-done.bias_ref = bf16[384,1536]{1,0:T(8,128)(2,1)} async-done(((bf16[48,1536]{1,0:T(8,128)(2,1)}), bf16[384,1536]{1,0:T(8,128)(2,1)}) %all-gather.5.cloned.1.call-update) | async-done | bytes 1179664 | tf_op jit(solution)/shard_map/all_gather | solution.py:837
  278.8 200.6 %columns.1 = (f32[48,384,128]{2,1,0:T(8,128)}, f32[48,384,128]{2,1,0:T(8,128)}, bf16[384,1536]{1,0:T(8,128)(2,1)}, f32[128,256]{1,0:T(8,128)}, f32[256,128]{1,0:...) custom-call(f32[48,384,128]{2,1,0:T(8,128)} %get-tuple-element.185.after_ref, ...), custom_call_target="tpu_custom_call" | custom-call | flops 43486543872 | bytes 37748736 | tf_op jit(solution)/shard_map/columns/pallas_call | solution.py:214
  479.4 20.2 %all_to_all.9 = bf16[8,48,1536]{2,1,0:T(8,128)(2,1)S(1)} all-to-all(bf16[8,48,1536]{2,1,0:T(8,128)(2,1)} %bitcast.150), channel_id=1, replica_groups=mesh['item'=4,'pair'=8] {'pair'}, dimensions={0} | all-to-all | bytes 2359296 | tf_op jit(solution)/shard_map/all_to_all | solution.py:843
  500.8 42.5 %back.1 = (bf16[48,64,384]{2,1,0:T(8,128)(2,1)}, bf16[48,64,384]{2,1,0:T(8,128)(2,1)}, f32[16,128]{1,0:T(8,128)}, f32[128,128]{1,0:T(8,128)}, f32[128,128]{1,0:T(8,128)}, /*index=5*/f32[8,128]{1,0:T(8,128)}) custom-call(f32[48,384,128]{2,1,0:T(8,128)} %get-tuple-element.185.after_ref, f32[48,384,128]{2,1,0:T(8,128)} %get-tuple-element.192.gx_ref, ...), custom_call_target="tpu_custom_call" | custom-call | flops 4831838208 | bytes 56623104 | tf_op jit(solution)/shard_map/back/pallas_call | solution.py:512
  543.4 4.7 collective-permute-done.23.refs_11_
  549.7 40.5 %operand_grads.1 = (bf16[192,64,512]{2,1,0:T(8,128)(2,1)}, bf16[192,64,512]{2,1,0:T(8,128)(2,1)}) custom-call(bf16[64,48,512]{2,1,0:T(8,128)(2,1)} %get-tuple-element.173.refs_0_, bf16[64,32,512]{2,1,0:T(8,128)(2,1)} %get-tuple-element.174.refs_1_, bf16[64,48,512]{2,1,0:T(8,128)(2,1)} %get-tuple-element.175.refs_2_, ...), custom_call_target="tpu_custom_call" | custom-call | flops 4831838208 | bytes 75497472 | tf_op jit(solution)/shard_map/operand_grads/pallas_call | solution.py:558
  602.4 23.0 %tri_grads.2 = (f32[128,128]{1,0:T(8,128)}, f32[128,128]{1,0:T(8,128)}) custom-call(bf16[192,384,128]{2,1,0:T(8,128)(2,1)} %get-tuple-element.202.n_ref, bf16[192,128,128]{2,1,0:T(8,128)(2,1)} %get-tuple-element.203.nc_ref, bf16[192,64,512]{2,1,0:T(8,128)(2,1)} %get-tuple-element.206.g_ref, bf16[128,128]{1,0:T(8,128)(2,1)} %pad_maximum_fusion.8.wl_ref, ...), custom_call_target="tpu_custom_call" | custom-call | flops 9663676416 | bytes 75497472 | tf_op jit(solution)/shard_map/tri_grads/pallas_call | solution.py:608
  627.5 23.0 %tri_grads.3 = (f32[128,128]{1,0:T(8,128)}, f32[128,128]{1,0:T(8,128)}) custom-call(bf16[192,384,128]{2,1,0:T(8,128)(2,1)} %get-tuple-element.202.n_ref, bf16[192,128,128]{2,1,0:T(8,128)(2,1)} %get-tuple-element.203.nc_ref, bf16[192,64,512]{2,1,0:T(8,128)(2,1)} %collective-permute-done.25.g_ref, bf16[128,128]{1,0:T(8,128)(2,1)} %pad_maximum_fusion.10.wl_ref, ...), custom_call_target="tpu_custom_call" | custom-call | flops 9663676416 | bytes 75497472 | tf_op jit(solution)/shard_map/tri_grads/pallas_call | solution.py:608
  660.4 5.5 collective-permute-done.26
  666.7 5.0 collective-permute-done.27
  678.1 9.2 %collective-permute-done.29 = f32[32,2446]{1,0:T(8,128)S(1)} collective-permute-done((f32[32,2446]{1,0:T(8,128)S(1)}, f32[32,2446]{1,0:T(8,128)S(1)}, u32[]{:S(2)}, u32[]{:S(2)}) %collective-permute-start.29) | collective-permute-done | bytes 313120 | tf_op jit(solution)/shard_map/ppermute | solution.py:723
  692.8 6.8 collective-permute-done.30
  (361 shorter events, 121.0 us)
Async XLA Ops:
  7.2 81.8 %all-gather.3.cloned.1.call-start = ((), (), s32[]{:S(2)}) async-start(), calls=%async_computation.1 | async-start | bytes 1327104 | tf_op jit(solution)/shard_map/all_gather | solution.py:801
  13.2 17.4 %collective-permute-start.4 = (bf16[32,2953]{1,0:T(8,128)(2,1)S(1)}, bf16[32,2953]{1,0:T(8,128)(2,1)S(1)}, u32[]{:S(2)}, u32[]{:S(2)}) collective-permute-start(bf16[32,2953]{1,0:T(8,128)(2,1)S(1)} %concatenate.59), channel_id=1, source_target_pairs={{0,24},{8,16},{16,8},{24,0},{1,25},{9,17},{17,9},{25,1},{2,26},{10... | collective-permute-start | bytes 566984 | tf_op jit(solution)/shard_map/ppermute | solution.py:723
  18.3 16.7 %collective-permute-start.3 = (bf16[32,2953]{1,0:T(8,128)(2,1)S(1)}, bf16[32,2953]{1,0:T(8,128)(2,1)S(1)}, u32[]{:S(2)}, u32[]{:S(2)}) collective-permute-start(bf16[32,2953]{1,0:T(8,128)(2,1)S(1)} %concatenate.59), channel_id=1, source_target_pairs={{0,16},{8,24},{16,0},{24,8},{1,17},{9,25},{17,1},{25,9},{2,18},{10... | collective-permute-start | bytes 566984 | tf_op jit(solution)/shard_map/ppermute | solution.py:723
  18.3 16.7 %collective-permute-start.2 = (bf16[32,2953]{1,0:T(8,128)(2,1)S(1)}, bf16[32,2953]{1,0:T(8,128)(2,1)S(1)}, u32[]{:S(2)}, u32[]{:S(2)}) collective-permute-start(bf16[32,2953]{1,0:T(8,128)(2,1)S(1)} %concatenate.59), channel_id=1, source_target_pairs={{0,8},{8,0},{16,24},{24,16},{1,9},{9,1},{17,25},{25,17},{2,10},{10... | collective-permute-start | bytes 566984 | tf_op jit(solution)/shard_map/ppermute | solution.py:723
  23.6 40.6 %collective-permute-start.1 = (bf16[16,384,128]{2,1,0:T(8,128)(2,1)}, bf16[16,384,128]{2,1,0:T(8,128)(2,1)}, u32[]{:S(2)}, u32[]{:S(2)}) collective-permute-start(bf16[16,384,128]{2,1,0:T(8,128)(2,1)} %get-tuple-element.350), channel_id=1, source_target_pairs={{0,4},{1,5},{2,6},{3,7},{4,0},{5,1},{6,2},{7,3},{8,12},{9,13},{10,... | collective-permute-start | bytes 4718600 | tf_op jit(solution)/shard_map/ppermute | solution.py:723
  25.3 40.2 %collective-permute-start = (bf16[16,384,128]{2,1,0:T(8,128)(2,1)}, bf16[16,384,128]{2,1,0:T(8,128)(2,1)}, u32[]{:S(2)}, u32[]{:S(2)}) collective-permute-start(bf16[16,384,128]{2,1,0:T(8,128)(2,1)} %get-tuple-element.350), channel_id=1, source_target_pairs={{0,2},{1,3},{2,0},{3,1},{4,6},{5,7},{6,4},{7,5},{8,10},{9,11},{10,... | collective-permute-start | bytes 4718600 | tf_op jit(solution)/shard_map/ppermute | solution.py:723
  27.5 251.4 %all-gather.5.cloned.1.call-start = ((), (), s32[]{:S(2)}) async-start(), calls=%async_computation.2 | async-start | bytes 1327104 | tf_op jit(solution)/shard_map/all_gather | solution.py:837
  60.7 56.6 %collective-permute-start.9 = (bf16[64,48,512]{2,1,0:T(8,128)(2,1)}, bf16[64,48,512]{2,1,0:T(8,128)(2,1)S(1)}, u32[]{:S(2)}, u32[]{:S(2)}) collective-permute-start(bf16[64,48,512]{2,1,0:T(8,128)(2,1)} %get-tuple-element.143), channel_id=1, source_target_pairs={{0,1},{1,0},{2,3},{3,2},{4,5},{5,4},{6,7},{7,6},{8,9},{9,8},{10,11... | collective-permute-start | bytes 9437192 | tf_op jit(solution)/shard_map/ppermute | solution.py:718
  65.5 51.8 %collective-permute-start.6 = (bf16[16,384,128]{2,1,0:T(8,128)(2,1)}, bf16[16,384,128]{2,1,0:T(8,128)(2,1)}, u32[]{:S(2)}, u32[]{:S(2)}) collective-permute-start(bf16[16,384,128]{2,1,0:T(8,128)(2,1)} %get-tuple-element.135), channel_id=1, source_target_pairs={{0,4},{1,5},{2,6},{3,7},{4,0},{5,1},{6,2},{7,3},{8,12},{9,13},{10,... | collective-permute-start | bytes 4718600 | tf_op jit(solution)/shard_map/ppermute | solution.py:723
  66.0 51.3 %collective-permute-start.5 = (bf16[16,384,128]{2,1,0:T(8,128)(2,1)}, bf16[16,384,128]{2,1,0:T(8,128)(2,1)}, u32[]{:S(2)}, u32[]{:S(2)}) collective-permute-start(bf16[16,384,128]{2,1,0:T(8,128)(2,1)} %get-tuple-element.135), channel_id=1, source_target_pairs={{0,2},{1,3},{2,0},{3,1},{4,6},{5,7},{6,4},{7,5},{8,10},{9,11},{10,... | collective-permute-start | bytes 4718600 | tf_op jit(solution)/shard_map/ppermute | solution.py:723
  71.6 45.6 %collective-permute-start.8 = (bf16[8,384,128]{2,1,0:T(8,128)(2,1)}, bf16[8,384,128]{2,1,0:T(8,128)(2,1)}, u32[]{:S(2)}, u32[]{:S(2)}) collective-permute-start(bf16[8,384,128]{2,1,0:T(8,128)(2,1)} %slice.200), channel_id=1, source_target_pairs={{0,2},{1,3},{2,0},{3,1},{4,6},{5,7},{6,4},{7,5},{8,10},{9,11},{10,... | collective-permute-start | bytes 2359304 | tf_op jit(solution)/shard_map/ppermute | solution.py:723
  72.2 45.1 %collective-permute-start.7 = (bf16[8,384,128]{2,1,0:T(8,128)(2,1)}, bf16[8,384,128]{2,1,0:T(8,128)(2,1)}, u32[]{:S(2)}, u32[]{:S(2)}) collective-permute-start(bf16[8,384,128]{2,1,0:T(8,128)(2,1)} %slice.199), channel_id=1, source_target_pairs={{0,4},{1,5},{2,6},{3,7},{4,0},{5,1},{6,2},{7,3},{8,12},{9,13},{10,... | collective-permute-start | bytes 2359304 | tf_op jit(solution)/shard_map/ppermute | solution.py:723
  117.3 29.6 %collective-permute-start.14 = (bf16[64,32,512]{2,1,0:T(8,128)(2,1)}, bf16[64,32,512]{2,1,0:T(8,128)(2,1)}, u32[]{:S(2)}, u32[]{:S(2)}) collective-permute-start(bf16[64,32,512]{2,1,0:T(8,128)(2,1)} %get-tuple-element.154), channel_id=1, source_target_pairs={{0,1},{1,0},{2,3},{3,2},{4,5},{5,4},{6,7},{7,6},{8,9},{9,8},{10,11... | collective-permute-start | bytes 6291464 | tf_op jit(solution)/shard_map/ppermute | solution.py:718
  117.3 55.1 %collective-permute-start.11 = (bf16[16,384,128]{2,1,0:T(8,128)(2,1)}, bf16[16,384,128]{2,1,0:T(8,128)(2,1)}, u32[]{:S(2)}, u32[]{:S(2)}) collective-permute-start(bf16[16,384,128]{2,1,0:T(8,128)(2,1)} %get-tuple-element.144), channel_id=1, source_target_pairs={{0,4},{1,5},{2,6},{3,7},{4,0},{5,1},{6,2},{7,3},{8,12},{9,13},{10,... | collective-permute-start | bytes 4718600 | tf_op jit(solution)/shard_map/ppermute | solution.py:723
  118.7 53.7 %collective-permute-start.10 = (bf16[16,384,128]{2,1,0:T(8,128)(2,1)}, bf16[16,384,128]{2,1,0:T(8,128)(2,1)}, u32[]{:S(2)}, u32[]{:S(2)}) collective-permute-start(bf16[16,384,128]{2,1,0:T(8,128)(2,1)} %get-tuple-element.144), channel_id=1, source_target_pairs={{0,2},{1,3},{2,0},{3,1},{4,6},{5,7},{6,4},{7,5},{8,10},{9,11},{10,... | collective-permute-start | bytes 4718600 | tf_op jit(solution)/shard_map/ppermute | solution.py:723
  124.5 48.0 %collective-permute-start.13 = (bf16[8,384,128]{2,1,0:T(8,128)(2,1)}, bf16[8,384,128]{2,1,0:T(8,128)(2,1)}, u32[]{:S(2)}, u32[]{:S(2)}) collective-permute-start(bf16[8,384,128]{2,1,0:T(8,128)(2,1)} %slice.202), channel_id=1, source_target_pairs={{0,2},{1,3},{2,0},{3,1},{4,6},{5,7},{6,4},{7,5},{8,10},{9,11},{10,... | collective-permute-start | bytes 2359304 | tf_op jit(solution)/shard_map/ppermute | solution.py:723
  125.0 47.4 %collective-permute-start.12 = (bf16[8,384,128]{2,1,0:T(8,128)(2,1)}, bf16[8,384,128]{2,1,0:T(8,128)(2,1)}, u32[]{:S(2)}, u32[]{:S(2)}) collective-permute-start(bf16[8,384,128]{2,1,0:T(8,128)(2,1)} %slice.201), channel_id=1, source_target_pairs={{0,4},{1,5},{2,6},{3,7},{4,0},{5,1},{6,2},{7,3},{8,12},{9,13},{10,... | collective-permute-start | bytes 2359304 | tf_op jit(solution)/shard_map/ppermute | solution.py:723
  146.9 52.5 %collective-permute-start.17 = (bf16[64,48,512]{2,1,0:T(8,128)(2,1)}, bf16[64,48,512]{2,1,0:T(8,128)(2,1)S(1)}, u32[]{:S(2)}, u32[]{:S(2)}) collective-permute-start(bf16[64,48,512]{2,1,0:T(8,128)(2,1)} %get-tuple-element.164), channel_id=1, source_target_pairs={{0,1},{1,0},{2,3},{3,2},{4,5},{5,4},{6,7},{7,6},{8,9},{9,8},{10,11... | collective-permute-start | bytes 9437192 | tf_op jit(solution)/shard_map/ppermute | solution.py:718
  175.8 23.6 %collective-permute-start.16 = (bf16[8,384,128]{2,1,0:T(8,128)(2,1)}, bf16[8,384,128]{2,1,0:T(8,128)(2,1)}, u32[]{:S(2)}, u32[]{:S(2)}) collective-permute-start(bf16[8,384,128]{2,1,0:T(8,128)(2,1)} %slice.204), channel_id=1, source_target_pairs={{0,2},{1,3},{2,0},{3,1},{4,6},{5,7},{6,4},{7,5},{8,10},{9,11},{10,... | collective-permute-start | bytes 2359304 | tf_op jit(solution)/shard_map/ppermute | solution.py:723
  177.2 22.1 %collective-permute-start.15 = (bf16[8,384,128]{2,1,0:T(8,128)(2,1)S(1)}, bf16[8,384,128]{2,1,0:T(8,128)(2,1)}, u32[]{:S(2)}, u32[]{:S(2)}) collective-permute-start(bf16[8,384,128]{2,1,0:T(8,128)(2,1)S(1)} %slice.203), channel_id=1, source_target_pairs={{0,4},{1,5},{2,6},{3,7},{4,0},{5,1},{6,2},{7,3},{8,12},{9,13},{10,... | collective-permute-start | bytes 2359304 | tf_op jit(solution)/shard_map/ppermute | solution.py:723
  209.6 22.6 %collective-permute-start.18 = (bf16[48,192,128]{2,1,0:T(8,128)(2,1)}, bf16[48,192,128]{2,1,0:T(8,128)(2,1)}, u32[]{:S(2)}, u32[]{:S(2)}) collective-permute-start(bf16[48,192,128]{2,1,0:T(8,128)(2,1)} %get-tuple-element.172), channel_id=1, source_target_pairs={{0,1},{1,0},{2,3},{3,2},{4,5},{5,4},{6,7},{7,6},{8,9},{9,8},{10,11... | collective-permute-start | bytes 7077896 | tf_op jit(solution)/shard_map/ppermute | solution.py:718
  590.3 37.2 %collective-permute-start.25 = (bf16[192,64,512]{2,1,0:T(8,128)(2,1)}, bf16[192,64,512]{2,1,0:T(8,128)(2,1)}, u32[]{:S(2)}, u32[]{:S(2)}) collective-permute-start(bf16[192,64,512]{2,1,0:T(8,128)(2,1)} %get-tuple-element.209), channel_id=1, source_target_pairs={{0,1},{1,0},{2,3},{3,2},{4,5},{5,4},{6,7},{7,6},{8,9},{9,8},{10,11... | collective-permute-start | bytes 37748744 | tf_op jit(solution)/shard_map/ppermute | solution.py:718
  599.9 25.5 %collective-permute-start.22 = (bf16[64,1932]{0,1:T(8,128)(2,1)S(1)}, bf16[64,1932]{0,1:T(8,128)(2,1)S(1)}, u32[]{:S(2)}, u32[]{:S(2)}) collective-permute-start(bf16[64,1932]{0,1:T(8,128)(2,1)S(1)} %dynamic-slice_convert_fusion.1), channel_id=1, source_target_pairs={{0,16},{8,24},{16,0},{24,8},{1,17},{9,25},{17,1},{25,9},{2,18},{10... | collective-permute-start | bytes 741896 | tf_op jit(solution)/shard_map/ppermute | solution.py:723
  626.0 24.5 %collective-permute-start.24 = (bf16[32,1932]{0,1:T(8,128)(2,1)S(1)}, bf16[32,1932]{0,1:T(8,128)(2,1)S(1)}, u32[]{:S(2)}, u32[]{:S(2)}) collective-permute-start(bf16[32,1932]{0,1:T(8,128)(2,1)S(1)} %dynamic-slice_convert_fusion), channel_id=1, source_target_pairs={{0,8},{8,0},{16,24},{24,16},{1,9},{9,1},{17,25},{25,17},{2,10},{10... | collective-permute-start | bytes 370952 | tf_op jit(solution)/shard_map/ppermute | solution.py:723
  (88 other events, 1351.4 us)
Sparse Core Ops, SparseCore 0:
  27.6 28.4 all-gather.2
  254.6 24.1 all-gather.4
